TPU v7x, 128 devices: a whole 4x4x4 slice. The times are simulated.
128 devices in a mesh: region: 4 (over z), brick: 32 (over x, y, core).
Axes of the slice: x: 4, y: 4, z: 4, core: 2. Of those that a mesh axis runs over, the one named last changes fastest.
Arguments:
- features: bfloat16 [512, 64, 512], P(('region', 'brick')), may hold values from -6 to 6
- active: int32 [512, 512], P(('region', 'brick')), may hold values 0 or 1
- neighbours: int32 [512, 26], P(('region', 'brick')), may hold values from -1 to 511, as said below
- first_weight: bfloat16 [27, 64, 64], replicated, may hold values from -0.15625 to 0.15625
- second_weight: bfloat16 [27, 64, 64], replicated, may hold values from -0.15625 to 0.15625
- film_scale: float32 [64], replicated, may hold values from -0.5 to 0.5
- film_shift: float32 [64], replicated, may hold values from -3 to 3
- cotangent: bfloat16 [512, 64, 512], P(('region', 'brick')), may hold values from -0.109375 to 0.109375
Outputs:
- block_output: bfloat16 [512, 64, 512], P(('region', 'brick'))
- grad_first: float32 [27, 64, 64], replicated
- grad_second: float32 [27, 64, 64], replicated
Inputs may be any that keep to these rules, and one draw needn't show every extreme that they name: The lists are symmetric: neighbours[b, e] = n >= 0 exactly when neighbours[n, e'] = b for the opposite offset e' = -e. Brick b is stored on the device of index b // 4 over region+brick. The devices of one region index form a grid of 8 columns by 4 rows, brick index = row * 8 + column, and every listed neighbour lies on the same device or on one of the eight devices whose column and row differ by at most one. The face of n read at offset e is n's face on the side of the first nonzero component of -e; counting distinct pairs (brick n, that face) that bricks of one device read from bricks of another, no pair of devices beside each other along columns has more than 4, along rows more than 2, diagonally more than 2, and in every draw some pair of each of these three kinds has exactly that many.
All inputs are finite; a program needn't handle non-finite values. No bound on the sum of `active` on one device may be relied on, other than what follows from the above.
Results may differ from a plain program's by a relative error of at most 0.0054.
Values may be sent and summed in bfloat16 or wider, within the bound.
No kernel may reach another device: no remote copies, remote signals or barrier semaphores. Data moves between devices by JAX's collectives and lax.ppermute only.
A program may use at most 128 MiB of HBM per device.

v0:
```python
import jax
import jax.numpy as jnp
import numpy as np
from jax import lax
from jax.sharding import PartitionSpec as P

CAPX = 4
CAPY = 2
CAPD = 2


def as_sent(array):

    def short(part):
        return part.astype(jnp.bfloat16) if part.dtype == jnp.float32 else part

    return jax.tree.map(short, array)


def passed_along(array, axis, by):
    count = lax.axis_size(axis)
    pairs = [(i, i + by) for i in range(count) if 0 <= i + by < count]
    return lax.ppermute(array, axis, pairs)


def direction_list():
    return [
        (a, b, c)
        for a in (-1, 0, 1)
        for b in (-1, 0, 1)
        for c in (-1, 0, 1)
        if (a, b, c) != (0, 0, 0)
    ]


def face_of(vector):
    if vector[0] != 0:
        return 0 if vector[0] < 0 else 1
    if vector[1] != 0:
        return 2 if vector[1] < 0 else 3
    return 4 if vector[2] < 0 else 5


def face_voxels():
    lookup = np.zeros((6, 64), np.int32)
    for face_index in range(6):
        axis_index = face_index // 2
        others = [i for i in range(3) if i != axis_index]
        for outer_cell in range(8):
            for inner_cell in range(8):
                coords = [0, 0, 0]
                coords[axis_index] = 7 if face_index % 2 else 0
                coords[others[0]] = outer_cell
                coords[others[1]] = inner_cell
                lookup[face_index, outer_cell * 8 + inner_cell] = (
                    coords[0] * 64 + coords[1] * 8 + coords[2]
                )
    return lookup.reshape(-1)


def halo_tables():
    directions = direction_list()
    cell_lists = [[] for _ in directions]
    place_lists = [[] for _ in directions]
    source = np.zeros(1000, np.int32)
    for position in range(1000):
        padded = (position // 100, position // 10 % 10, position % 10)
        vector = tuple((-1 if t == 0 else 1 if t == 9 else 0 for t in padded))
        if vector == (0, 0, 0):
            source[position] = (padded[0] - 1) * 64 + (padded[1] - 1) * 8 + padded[2] - 1
            continue
        direction_index = directions.index(vector)
        coords = [7 if vector[i] < 0 else 0 if vector[i] > 0 else padded[i] - 1 for i in range(3)]
        face_index = face_of(tuple((-t for t in vector)))
        others = [i for i in range(3) if i != face_index // 2]
        cell_lists[direction_index].append(coords[others[0]] * 8 + coords[others[1]])
        place_lists[direction_index].append(position)
    offset = 512
    for direction_index in range(len(directions)):
        for position in place_lists[direction_index]:
            source[position] = offset
            offset += 1
    read_faces = np.array([face_of(tuple((-t for t in d))) for d in directions], np.int32)
    return ([np.array(c, np.int32) for c in cell_lists], source, read_faces)


def conv_tables():
    valid_places = np.zeros(512, np.int32)
    embed_places = np.full(896, 512, np.int32)
    for voxel_index in range(512):
        coords = (voxel_index // 64, voxel_index // 8 % 8, voxel_index % 8)
        position = (coords[0] + 1) * 100 + (coords[1] + 1) * 10 + coords[2] + 1 - 104
        valid_places[voxel_index] = position
        embed_places[position] = voxel_index
    return (valid_places, embed_places)


def extended_source(source):
    lookup = np.full(1152, 1000, np.int32)
    lookup[8:1008] = source
    return lookup


def shift_of(k):
    return (k // 9 - 1) * 100 + (k // 3 % 3 - 1) * 10 + k % 3 - 1


def faces_of(values):
    bricks, channels = (values.shape[0], values.shape[1])
    faces = jnp.take(values, jnp.asarray(face_voxels()), axis=2)
    return (
        faces.reshape(bricks, channels, 6, 64)
        .transpose(0, 2, 1, 3)
        .reshape(bricks * 6, channels * 64)
    )


def assemble(own_values, face_table, gather_index, cell_lists, lookup):
    bricks, channels = (own_values.shape[0], own_values.shape[1])
    pieces = [own_values]
    for direction_index in range(26):
        face_rows = jnp.take(face_table, gather_index[:, direction_index], axis=0).reshape(
            bricks, channels, 64
        )
        pieces.append(jnp.take(face_rows, jnp.asarray(cell_lists[direction_index]), axis=2))
    pieces.append(jnp.zeros((bricks, channels, 1), own_values.dtype))
    return jnp.take(jnp.concatenate(pieces, axis=2), jnp.asarray(lookup), axis=2)


def convolve(extended, weight, flipped, valid_places):
    accumulated = None
    for k in range(27):
        window_start = 112 - shift_of(k) if flipped else 112 + shift_of(k)
        window = lax.slice_in_dim(extended, window_start, window_start + 896, axis=2)
        if flipped:
            contribution = jnp.einsum(
                "oc,bop->bcp", weight[k], window, preferred_element_type=jnp.float32
            )
        else:
            contribution = jnp.einsum(
                "oc,bcp->bop", weight[k], window, preferred_element_type=jnp.float32
            )
        accumulated = contribution if accumulated is None else accumulated + contribution
    return jnp.take(accumulated, jnp.asarray(valid_places), axis=2)


def weight_grad(extended, slope, embed_places):
    bricks, channels = (slope.shape[0], slope.shape[1])
    widened = jnp.concatenate([slope, jnp.zeros((bricks, channels, 1), slope.dtype)], axis=2)
    padded_slope = jnp.take(widened, jnp.asarray(embed_places), axis=2)
    gradients = []
    for k in range(27):
        window_start = 112 + shift_of(k)
        window = lax.slice_in_dim(extended, window_start, window_start + 896, axis=2)
        gradients.append(
            jnp.einsum("bop,bcp->oc", padded_slope, window, preferred_element_type=jnp.float32)
        )
    return jnp.stack(gradients)


def shards(
    features, active, neighbours, first_weight, second_weight, film_scale, film_shift, cotangent
):
    bricks, channels = (features.shape[0], features.shape[1])
    group_size = lax.axis_size("brick")
    grid_width = group_size // 4
    my_column = lax.axis_index("brick")
    my_x = my_column % grid_width
    my_y = my_column // grid_width
    base_brick = (lax.axis_index("region") * group_size + my_column) * bricks
    cell_lists, source, read_faces = halo_tables()
    lookup = extended_source(source)
    valid_places, embed_places = conv_tables()
    send_faces = np.array([face_of(d) for d in direction_list()], np.int32)
    grid_steps = [
        (step_x, step_y)
        for step_y in (-1, 0, 1)
        for step_x in (-1, 0, 1)
        if (step_x, step_y) != (0, 0)
    ]
    owner_column = neighbours // bricks - lax.axis_index("region") * group_size
    owner_x = owner_column % grid_width
    owner_y = owner_column // grid_width
    present = neighbours >= 0
    remote = present & (owner_column != my_column)
    local_link = present & (owner_column == my_column)
    face_range = jnp.arange(bricks * 6)
    send_local = jnp.arange(bricks)[:, None] * 6 + jnp.asarray(send_faces)[None, :]
    wanted = neighbours * 6 + jnp.asarray(read_faces)[None, :]
    wanted_local = (neighbours % bricks * 6 + jnp.asarray(read_faces)[None, :]).astype(jnp.int32)

    def marks(local_ids, chosen_links):
        hits = chosen_links[:, :, None] & (local_ids[:, :, None] == face_range[None, None, :])
        return jnp.any(hits, axis=(0, 1)).astype(jnp.int32)

    selectors = []
    found = jnp.zeros(neighbours.shape, jnp.int32)
    slot_start = 0
    for step_x, step_y in grid_steps:
        capacity = CAPX if step_y == 0 else CAPY if step_x == 0 else CAPD
        outgoing = remote & (owner_x == my_x + step_x) & (owner_y == my_y + step_y)
        needed = marks(send_local, outgoing)
        ranks = jnp.cumsum(needed) - needed
        chosen = (needed[None, :] > 0) & (ranks[None, :] == jnp.arange(capacity)[:, None])
        selectors.append(chosen.astype(jnp.bfloat16))
        incoming = remote & (owner_x == my_x - step_x) & (owner_y == my_y - step_y)
        held = marks(wanted_local, incoming)
        held_ranks = jnp.cumsum(held) - held
        found = jnp.where(incoming, slot_start + jnp.take(held_ranks, wanted_local), found)
        slot_start += capacity

    def delivered(face_rows, mover):
        arrivals = []
        for position, (step_x, step_y) in enumerate(grid_steps):
            if face_rows.ndim == 2:
                packed = jnp.dot(
                    selectors[position], face_rows, preferred_element_type=jnp.float32
                ).astype(jnp.bfloat16)
            else:
                packed = jnp.einsum(
                    "ir,orn->oin",
                    selectors[position],
                    face_rows,
                    preferred_element_type=jnp.float32,
                ).astype(jnp.bfloat16)
            arrivals.append(mover(packed, step_y * grid_width + step_x))
        return jnp.concatenate(arrivals, axis=face_rows.ndim - 2)

    active_mask = active.astype(jnp.float32)[:, None, :]
    activated = (active_mask * jax.nn.silu(features.astype(jnp.float32))).astype(jnp.bfloat16)
    slope_second = (active_mask * cotangent.astype(jnp.float32)).astype(jnp.bfloat16)
    act_faces = faces_of(activated)
    slope_faces = faces_of(slope_second)
    act_arrived = delivered(
        act_faces,
        lambda payload, distance: jax.tree.map(
            lambda part, own: part.astype(own.dtype),
            passed_along(as_sent(payload), "brick", distance),
            payload,
        ),
    )
    zero_row = bricks * 6 + slot_start
    gather_index = jnp.where(
        local_link, wanted - base_brick * 6, jnp.where(remote, bricks * 6 + found, zero_row)
    ).astype(jnp.int32)
    zero_face = jnp.zeros((1, channels * 64), jnp.bfloat16)

    def extended_of(own_values, own_faces, arrived):
        face_table = jnp.concatenate([own_faces, arrived, zero_face], axis=0)
        return assemble(own_values, face_table, gather_index, cell_lists, lookup)

    first_extended = extended_of(activated, act_faces, act_arrived)
    pre_first = convolve(first_extended, first_weight, False, valid_places)
    film_gain = 1.0 + film_scale[None, :, None]
    shaped = pre_first * film_gain + film_shift[None, :, None]
    hidden = (active_mask * jax.nn.silu(shaped)).astype(jnp.bfloat16)
    hidden_faces = faces_of(hidden)
    hidden_arrived = delivered(
        hidden_faces,
        lambda payload, distance: jax.tree.map(
            lambda part, own: part.astype(own.dtype),
            passed_along(as_sent(payload), "brick", distance),
            payload,
        ),
    )
    second_extended = extended_of(hidden, hidden_faces, hidden_arrived)
    second = convolve(second_extended, second_weight, False, valid_places)
    block_output = (features.astype(jnp.float32) + active_mask * second).astype(jnp.bfloat16)
    grad_second = weight_grad(second_extended, slope_second, embed_places)
    grad_second = lax.psum(grad_second, ("region", "brick"))
    slope_arrived = delivered(
        slope_faces,
        lambda payload, distance: jax.tree.map(
            lambda part, own: part.astype(own.dtype),
            passed_along(as_sent(payload), "brick", distance),
            payload,
        ),
    )
    slope_extended = extended_of(slope_second, slope_faces, slope_arrived)
    back_hidden = convolve(slope_extended, second_weight, True, valid_places)
    sigmoid_gate = jax.nn.sigmoid(shaped)
    slope_first = (
        back_hidden * active_mask * sigmoid_gate * (1.0 + shaped * (1.0 - sigmoid_gate)) * film_gain
    ).astype(jnp.bfloat16)
    grad_first = weight_grad(first_extended, slope_first, embed_places)
    grad_first = lax.psum(grad_first, ("region", "brick"))
    return (block_output, grad_first, grad_second)


def solution(mesh):
    return jax.shard_map(
        shards,
        mesh=mesh,
        in_specs=(
            P(("region", "brick"), None, None),
            P(("region", "brick"), None),
            P(("region", "brick"), None),
            P(),
            P(),
            P(),
            P(),
            P(("region", "brick"), None, None),
        ),
        out_specs=(P(("region", "brick"), None, None), P(), P()),
        check_vma=False,
    )
```

profile of v0, /device:TPU:1, one launch (start us, length us, event | category | flops | bytes accessed | tf_op | source)
XLA Modules:
  0.0 680.1 jit_solution(8469782822787526356)
XLA Ops:
  19.9 6.2 collective-permute-start.21
  26.6 5.7 collective-permute-start.22
  67.6 4.0 collective-permute-start.23
  74.1 3.6 collective-permute-start.20
  83.7 7.0 %collective-permute-start.5 = (bf16[2,4096]{1,0:T(2,128)(2,1)S(1)}, bf16[2,4096]{1,0:T(2,128)(2,1)S(1)}, u32[]{:S(2)}, u32[]{:S(2)}) collective-permute-start(bf16[2,4096]{1,0:T(2,128)(2,1)S(1)} %convolution_convert_fusion.20), channel_id=1, source_target_pairs={{0,7},{1,8},{2,9},{3,10},{4,11},{5,12},{6,13},{7,14},{8,15},{9,16}... | collective-permute-start | bytes 49160 | tf_op jit(solution)/shard_map/ppermute | solution.py:23
  90.7 7.6 %collective-permute-start.6 = (bf16[2,4096]{1,0:T(2,128)(2,1)S(1)}, bf16[2,4096]{1,0:T(2,128)(2,1)S(1)}, u32[]{:S(2)}, u32[]{:S(2)}) collective-permute-start(bf16[2,4096]{1,0:T(2,128)(2,1)S(1)} %convolution_convert_fusion.19), channel_id=1, source_target_pairs={{0,8},{1,9},{2,10},{3,11},{4,12},{5,13},{6,14},{7,15},{8,16},{9,17... | collective-permute-start | bytes 49160 | tf_op jit(solution)/shard_map/ppermute | solution.py:23
  99.6 4.7 collective-permute-start.3
  104.2 2.1 collective-permute-start.4
  107.5 3.2 gather_fusion.150
  204.2 4.6 concatenate.29
  210.1 4.3 gather_fusion.147
  231.7 2.1 fusion.124
  278.4 4.1 concatenate.25
  282.4 2.2 copy.707
  284.6 4.6 gather_fusion.53
  289.2 2.6 copy.708
  291.8 2.1 convolution_bitcast_fusion.10
  307.9 2.1 convolution_bitcast_fusion.18
  321.9 2.8 copy.846
  324.7 3.1 gather_fusion.148
  338.5 3.0 gather_fusion.54
  347.5 4.0 gather_fusion.149
  356.5 10.2 %collective-permute-start.13 = (bf16[2,4096]{1,0:T(2,128)(2,1)S(1)}, bf16[2,4096]{1,0:T(2,128)(2,1)S(1)}, u32[]{:S(2)}, u32[]{:S(2)}) collective-permute-start(bf16[2,4096]{1,0:T(2,128)(2,1)S(1)} %convolution_convert_fusion.14), channel_id=1, source_target_pairs={{0,7},{1,8},{2,9},{3,10},{4,11},{5,12},{6,13},{7,14},{8,15},{9,16}... | collective-permute-start | bytes 49160 | tf_op jit(solution)/shard_map/ppermute | solution.py:23
  366.7 7.6 %collective-permute-start.14 = (bf16[2,4096]{1,0:T(2,128)(2,1)S(1)}, bf16[2,4096]{1,0:T(2,128)(2,1)S(1)}, u32[]{:S(2)}, u32[]{:S(2)}) collective-permute-start(bf16[2,4096]{1,0:T(2,128)(2,1)S(1)} %convolution_convert_fusion.13), channel_id=1, source_target_pairs={{0,8},{1,9},{2,10},{3,11},{4,12},{5,13},{6,14},{7,15},{8,16},{9,17... | collective-permute-start | bytes 49160 | tf_op jit(solution)/shard_map/ppermute | solution.py:23
  384.7 4.7 collective-permute-start.11
  450.3 4.4 concatenate.27
  456.0 4.3 gather_fusion.100
  475.4 2.1 convolution_bitcast_fusion.8
  511.8 4.4 fusion.29
  516.2 2.1 copy.764
  521.6 148.0 %all-reduce.5.cloned.1.call-done = (f32[27,64,64]{2,1,0:T(8,128)}, f32[27,64,64]{2,1,0:T(8,128)}) async-done(((f32[27,64,64]{2,1,0:T(8,128)}, f32[27,64,64]{2,1,0:T(8,128)}), (f32[27,64,64]{2,1,0:T(8,128)}, f32[27,64,64]{2,1,0:T(8,128)})) %all-reduce.5.cloned.1.call-update) | async-done | bytes 884752 | tf_op jit(solution)/shard_map/psum | solution.py:286
  669.6 2.3 copy.1020
  (1078 shorter events, 385.4 us)
Async XLA Ops:
  7.2 662.4 %all-reduce.5.cloned.1.call-start = ((), (), s32[]{:S(2)}) async-start(), calls=%async_computation | async-start | bytes 3538944 | tf_op jit(solution)/shard_map/psum | solution.py:286
  11.8 175.5 %copy-start.53 = (s32[1024]{0:T(1024)}, s32[1024]{0:T(1024)S(1)}, u32[]{:S(2)}) copy-start(s32[1024]{0:T(1024)S(1)} %get-tuple-element.225) | copy-start | bytes 12292
  14.6 52.9 %collective-permute-start.16 = (bf16[2,4096]{1,0:T(2,128)(2,1)S(1)}, bf16[2,4096]{1,0:T(2,128)(2,1)S(1)}, u32[]{:S(2)}, u32[]{:S(2)}) collective-permute-start(bf16[2,4096]{1,0:T(2,128)(2,1)S(1)} %convolution_convert_fusion.11), channel_id=1, source_target_pairs={{9,0},{10,1},{11,2},{12,3},{13,4},{14,5},{15,6},{16,7},{17,8},{18,... | collective-permute-start | bytes 49160 | tf_op jit(solution)/shard_map/ppermute | solution.py:23
  16.4 55.7 %collective-permute-start.17 = (bf16[2,4096]{1,0:T(2,128)(2,1)S(1)}, bf16[2,4096]{1,0:T(2,128)(2,1)S(1)}, u32[]{:S(2)}, u32[]{:S(2)}) collective-permute-start(bf16[2,4096]{1,0:T(2,128)(2,1)S(1)} %convolution_convert_fusion.10), channel_id=1, source_target_pairs={{8,0},{9,1},{10,2},{11,3},{12,4},{13,5},{14,6},{15,7},{16,8},{17,9... | collective-permute-start | bytes 49160 | tf_op jit(solution)/shard_map/ppermute | solution.py:23
  18.1 56.0 %collective-permute-start.18 = (bf16[2,4096]{1,0:T(2,128)(2,1)S(1)}, bf16[2,4096]{1,0:T(2,128)(2,1)S(1)}, u32[]{:S(2)}, u32[]{:S(2)}) collective-permute-start(bf16[2,4096]{1,0:T(2,128)(2,1)S(1)} %convolution_convert_fusion.9), channel_id=1, source_target_pairs={{7,0},{8,1},{9,2},{10,3},{11,4},{12,5},{13,6},{14,7},{15,8},{16,9}... | collective-permute-start | bytes 49160 | tf_op jit(solution)/shard_map/ppermute | solution.py:23
  19.9 57.8 %collective-permute-start.21 = (bf16[2,4096]{1,0:T(2,128)(2,1)S(1)}, bf16[2,4096]{1,0:T(2,128)(2,1)S(1)}, u32[]{:S(2)}, u32[]{:S(2)}) collective-permute-start(bf16[2,4096]{1,0:T(2,128)(2,1)S(1)} %convolution_convert_fusion.8), channel_id=1, source_target_pairs={{0,7},{1,8},{2,9},{3,10},{4,11},{5,12},{6,13},{7,14},{8,15},{9,16}... | collective-permute-start | bytes 49160 | tf_op jit(solution)/shard_map/ppermute | solution.py:23
  26.6 52.5 %collective-permute-start.22 = (bf16[2,4096]{1,0:T(2,128)(2,1)S(1)}, bf16[2,4096]{1,0:T(2,128)(2,1)S(1)}, u32[]{:S(2)}, u32[]{:S(2)}) collective-permute-start(bf16[2,4096]{1,0:T(2,128)(2,1)S(1)} %convolution_convert_fusion.7), channel_id=1, source_target_pairs={{0,8},{1,9},{2,10},{3,11},{4,12},{5,13},{6,14},{7,15},{8,16},{9,17... | collective-permute-start | bytes 49160 | tf_op jit(solution)/shard_map/ppermute | solution.py:23
  66.8 217.9 %copy-start.30 = (s32[2048]{0:T(1024)}, s32[2048]{0:T(1024)S(1)}, u32[]{:S(2)}) copy-start(s32[2048]{0:T(1024)S(1)} %pad_clamp_fusion) | copy-start | bytes 24580
  67.4 132.4 %copy-start.47 = (s32[1024]{0:T(1024)}, s32[1024]{0:T(1024)S(1)}, u32[]{:S(2)}) copy-start(s32[1024]{0:T(1024)S(1)} %get-tuple-element.222) | copy-start | bytes 12292
  67.4 134.5 %copy-start.54 = (s32[1024]{0:T(1024)}, s32[1024]{0:T(1024)S(1)}, u32[]{:S(2)}) copy-start(s32[1024]{0:T(1024)S(1)} %get-tuple-element.221) | copy-start | bytes 12292
  67.5 115.4 %copy-start.49 = (s32[1024]{0:T(1024)}, s32[1024]{0:T(1024)S(1)}, u32[]{:S(2)}) copy-start(s32[1024]{0:T(1024)S(1)} %get-tuple-element.224) | copy-start | bytes 12292
  67.5 131.3 %copy-start.38 = (s32[1024]{0:T(1024)}, s32[1024]{0:T(1024)S(1)}, u32[]{:S(2)}) copy-start(s32[1024]{0:T(1024)S(1)} %get-tuple-element.223) | copy-start | bytes 12292
  67.5 257.2 %copy-start.42 = (s32[1024]{0:T(1024)}, s32[1024]{0:T(1024)S(1)}, u32[]{:S(2)}) copy-start(s32[1024]{0:T(1024)S(1)} %get-tuple-element.220) | copy-start | bytes 12292
  67.6 12.8 %collective-permute-start.23 = (bf16[2,4096]{1,0:T(2,128)(2,1)S(1)}, bf16[2,4096]{1,0:T(2,128)(2,1)S(1)}, u32[]{:S(2)}, u32[]{:S(2)}) collective-permute-start(bf16[2,4096]{1,0:T(2,128)(2,1)S(1)} %convolution_convert_fusion.6), channel_id=1, source_target_pairs={{0,9},{1,10},{2,11},{3,12},{4,13},{5,14},{6,15},{7,16},{8,17},{9,1... | collective-permute-start | bytes 49160 | tf_op jit(solution)/shard_map/ppermute | solution.py:23
  72.1 27.5 %collective-permute-start.19 = (bf16[4,4096]{1,0:T(4,128)(2,1)S(1)}, bf16[4,4096]{1,0:T(4,128)(2,1)S(1)}, u32[]{:S(2)}, u32[]{:S(2)}) collective-permute-start(bf16[4,4096]{1,0:T(4,128)(2,1)S(1)} %convolution_convert_fusion.1), channel_id=1, source_target_pairs={{1,0},{2,1},{3,2},{4,3},{5,4},{6,5},{7,6},{8,7},{9,8},{10,9},{11,1... | collective-permute-start | bytes 98312 | tf_op jit(solution)/shard_map/ppermute | solution.py:23
  74.1 30.1 %collective-permute-start.20 = (bf16[4,4096]{1,0:T(4,128)(2,1)S(1)}, bf16[4,4096]{1,0:T(4,128)(2,1)S(1)}, u32[]{:S(2)}, u32[]{:S(2)}) collective-permute-start(bf16[4,4096]{1,0:T(4,128)(2,1)S(1)} %convolution_convert_fusion), channel_id=1, source_target_pairs={{0,1},{1,2},{2,3},{3,4},{4,5},{5,6},{6,7},{7,8},{8,9},{9,10},{10,1... | collective-permute-start | bytes 98312 | tf_op jit(solution)/shard_map/ppermute | solution.py:23
  77.7 6.0 collective-permute-start
  79.0 11.6 %collective-permute-start.1 = (bf16[2,4096]{1,0:T(2,128)(2,1)S(1)}, bf16[2,4096]{1,0:T(2,128)(2,1)S(1)}, u32[]{:S(2)}, u32[]{:S(2)}) collective-permute-start(bf16[2,4096]{1,0:T(2,128)(2,1)S(1)} %convolution_convert_fusion.22), channel_id=1, source_target_pairs={{8,0},{9,1},{10,2},{11,3},{12,4},{13,5},{14,6},{15,7},{16,8},{17,9... | collective-permute-start | bytes 49160 | tf_op jit(solution)/shard_map/ppermute | solution.py:23
  80.4 17.9 %collective-permute-start.2 = (bf16[2,4096]{1,0:T(2,128)(2,1)S(1)}, bf16[2,4096]{1,0:T(2,128)(2,1)S(1)}, u32[]{:S(2)}, u32[]{:S(2)}) collective-permute-start(bf16[2,4096]{1,0:T(2,128)(2,1)S(1)} %convolution_convert_fusion.21), channel_id=1, source_target_pairs={{7,0},{8,1},{9,2},{10,3},{11,4},{12,5},{13,6},{14,7},{15,8},{16,9}... | collective-permute-start | bytes 49160 | tf_op jit(solution)/shard_map/ppermute | solution.py:23
  83.7 30.4 %collective-permute-start.5 = (bf16[2,4096]{1,0:T(2,128)(2,1)S(1)}, bf16[2,4096]{1,0:T(2,128)(2,1)S(1)}, u32[]{:S(2)}, u32[]{:S(2)}) collective-permute-start(bf16[2,4096]{1,0:T(2,128)(2,1)S(1)} %convolution_convert_fusion.20), channel_id=1, source_target_pairs={{0,7},{1,8},{2,9},{3,10},{4,11},{5,12},{6,13},{7,14},{8,15},{9,16}... | collective-permute-start | bytes 49160 | tf_op jit(solution)/shard_map/ppermute | solution.py:23
  90.7 23.4 %collective-permute-start.6 = (bf16[2,4096]{1,0:T(2,128)(2,1)S(1)}, bf16[2,4096]{1,0:T(2,128)(2,1)S(1)}, u32[]{:S(2)}, u32[]{:S(2)}) collective-permute-start(bf16[2,4096]{1,0:T(2,128)(2,1)S(1)} %convolution_convert_fusion.19), channel_id=1, source_target_pairs={{0,8},{1,9},{2,10},{3,11},{4,12},{5,13},{6,14},{7,15},{8,16},{9,17... | collective-permute-start | bytes 49160 | tf_op jit(solution)/shard_map/ppermute | solution.py:23
  98.3 15.8 %collective-permute-start.7 = (bf16[2,4096]{1,0:T(2,128)(2,1)S(1)}, bf16[2,4096]{1,0:T(2,128)(2,1)S(1)}, u32[]{:S(2)}, u32[]{:S(2)}) collective-permute-start(bf16[2,4096]{1,0:T(2,128)(2,1)S(1)} %convolution_convert_fusion.18), channel_id=1, source_target_pairs={{0,9},{1,10},{2,11},{3,12},{4,13},{5,14},{6,15},{7,16},{8,17},{9,1... | collective-permute-start | bytes 49160 | tf_op jit(solution)/shard_map/ppermute | solution.py:23
  99.6 14.5 %collective-permute-start.3 = (bf16[4,4096]{1,0:T(4,128)(2,1)S(1)}, bf16[4,4096]{1,0:T(4,128)(2,1)S(1)}, u32[]{:S(2)}, u32[]{:S(2)}) collective-permute-start(bf16[4,4096]{1,0:T(4,128)(2,1)S(1)} %convolution_convert_fusion.5), channel_id=1, source_target_pairs={{1,0},{2,1},{3,2},{4,3},{5,4},{6,5},{7,6},{8,7},{9,8},{10,9},{11,1... | collective-permute-start | bytes 98312 | tf_op jit(solution)/shard_map/ppermute | solution.py:23
  104.2 9.9 %collective-permute-start.4 = (bf16[4,4096]{1,0:T(4,128)(2,1)S(1)}, bf16[4,4096]{1,0:T(4,128)(2,1)S(1)}, u32[]{:S(2)}, u32[]{:S(2)}) collective-permute-start(bf16[4,4096]{1,0:T(4,128)(2,1)S(1)} %convolution_convert_fusion.4), channel_id=1, source_target_pairs={{0,1},{1,2},{2,3},{3,4},{4,5},{5,6},{6,7},{7,8},{8,9},{9,10},{10,1... | collective-permute-start | bytes 98312 | tf_op jit(solution)/shard_map/ppermute | solution.py:23
  352.6 30.8 %collective-permute-start.8 = (bf16[2,4096]{1,0:T(2,128)(2,1)S(1)}, bf16[2,4096]{1,0:T(2,128)(2,1)S(1)}, u32[]{:S(2)}, u32[]{:S(2)}) collective-permute-start(bf16[2,4096]{1,0:T(2,128)(2,1)S(1)} %convolution_convert_fusion.17), channel_id=1, source_target_pairs={{9,0},{10,1},{11,2},{12,3},{13,4},{14,5},{15,6},{16,7},{17,8},{18,... | collective-permute-start | bytes 49160 | tf_op jit(solution)/shard_map/ppermute | solution.py:23
  353.9 30.8 %collective-permute-start.9 = (bf16[2,4096]{1,0:T(2,128)(2,1)S(1)}, bf16[2,4096]{1,0:T(2,128)(2,1)S(1)}, u32[]{:S(2)}, u32[]{:S(2)}) collective-permute-start(bf16[2,4096]{1,0:T(2,128)(2,1)S(1)} %convolution_convert_fusion.16), channel_id=1, source_target_pairs={{8,0},{9,1},{10,2},{11,3},{12,4},{13,5},{14,6},{15,7},{16,8},{17,9... | collective-permute-start | bytes 49160 | tf_op jit(solution)/shard_map/ppermute | solution.py:23
  355.2 34.2 %collective-permute-start.10 = (bf16[2,4096]{1,0:T(2,128)(2,1)S(1)}, bf16[2,4096]{1,0:T(2,128)(2,1)S(1)}, u32[]{:S(2)}, u32[]{:S(2)}) collective-permute-start(bf16[2,4096]{1,0:T(2,128)(2,1)S(1)} %convolution_convert_fusion.15), channel_id=1, source_target_pairs={{7,0},{8,1},{9,2},{10,3},{11,4},{12,5},{13,6},{14,7},{15,8},{16,9}... | collective-permute-start | bytes 49160 | tf_op jit(solution)/shard_map/ppermute | solution.py:23
  356.5 35.2 %collective-permute-start.13 = (bf16[2,4096]{1,0:T(2,128)(2,1)S(1)}, bf16[2,4096]{1,0:T(2,128)(2,1)S(1)}, u32[]{:S(2)}, u32[]{:S(2)}) collective-permute-start(bf16[2,4096]{1,0:T(2,128)(2,1)S(1)} %convolution_convert_fusion.14), channel_id=1, source_target_pairs={{0,7},{1,8},{2,9},{3,10},{4,11},{5,12},{6,13},{7,14},{8,15},{9,16}... | collective-permute-start | bytes 49160 | tf_op jit(solution)/shard_map/ppermute | solution.py:23
  366.7 25.0 %collective-permute-start.14 = (bf16[2,4096]{1,0:T(2,128)(2,1)S(1)}, bf16[2,4096]{1,0:T(2,128)(2,1)S(1)}, u32[]{:S(2)}, u32[]{:S(2)}) collective-permute-start(bf16[2,4096]{1,0:T(2,128)(2,1)S(1)} %convolution_convert_fusion.13), channel_id=1, source_target_pairs={{0,8},{1,9},{2,10},{3,11},{4,12},{5,13},{6,14},{7,15},{8,16},{9,17... | collective-permute-start | bytes 49160 | tf_op jit(solution)/shard_map/ppermute | solution.py:23
  383.4 8.3 %collective-permute-start.15 = (bf16[2,4096]{1,0:T(2,128)(2,1)S(1)}, bf16[2,4096]{1,0:T(2,128)(2,1)S(1)}, u32[]{:S(2)}, u32[]{:S(2)}) collective-permute-start(bf16[2,4096]{1,0:T(2,128)(2,1)S(1)} %convolution_convert_fusion.12), channel_id=1, source_target_pairs={{0,9},{1,10},{2,11},{3,12},{4,13},{5,14},{6,15},{7,16},{8,17},{9,1... | collective-permute-start | bytes 49160 | tf_op jit(solution)/shard_map/ppermute | solution.py:23
  384.7 7.0 %collective-permute-start.11 = (bf16[4,4096]{1,0:T(4,128)(2,1)S(1)}, bf16[4,4096]{1,0:T(4,128)(2,1)S(1)}, u32[]{:S(2)}, u32[]{:S(2)}) collective-permute-start(bf16[4,4096]{1,0:T(4,128)(2,1)S(1)} %convolution_convert_fusion.3), channel_id=1, source_target_pairs={{1,0},{2,1},{3,2},{4,3},{5,4},{6,5},{7,6},{8,7},{9,8},{10,9},{11,1... | collective-permute-start | bytes 98312 | tf_op jit(solution)/shard_map/ppermute | solution.py:23
  389.4 3.1 collective-permute-start.12
  (122 other events, 2651.2 us)
Sparse Core Ops, SparseCore 0:
  511.9 157.6 all-reduce.4
where the time goes:
time: 693 us; the launch traced here: 680 us
  local copies, waits for them, and re-layouts  236 us (34%)
  waiting for transfers between devices  150 us (22%)
  matrix products  121 us (17%)
  starting transfers between devices  81.3 us (12%)
  other arithmetic  72 us (10%)
  between operations  19.1 us (3%)
    psum x1, waiting for transfers between devices, shards(): grad_first = lax.psum(grad_first, ('region', 'brick'))  148 us
    ppermute x24, starting transfers between devices, passed_along(): return lax.ppermute(array, axis, pairs)  81.3 us
    dot_general x54, matrix products, convolve(): jnp.einsum('oc,bcp->bop', weight[k], window, preferred_element_type=jnp.f...  54.9 us
    gather x78, local copies, waits for them, and re-layouts, assemble(): jnp.take(face_table, gather_index[:, direction_index], axis=0)  48.8 us
    select_n x78, other arithmetic, assemble(): jnp.take(face_table, gather_index[:, direction_index], axis=0)  46.4 us
    gather x90, local copies, waits for them, and re-layouts, assemble(): jnp.take(face_rows, jnp.asarray(cell_lists[direction_index]), axis=2)  43.5 us
    dot_general x54, matrix products, weight_grad(): jnp.einsum('bop,bcp->oc', padded_slope, window, preferred_element_type=jn...  35.6 us
    reshape x132, local copies, waits for them, and re-layouts, assemble(): jnp.take(face_table, gather_index[:, direction_index], axis=0)  33.7 us
  transfers between devices with their start and end apart: 25, of which 3 were waited for; matrix products, arithmetic and copies ran while one was open for 9% of the time, Pallas kernels for 0%

commit v1 on v0

v1 whole, which is shorter than its diff:
```python
import jax
import jax.numpy as jnp
import numpy as np
from jax import lax
from jax.experimental import pallas as pl
from jax.experimental.pallas import tpu as pltpu
from jax.sharding import PartitionSpec as P

AXES = ("region", "brick")
GRID_X = 8
ZERO_ROW = 44
ARRIVALS = {
    (-1, 0): (24, 4),
    (1, 0): (28, 4),
    (0, -1): (32, 2),
    (-1, -1): (34, 2),
    (1, -1): (36, 2),
    (0, 1): (38, 2),
    (-1, 1): (40, 2),
    (1, 1): (42, 2),
}
VMEM_LIMIT = 48 * 1024 * 1024
BF = jnp.bfloat16
F32 = jnp.float32


def direction_list():
    return [
        (a, b, c)
        for a in (-1, 0, 1)
        for b in (-1, 0, 1)
        for c in (-1, 0, 1)
        if (a, b, c) != (0, 0, 0)
    ]


DIRECTIONS = direction_list()


def face_of(vector):
    if vector[0] != 0:
        return 0 if vector[0] < 0 else 1
    if vector[1] != 0:
        return 2 if vector[1] < 0 else 3
    return 4 if vector[2] < 0 else 5


SEND_FACE = [face_of(d) for d in DIRECTIONS]
READ_FACE = [face_of(tuple(-t for t in d)) for d in DIRECTIONS]


def face_matrix():
    m = np.zeros((512, 768), np.float32)
    for face in range(6):
        axis = face // 2
        others = [i for i in range(3) if i != axis]
        for u in range(8):
            for v in range(8):
                c = [0, 0, 0]
                c[axis] = 7 if face % 2 else 0
                c[others[0]], c[others[1]] = u, v
                voxel = c[0] * 64 + c[1] * 8 + c[2]
                for half in (0, 64):
                    m[voxel, face * 128 + half + u * 8 + v] = 1
    return m


def spread_matrix(shift):
    m = np.zeros((128, 256), np.float32)
    for p in range(2):
        for y in range(8):
            for z in range(8):
                m[p * 64 + 8 * y + z, p * 128 + 10 * (y + shift) + z + shift] = 1
    return m


def ends(step):
    if step == 0:
        return [(t, t + 1) for t in range(8)]
    return [(7, 0)] if step < 0 else [(0, 9)]


YZ_GROUPS = [((0, 1, c), (0, -1, c)) for c in (-1, 0, 1)] + [((0, 0, 1), (0, 0, -1))]
X_GROUPS = [((1, b, c), (-1, b, c)) for b in (-1, 0, 1) for c in (-1, 0, 1)]


def yz_matrix():
    m = np.zeros((512, 1024), np.float32)
    for g, pair in enumerate(YZ_GROUPS):
        for h, (_, b, c) in enumerate(pair):
            for x in range(8):
                for ys, yd in ends(b):
                    for zs, zd in ends(c):
                        cell = x * 8 + (zs if b != 0 else ys)
                        m[g * 128 + h * 64 + cell, x * 128 + 10 * yd + zd] = 1
    return m


def x_matrix():
    m = np.zeros((1152, 256), np.float32)
    for g, pair in enumerate(X_GROUPS):
        for h, (a, b, c) in enumerate(pair):
            for ys, yd in ends(b):
                for zs, zd in ends(c):
                    lane = (128 if a > 0 else 0) + 10 * yd + zd
                    m[g * 128 + h * 64 + ys * 8 + zs, lane] = 1
    return m


def constant(array):
    return jnp.asarray(array, BF)


def dot(a, b):
    return lax.dot_general(a, b, (((1,), (0,)), ((), ())), preferred_element_type=F32)


def dot_nt(a, b):
    return lax.dot_general(a, b, (((1,), (1,)), ((), ())), preferred_element_type=F32)


def low_half(shape):
    return lax.broadcasted_iota(jnp.int32, shape, len(shape) - 1) < 64


def place(neighbours, place_ref, b, e):
    n = neighbours[b, e]
    mine = lax.axis_index("brick")
    owner = (n >> 2) - lax.axis_index("region") * 32
    dx = (owner & 7) - (mine & 7) + 1
    dy = (owner >> 3) - (mine >> 3) + 1
    where = jnp.where(n >= 0, dy * 3 + dx, 9)
    return n, jnp.clip(where, 0, 9)


def tables_kernel(neighbours, send_ref, index_ref, need, held, where_ref, rank_ref):
    for s in range(10):
        need[s] = 0
        held[s] = 0

    def mark(b, carry):
        for e in range(26):
            n, where = place(neighbours, None, b, e)
            where_ref[b * 26 + e] = where
            need[where] = need[where] | jnp.left_shift(1, b * 6 + SEND_FACE[e])
            held[where] = held[where] | jnp.left_shift(1, (n & 3) * 6 + READ_FACE[e])
        return carry

    lax.fori_loop(0, 4, mark, 0)
    for f in range(24):
        rank_ref[4 * 24 + f] = f
        rank_ref[9 * 24 + f] = ZERO_ROW
    for (x, y), (base, count) in ARRIVALS.items():
        s = (y + 1) * 3 + x + 1
        for t in range(8):
            send_ref[s * 8 + t] = 0
        need_bits, held_bits = need[s], held[s]

        def rank(f, carry):
            sent, got = carry
            send_ref[s * 8 + jnp.minimum(sent, 7)] = f
            rank_ref[s * 24 + f] = base + jnp.minimum(got, count - 1)
            return sent + ((need_bits >> f) & 1), got + ((held_bits >> f) & 1)

        lax.fori_loop(0, 24, rank, (0, 0), unroll=True)

    def index(b, carry):
        for e in range(26):
            n = neighbours[b, e]
            row = where_ref[b * 26 + e] * 24 + (n & 3) * 6 + READ_FACE[e]
            index_ref[b * 26 + e] = rank_ref[row]
        return carry

    lax.fori_loop(0, 4, index, 0)


def tables(neighbours):
    smem = pl.BlockSpec(memory_space=pltpu.SMEM)
    return pl.pallas_call(
        tables_kernel,
        out_shape=(
            jax.ShapeDtypeStruct((80,), jnp.int32),
            jax.ShapeDtypeStruct((104,), jnp.int32),
        ),
        in_specs=[smem],
        out_specs=(smem, smem),
        scratch_shapes=[
            pltpu.SMEM((10,), jnp.int32),
            pltpu.SMEM((10,), jnp.int32),
            pltpu.SMEM((104,), jnp.int32),
            pltpu.SMEM((240,), jnp.int32),
        ],
        name="link_tables",
    )(neighbours)


def send_slots(send_ref, x, y):
    s = (y + 1) * 3 + x + 1
    return [send_ref[s * 8 + t] for t in range(4 if y == 0 else 2)]


def pack(send_ref, tile_of, right_ref, left_ref, up_ref, down_ref):
    for ref, x in ((right_ref, 1), (left_ref, -1)):
        ids = send_slots(send_ref, x, 0) + send_slots(send_ref, x, -1) + send_slots(send_ref, x, 1)
        for t, face in enumerate(ids):
            ref[t] = tile_of(face)
    for ref, y in ((up_ref, 1), (down_ref, -1)):
        for t, face in enumerate(send_slots(send_ref, 0, y)):
            ref[t] = tile_of(face)


def first_kernel(
    send_ref, features, cotangent, active, face_mat,
    values_ref, faces_ref, right_ref, left_ref, up_ref, down_ref,
):
    for b in range(4):
        mask = active[b : b + 1, :].astype(F32)
        f = features[b].astype(F32)
        values_ref[b * 64 : b * 64 + 64, :] = (mask * (f / (1.0 + jnp.exp(-f)))).astype(BF)
        values_ref[256 + b * 64 : 320 + b * 64, :] = (mask * cotangent[b].astype(F32)).astype(BF)
    faces = dot(values_ref[...], face_mat[...]).astype(BF)
    for a in range(2):
        for b in range(4):
            for f in range(6):
                row = (a * 4 + b) * 64
                faces_ref[a, b * 6 + f] = faces[row : row + 64, f * 128 : f * 128 + 128]
    low = low_half((64, 128))
    pack(
        send_ref,
        lambda face: jnp.where(low, faces_ref[0, face], faces_ref[1, face]),
        right_ref, left_ref, up_ref, down_ref,
    )


def fill_table(table, faces, zero_too, arrays, groups):
    low = low_half((64, 128))
    for a in range(arrays):
        for f in range(24):
            table[a, f] = faces[a, f] if arrays == 2 else faces[f]
        table[a, ZERO_ROW] = jnp.zeros((64, 128), BF)
    for ref, start, base in groups:
        for t in range(start, ref.shape[0]) if start else range(4 if base < 32 else 6):
            tile = ref[t]
            if arrays == 1:
                table[0, base + t] = tile
                continue
            swapped = jnp.concatenate([tile[:, 64:], tile[:, :64]], axis=1)
            table[0, base + t] = jnp.where(low, tile, swapped)
            table[1, base + t] = jnp.where(low, swapped, tile)


def build_padded(index_ref, table, values, ext, side_yz, side_x, e_int, e_yz, e_x, arrays):
    low = low_half((64, 128))
    for a in range(arrays):
        for b in range(4):
            row = (a * 4 + b) * 64
            for side, pairs in ((side_yz, YZ_GROUPS), (side_x, X_GROUPS)):
                for g, (first, second) in enumerate(pairs):
                    lo = index_ref[b * 26 + DIRECTIONS.index(first)]
                    hi = index_ref[b * 26 + DIRECTIONS.index(second)]
                    side[row : row + 64, g * 128 : g * 128 + 128] = jnp.where(
                        low, table[a, lo], table[a, hi]
                    )
    outer = dot(side_x[...], e_x[...]).astype(BF)
    ext[:, 0:128] = outer[:, 0:128]
    ext[:, 1152:1280] = outer[:, 128:256]
    for m in range(4):
        inner = dot(values[:, m * 128 : m * 128 + 128], e_int[...])
        inner = inner + dot(side_yz[...], e_yz[:, m * 256 : m * 256 + 256])
        ext[:, 128 + m * 256 : 384 + m * 256] = inner.astype(BF)


def columns(ext, row, col):
    for p in range(10):
        plane = ext[row : row + 64, p * 128 : p * 128 + 128]
        for j in range(3):
            for l in range(3):
                s = 10 * j + l
                k = 3 * j + l
                moved = plane if s == 0 else pltpu.roll(plane, 128 - s, 1)
                col[k * 64 : k * 64 + 64, p * 128 : p * 128 + 128] = moved


def three_planes(product):
    return (
        product[0:64, 0:1024] + product[64:128, 128:1152] + product[128:192, 256:1280]
    )


def second_kernel(
    send_ref, index_ref, values, faces, from_left, from_right, from_up, from_down, active,
    w_first, w_back, gain_ref, shift_ref, face_mat, e_int, e_out, e_back, e_yz, e_x,
    hidden_ref, hidden_faces, right_ref, left_ref, up_ref, down_ref, sums_ref,
    table, ext, side_yz, side_x, col_a, col_s, stack_h, stack_s, total_h, total_s, mask_ref,
):
    groups = ((from_left, 0, 24), (from_right, 0, 28), (from_up, 0, 32), (from_down, 0, 38))
    fill_table(table, faces, True, 2, groups)
    build_padded(index_ref, table, values, ext, side_yz, side_x, e_int, e_yz, e_x, 2)
    stack_h[...] = jnp.zeros_like(stack_h)
    stack_s[...] = jnp.zeros_like(stack_s)
    on = active[...].astype(F32).astype(BF)
    for m in range(4):
        mask_ref[:, m * 256 : m * 256 + 256] = dot(on[:, m * 128 : m * 128 + 128], e_out[...])
    gain = 1.0 + gain_ref[...]
    shift = shift_ref[...]
    for b in range(4):
        columns(ext, b * 64, col_a)
        columns(ext, 256 + b * 64, col_s)
        pre = three_planes(dot(w_first[...], col_a[...]))
        back = three_planes(dot(w_back[...], col_s[...]))
        mask = mask_ref[b : b + 1, :]
        shaped = pre * gain + shift
        gate = 1.0 / (1.0 + jnp.exp(-shaped))
        hidden = (mask * (shaped * gate)).astype(BF)
        slope = (back * mask * gate * (1.0 + shaped * (1.0 - gate)) * gain).astype(BF)
        for i in range(3):
            stack_h[i * 64 : i * 64 + 64, i * 128 : i * 128 + 1024] = hidden
            stack_s[i * 64 : i * 64 + 64, i * 128 : i * 128 + 1024] = slope
        for m in range(4):
            hidden_ref[b * 64 : b * 64 + 64, m * 128 : m * 128 + 128] = dot(
                hidden[:, m * 256 : m * 256 + 256], e_back[...]
            ).astype(BF)
        part_h = dot_nt(col_s[...], stack_h[...])
        part_s = dot_nt(col_a[...], stack_s[...])
        total_h[...] = part_h if b == 0 else total_h[...] + part_h
        total_s[...] = part_s if b == 0 else total_s[...] + part_s
    for t, total in enumerate((total_h, total_s)):
        base = t * 864
        sums_ref[base : base + 576, :] = total[:, 0:128]
        sums_ref[base + 576 : base + 864, :] = jnp.concatenate(
            [total[0:288, 128:192], total[288:576, 128:192]], axis=1
        )
    sums_ref[1728:2048, :] = jnp.zeros((320, 128), F32)
    out = dot(hidden_ref[...], face_mat[...]).astype(BF)
    for b in range(4):
        for f in range(6):
            hidden_faces[b * 6 + f] = out[b * 64 : b * 64 + 64, f * 128 : f * 128 + 128]
    pack(send_ref, lambda face: hidden_faces[face], right_ref, left_ref, up_ref, down_ref)


def third_kernel(
    index_ref, hidden, hidden_faces, from_left, from_right, from_up, from_down, active, features,
    w_second, e_int, e_out, e_back, e_yz, e_x, sums,
    out_ref, first_ref, second_ref,
    table, ext, side_yz, side_x, col, mask_ref,
):
    groups = ((from_left, 0, 24), (from_right, 0, 28), (from_up, 0, 32), (from_down, 0, 38))
    fill_table(table, hidden_faces, True, 1, groups)
    build_padded(index_ref, table, hidden, ext, side_yz, side_x, e_int, e_yz, e_x, 1)
    on = active[...].astype(F32).astype(BF)
    for m in range(4):
        mask_ref[:, m * 256 : m * 256 + 256] = dot(on[:, m * 128 : m * 128 + 128], e_out[...])
    for b in range(4):
        columns(ext, b * 64, col)
        second = mask_ref[b : b + 1, :] * three_planes(dot(w_second[...], col[...]))
        for m in range(4):
            own = dot(features[b, :, m * 128 : m * 128 + 128], e_out[...])
            own = (own + second[:, m * 256 : m * 256 + 256]).astype(BF)
            out_ref[b, :, m * 128 : m * 128 + 128] = dot(own, e_back[...]).astype(BF)
    for t in range(2):
        base = t * 864
        for i in range(3):
            for jl in range(9):
                if i < 2:
                    block = sums[base + jl * 64 : base + jl * 64 + 64, i * 64 : i * 64 + 64]
                else:
                    pieces = []
                    for r in (jl * 64, jl * 64 + 32):
                        lane, at = (0, r) if r < 288 else (64, r - 288)
                        at += base + 576
                        pieces.append(sums[at : at + 32, lane : lane + 64])
                    block = jnp.concatenate(pieces, axis=0)
                k = 9 * i + jl
                if t == 0:
                    second_ref[26 - k] = block
                else:
                    first_ref[k] = block.T


def sent(array, step):
    pairs = []
    for i in range(32):
        j = i + step
        if 0 <= j < 32 and (abs(step) == GRID_X or i // GRID_X == j // GRID_X):
            pairs.append((i, j))
    return lax.ppermute(array, "brick", pairs)


def exchange(right, left, up, down):
    from_left = sent(right, 1)
    from_right = sent(left, -1)
    from_up = sent(jnp.concatenate([up, from_left[6:8], from_right[6:8]], axis=0), GRID_X)
    from_down = sent(jnp.concatenate([down, from_left[4:6], from_right[4:6]], axis=0), -GRID_X)
    return from_left, from_right, from_up, from_down


def stacked(weight):
    return weight.reshape(3, 9, 64, 64).transpose(0, 2, 1, 3).reshape(192, 576)


def shape(dims, dtype=BF):
    return jax.ShapeDtypeStruct(dims, dtype)


def call(kernel, outs, scratch, prefetch, *operands):
    smem = pl.BlockSpec(memory_space=pltpu.SMEM)
    vmem = pl.BlockSpec(memory_space=pltpu.VMEM)
    return pl.pallas_call(
        kernel,
        out_shape=tuple(outs),
        in_specs=[smem] * prefetch + [vmem] * (len(operands) - prefetch),
        out_specs=tuple(vmem for _ in outs),
        scratch_shapes=scratch,
        compiler_params=pltpu.CompilerParams(vmem_limit_bytes=VMEM_LIMIT),
        name=kernel.__name__,
    )(*operands)


def shards(
    features, active, neighbours, first_weight, second_weight, film_scale, film_shift, cotangent
):
    face_mat = constant(face_matrix())
    e_int, e_out = constant(spread_matrix(1)), constant(spread_matrix(0))
    e_back = constant(spread_matrix(0).T)
    e_yz, e_x = constant(yz_matrix()), constant(x_matrix())
    messages = [shape((8, 64, 128)), shape((8, 64, 128)), shape((2, 64, 128)), shape((2, 64, 128))]

    send_ids, index = tables(neighbours)
    values, faces, *outgoing = call(
        first_kernel,
        [shape((512, 512)), shape((2, 24, 64, 128))] + messages,
        [],
        1,
        send_ids, features, cotangent, active, face_mat,
    )
    arrived = exchange(*outgoing)
    w_first = stacked(first_weight)
    w_second = stacked(second_weight)
    w_back = stacked(second_weight[::-1].transpose(0, 2, 1))

    hidden, hidden_faces, *outgoing, sums = call(
        second_kernel,
        [shape((256, 512)), shape((24, 64, 128))] + messages + [shape((2048, 128), F32)],
        [
            pltpu.VMEM((2, 45, 64, 128), BF),
            pltpu.VMEM((512, 1280), BF),
            pltpu.VMEM((512, 512), BF),
            pltpu.VMEM((512, 1152), BF),
            pltpu.VMEM((576, 1280), BF),
            pltpu.VMEM((576, 1280), BF),
            pltpu.VMEM((192, 1280), BF),
            pltpu.VMEM((192, 1280), BF),
            pltpu.VMEM((576, 192), F32),
            pltpu.VMEM((576, 192), F32),
            pltpu.VMEM((4, 1024), F32),
        ],
        2,
        send_ids, index, values, faces, *arrived, active, w_first, w_back,
        film_scale.reshape(64, 1), film_shift.reshape(64, 1),
        face_mat, e_int, e_out, e_back, e_yz, e_x,
    )
    arrived = exchange(*outgoing)
    parts = lax.all_to_all(sums.reshape(128, 16, 128), AXES, 0, 0, tiled=True)
    mine = jnp.sum(parts, axis=0)
    sums = lax.all_to_all(jnp.broadcast_to(mine, (128, 16, 128)), AXES, 0, 0, tiled=True)
    block_output, grad_first, grad_second = call(
        third_kernel,
        [shape((4, 64, 512)), shape((27, 64, 64), F32), shape((27, 64, 64), F32)],
        [
            pltpu.VMEM((1, 45, 64, 128), BF),
            pltpu.VMEM((256, 1280), BF),
            pltpu.VMEM((256, 512), BF),
            pltpu.VMEM((256, 1152), BF),
            pltpu.VMEM((576, 1280), BF),
            pltpu.VMEM((4, 1024), F32),
        ],
        1,
        index, hidden, hidden_faces, *arrived, active, features, w_second,
        e_int, e_out, e_back, e_yz, e_x, sums.reshape(2048, 128),
    )
    return block_output, grad_first, grad_second


def solution(mesh):
    split = P(AXES, None, None)
    rows = P(AXES, None)
    return jax.shard_map(
        shards,
        mesh=mesh,
        in_specs=(split, rows, rows, P(), P(), P(), P(), split),
        out_specs=(split, P(), P()),
        check_vma=False,
    )
```

time: 693 us -> 131 us (0.19); the launches traced: 680 us -> 130 us
  local copies, waits for them, and re-layouts: 236 us -> 34.7 us
  waiting for transfers between devices: 150 us -> 13.1 us
  matrix products: 121 us -> 0 us
  other arithmetic: 72 us -> 2.1 us
  starting transfers between devices: 81.3 us -> 28.5 us
  blocking collectives: 0 us -> 28.5 us
  Pallas kernels: 0 us -> 22 us
  between operations: 19.1 us -> 1.02 us
    psum x1 -> x0, waiting for transfers between devices: 148 us -> none  [shards(): grad_first = lax.psum(grad_first, ('region', 'brick'))]
    gather x203 -> x0, local copies, waits for them, and re-layouts: 146 us -> none  [the longest x78 48.8 us: assemble(): jnp.take(face_table, gather_index[:, direction_index], axis=0)]
    dot_general x159 -> x0, matrix products: 121 us -> none  [the longest x54 54.9 us: convolve(): jnp.einsum('oc,bcp->bop', weight[k], window, preferred_element_type=jnp.f...]
    ppermute x24 -> x8, starting transfers between devices: 81.3 us -> 23.7 us  [sent(): return lax.ppermute(array, 'brick', pairs)]
    select_n x87 -> x0, other arithmetic: 48.9 us -> none  [the longest x78 46.4 us: assemble(): jnp.take(face_table, gather_index[:, direction_index], axis=0)]
    all_to_all x0 -> x1, blocking collectives: none -> 28.5 us  [shards(): parts = lax.all_to_all(sums.reshape(128, 16, 128), AXES, 0, 0, tiled=True)]
    reshape x135 -> x11, local copies, waits for them, and re-layouts: 34.8 us -> 9.53 us  [the longest x9 8.74 us: stacked(): return weight.reshape(3, 9, 64, 64).transpose(0, 2, 1, 3).reshape(192, 576)]
    pallas_call x0 -> x4, Pallas kernels: none -> 22 us  [the longest x3 18.7 us: call(): pl.pallas_call(kernel, out_shape=tuple(outs), in_specs=[smem] * prefetch...]
  transfers between devices with their start and end apart: 25 -> 9, of which waited for: 3 -> 3; matrix products, arithmetic and copies ran while one was open for 9% -> 9% of each run, Pallas kernels for 0% -> 0%
where the time goes in v1:
time: 131 us; the launch traced here: 130 us
  local copies, waits for them, and re-layouts  34.7 us (26%)
  starting transfers between devices  28.5 us (22%)
  blocking collectives  28.5 us (22%)
  Pallas kernels  22 us (17%)
  waiting for transfers between devices  13.1 us (10%)
  other arithmetic  2.1 us (2%)
    all_to_all x1, blocking collectives, shards(): parts = lax.all_to_all(sums.reshape(128, 16, 128), AXES, 0, 0, tiled=True)  28.5 us
    unnamed x90, local copies, waits for them, and re-layouts  24 us
    ppermute x8, starting transfers between devices, sent(): return lax.ppermute(array, 'brick', pairs)  23.7 us
    pallas_call x3, Pallas kernels, call(): pl.pallas_call(kernel, out_shape=tuple(outs), in_specs=[smem] * prefetch...  18.7 us
    ppermute x8, waiting for transfers between devices, sent(): return lax.ppermute(array, 'brick', pairs)  13.1 us
    reshape x9, local copies, waits for them, and re-layouts, stacked(): return weight.reshape(3, 9, 64, 64).transpose(0, 2, 1, 3).reshape(192, 576)  8.74 us
    all_to_all x1, starting transfers between devices, shards(): lax.all_to_all(jnp.broadcast_to(mine, (128, 16, 128)), AXES, 0, 0, tiled=...  4.8 us
    pallas_call x1, Pallas kernels, tables(): pl.pallas_call(tables_kernel, out_shape=(jax.ShapeDtypeStruct((80,), jnp....  3.35 us
  transfers between devices with their start and end apart: 9, of which 3 were waited for; matrix products, arithmetic and copies ran while one was open for 9% of the time, Pallas kernels for 0%

profile of v1, /device:TPU:1, one launch (start us, length us, event | category | flops | bytes accessed | tf_op | source)
XLA Modules:
  0.0 129.9 jit_solution(16887979727102339577)
XLA Ops:
  0.6 3.3 %link_tables.1 = (s32[80]{0:T(128)}, s32[104]{0:T(128)}) custom-call(s32[4,26]{1,0:T(4,128)} %neighbours.1), custom_call_target="tpu_custom_call" | custom-call | tf_op jit(solution)/shard_map/link_tables/pallas_call | solution.py:179
  4.6 1.1 copy-done.1
  5.8 0.9 copy-done.4
  6.7 0.9 copy-done.19
  8.4 1.3 first_kernel.1
  10.6 4.7 %collective-permute-start = (bf16[8,64,128]{2,1,0:T(8,128)(2,1)S(1)}, bf16[8,64,128]{2,1,0:T(8,128)(2,1)S(1)}, u32[]{:S(2)}, u32[]{:S(2)}) collective-permute-start(bf16[8,64,128]{2,1,0:T(8,128)(2,1)S(1)} %get-tuple-element.22), channel_id=1, source_target_pairs={{0,1},{1,2},{2,3},{3,4},{4,5},{5,6},{6,7},{8,9},{9,10},{10,11},{11... | collective-permute-start | bytes 393224 | tf_op jit(solution)/shard_map/ppermute | solution.py:386
  15.3 1.9 %collective-permute-start.1 = (bf16[8,64,128]{2,1,0:T(8,128)(2,1)S(1)}, bf16[8,64,128]{2,1,0:T(8,128)(2,1)S(1)}, u32[]{:S(2)}, u32[]{:S(2)}) collective-permute-start(bf16[8,64,128]{2,1,0:T(8,128)(2,1)S(1)} %get-tuple-element.23), channel_id=1, source_target_pairs={{1,0},{2,1},{3,2},{4,3},{5,4},{6,5},{7,6},{9,8},{10,9},{11,10},{12... | collective-permute-start | bytes 393224 | tf_op jit(solution)/shard_map/ppermute | solution.py:386
  17.2 4.3 %collective-permute-done.1.from_right = bf16[8,64,128]{2,1,0:T(8,128)(2,1)S(1)} collective-permute-done((bf16[8,64,128]{2,1,0:T(8,128)(2,1)S(1)}, bf16[8,64,128]{2,1,0:T(8,128)(2,1)S(1)}, u32[]{:S(2)}, u32[]{:S(2)}) %collective-permute-start.1) | collective-permute-done | bytes 131104 | tf_op jit(solution)/shard_map/ppermute | solution.py:386
  22.2 1.3 collective-permute-start.3
  24.2 4.2 %collective-permute-start.2 = (bf16[6,64,128]{2,1,0:T(8,128)(2,1)}, bf16[6,64,128]{2,1,0:T(8,128)(2,1)S(1)}, u32[]{:S(2)}, u32[]{:S(2)}) collective-permute-start(bf16[6,64,128]{2,1,0:T(8,128)(2,1)} %pad_maximum_fusion), channel_id=1, source_target_pairs={{0,8},{1,9},{2,10},{3,11},{4,12},{5,13},{6,14},{7,15},{8,16},{9,17... | collective-permute-start | bytes 294920 | tf_op jit(solution)/shard_map/ppermute | solution.py:386
  30.1 0.9 copy.22
  31.1 1.1 reshape.37
  32.1 1.2 copy.24.w_first
  36.1 1.1 copy-done.7
  37.2 0.9 copy-done.11
  38.1 0.9 copy-done.13
  43.3 10.7 %second_kernel.1 = (bf16[256,512]{1,0:T(8,128)(2,1)S(1)}, bf16[24,64,128]{2,1,0:T(8,128)(2,1)S(1)}, bf16[8,64,128]{2,1,0:T(8,128)(2,1)S(1)}, bf16[8,64,128]{2,1,...) custom-call(s32[80]{0:T(128)S(1)} %copy-done.36, ...), custom_call_target="tpu_custom_call" | custom-call | tf_op jit(solution)/shard_map/second_kernel/pallas_call | solution.py:408
  57.9 28.5 %all_to_all.10 = f32[128,16,128]{2,1,0:T(8,128)S(1)} all-to-all(f32[128,16,128]{2,1,0:T(8,128)S(1)} %bitcast.21), channel_id=1, replica_groups=mesh['region'=4,'brick'=32] {'region','brick'}, dimensions={0} | all-to-all | bytes 2097152 | tf_op jit(solution)/shard_map/all_to_all | solution.py:463
  86.6 1.1 broadcast_in_dim.3
  87.7 4.8 %all-to-all-start.1 = ((f32[128,16,128]{2,1,0:T(8,128)}), f32[128,16,128]{2,1,0:T(8,128)S(1)}, u32[]{:S(2)}, u32[]{:S(2)}) async-start(f32[128,16,128]{2,1,0:T(8,128)} %broadcast_in_dim.3), calls=%async_computation.1 | async-start | bytes 2097152 | tf_op jit(solution)/shard_map/all_to_all | solution.py:465
  92.5 3.8 %collective-permute-start.4 = (bf16[8,64,128]{2,1,0:T(8,128)(2,1)S(1)}, bf16[8,64,128]{2,1,0:T(8,128)(2,1)S(1)}, u32[]{:S(2)}, u32[]{:S(2)}) collective-permute-start(bf16[8,64,128]{2,1,0:T(8,128)(2,1)S(1)} %copy-done.40), channel_id=1, source_target_pairs={{0,1},{1,2},{2,3},{3,4},{4,5},{5,6},{6,7},{8,9},{9,10},{10,11},{11... | collective-permute-start | bytes 393224 | tf_op jit(solution)/shard_map/ppermute | solution.py:386
  96.3 1.9 %collective-permute-start.5 = (bf16[8,64,128]{2,1,0:T(8,128)(2,1)S(1)}, bf16[8,64,128]{2,1,0:T(8,128)(2,1)S(1)}, u32[]{:S(2)}, u32[]{:S(2)}) collective-permute-start(bf16[8,64,128]{2,1,0:T(8,128)(2,1)S(1)} %copy-done.38), channel_id=1, source_target_pairs={{1,0},{2,1},{3,2},{4,3},{5,4},{6,5},{7,6},{9,8},{10,9},{11,10},{12... | collective-permute-start | bytes 393224 | tf_op jit(solution)/shard_map/ppermute | solution.py:386
  98.2 6.3 %collective-permute-done.4.from_left = bf16[8,64,128]{2,1,0:T(8,128)(2,1)S(1)} collective-permute-done((bf16[8,64,128]{2,1,0:T(8,128)(2,1)S(1)}, bf16[8,64,128]{2,1,0:T(8,128)(2,1)S(1)}, u32[]{:S(2)}, u32[]{:S(2)}) %collective-permute-start.4) | collective-permute-done | bytes 131104 | tf_op jit(solution)/shard_map/ppermute | solution.py:386
  104.5 2.4 %collective-permute-done.5.from_right = bf16[8,64,128]{2,1,0:T(8,128)(2,1)S(1)} collective-permute-done((bf16[8,64,128]{2,1,0:T(8,128)(2,1)S(1)}, bf16[8,64,128]{2,1,0:T(8,128)(2,1)S(1)}, u32[]{:S(2)}, u32[]{:S(2)}) %collective-permute-start.5) | collective-permute-done | bytes 131104 | tf_op jit(solution)/shard_map/ppermute | solution.py:386
  107.7 1.3 collective-permute-start.7
  109.6 4.6 %collective-permute-start.6 = (bf16[6,64,128]{2,1,0:T(8,128)(2,1)}, bf16[6,64,128]{2,1,0:T(8,128)(2,1)}, u32[]{:S(2)}, u32[]{:S(2)}) collective-permute-start(bf16[6,64,128]{2,1,0:T(8,128)(2,1)} %pad_maximum_fusion.2), channel_id=1, source_target_pairs={{0,8},{1,9},{2,10},{3,11},{4,12},{5,13},{6,14},{7,15},{8,16},{9,17... | collective-permute-start | bytes 294920 | tf_op jit(solution)/shard_map/ppermute | solution.py:386
  114.2 1.3 %copy.28 = bf16[3,9,64,64]{2,0,3,1:T(4,128)(2,1)} copy(bf16[3,9,64,64]{3,2,1,0:T(8,128)(2,1)S(1)} %bitcast.25) | data formatting | bytes 442368 | tf_op jit(solution)/shard_map/reshape | solution.py:398
  115.6 2.2 %reshape.43 = bf16[192,576]{0,1:T(8,128)(2,1)} reshape(bf16[3,64,9,64]{1,0,3,2:T(4,128)(2,1)} %bitcast.24) | data formatting | bytes 442368 | tf_op jit(solution)/shard_map/reshape | solution.py:398
  117.7 1.2 copy.29.w_second
  119.6 1.0 copy-done.9
  122.3 0.9 copy-done.21
  123.2 6.7 %third_kernel.1 = (bf16[4,64,512]{2,1,0:T(8,128)(2,1)}, f32[27,64,64]{2,1,0:T(8,128)}, f32[27,64,64]{2,1,0:T(8,128)}) custom-call(s32[104]{0:T(128)S(1)} %copy-done.35, bf16[256,512]{1,0:T(8,128)(2,1)S(1)} %copy-done.21, bf16[24,64,128]{2,1,0:T(8,128)(2,1)S(1)} %copy-done.9, bf16[8,64,128]{2,1,0:T(8,128)(2,1)S(1)} %collective-permute-done.4.from_left, ...), custom_call_target="tpu_custom_call" | custom-call | tf_op jit(solution)/shard_map/third_kernel/pallas_call | solution.py:408
  (103 shorter events, 20.0 us)
Async XLA Ops:
  4.6 1.1 copy-start.1
  5.8 0.9 copy-start.4
  6.7 0.9 copy-start.19
  10.6 17.8 %copy-start.41 = (bf16[27,64,64]{2,1,0:T(8,128)(2,1)S(1)}, bf16[27,64,64]{2,1,0:T(8,128)(2,1)}, u32[]{:S(2)}) copy-start(bf16[27,64,64]{2,1,0:T(8,128)(2,1)} %param.18) | copy-start | bytes 663556
  10.6 6.7 %collective-permute-start = (bf16[8,64,128]{2,1,0:T(8,128)(2,1)S(1)}, bf16[8,64,128]{2,1,0:T(8,128)(2,1)S(1)}, u32[]{:S(2)}, u32[]{:S(2)}) collective-permute-start(bf16[8,64,128]{2,1,0:T(8,128)(2,1)S(1)} %get-tuple-element.22), channel_id=1, source_target_pairs={{0,1},{1,2},{2,3},{3,4},{4,5},{5,6},{6,7},{8,9},{9,10},{10,11},{11... | collective-permute-start | bytes 393224 | tf_op jit(solution)/shard_map/ppermute | solution.py:386
  15.3 6.3 %collective-permute-start.1 = (bf16[8,64,128]{2,1,0:T(8,128)(2,1)S(1)}, bf16[8,64,128]{2,1,0:T(8,128)(2,1)S(1)}, u32[]{:S(2)}, u32[]{:S(2)}) collective-permute-start(bf16[8,64,128]{2,1,0:T(8,128)(2,1)S(1)} %get-tuple-element.23), channel_id=1, source_target_pairs={{1,0},{2,1},{3,2},{4,3},{5,4},{6,5},{7,6},{9,8},{10,9},{11,10},{12... | collective-permute-start | bytes 393224 | tf_op jit(solution)/shard_map/ppermute | solution.py:386
  17.2 4.4 %copy-start.10 = (bf16[8,64,128]{2,1,0:T(8,128)(2,1)}, bf16[8,64,128]{2,1,0:T(8,128)(2,1)S(1)}, u32[]{:S(2)}) copy-start(bf16[8,64,128]{2,1,0:T(8,128)(2,1)S(1)} %collective-permute-done.from_left) | copy-start | bytes 393220
  22.2 11.9 %collective-permute-start.3 = (bf16[6,64,128]{2,1,0:T(8,128)(2,1)S(1)}, bf16[6,64,128]{2,1,0:T(8,128)(2,1)S(1)}, u32[]{:S(2)}, u32[]{:S(2)}) collective-permute-start(bf16[6,64,128]{2,1,0:T(8,128)(2,1)S(1)} %pad_maximum_fusion.1), channel_id=1, source_target_pairs={{8,0},{9,1},{10,2},{11,3},{12,4},{13,5},{14,6},{15,7},{16,8},{17,9... | collective-permute-start | bytes 294920 | tf_op jit(solution)/shard_map/ppermute | solution.py:386
  24.2 10.6 %collective-permute-start.2 = (bf16[6,64,128]{2,1,0:T(8,128)(2,1)}, bf16[6,64,128]{2,1,0:T(8,128)(2,1)S(1)}, u32[]{:S(2)}, u32[]{:S(2)}) collective-permute-start(bf16[6,64,128]{2,1,0:T(8,128)(2,1)} %pad_maximum_fusion), channel_id=1, source_target_pairs={{0,8},{1,9},{2,10},{3,11},{4,12},{5,13},{6,14},{7,15},{8,16},{9,17... | collective-permute-start | bytes 294920 | tf_op jit(solution)/shard_map/ppermute | solution.py:386
  29.1 1.0 copy-start.42
  31.0 4.4 %copy-start.2 = (bf16[512,768]{1,0:T(8,128)(2,1)S(1)}, bf16[512,768]{1,0:T(8,128)(2,1)}, u32[]{:S(2)}) copy-start(bf16[512,768]{1,0:T(8,128)(2,1)} %constant.14.clone.face_mat) | copy-start | bytes 2359300
  31.1 4.4 %copy-start.3 = (bf16[1152,256]{1,0:T(8,128)(2,1)S(1)}, bf16[1152,256]{1,0:T(8,128)(2,1)}, u32[]{:S(2)}) copy-start(bf16[1152,256]{1,0:T(8,128)(2,1)} %constant.19.clone.e_x) | copy-start | bytes 1769476
  32.1 1.2 copy-start.43
  32.1 1.3 copy-start.44
  33.3 2.1 %copy-start.14 = (bf16[128,256]{1,0:T(8,128)(2,1)S(1)}, bf16[128,256]{1,0:T(8,128)(2,1)}, u32[]{:S(2)}) copy-start(bf16[128,256]{1,0:T(8,128)(2,1)} %constant.15.clone.e_int) | copy-start | bytes 196612
  33.4 2.0 %copy-start.28 = (s32[4,512]{1,0:T(4,128)S(1)}, s32[4,512]{1,0:T(4,128)}, u32[]{:S(2)}) copy-start(s32[4,512]{1,0:T(4,128)} %active.5) | copy-start | bytes 24580
  36.1 1.1 copy-start.7
  38.1 0.9 copy-start.13
  87.7 4.8 %copy-start.40 = (bf16[8,64,128]{2,1,0:T(8,128)(2,1)S(1)}, bf16[8,64,128]{2,1,0:T(8,128)(2,1)}, u32[]{:S(2)}) copy-start(bf16[8,64,128]{2,1,0:T(8,128)(2,1)} %copy-done.39) | copy-start | bytes 393220
  87.7 8.7 %copy-start.38 = (bf16[8,64,128]{2,1,0:T(8,128)(2,1)S(1)}, bf16[8,64,128]{2,1,0:T(8,128)(2,1)}, u32[]{:S(2)}) copy-start(bf16[8,64,128]{2,1,0:T(8,128)(2,1)} %copy-done.37) | copy-start | bytes 393220
  87.7 31.3 %all-to-all-start.1 = ((f32[128,16,128]{2,1,0:T(8,128)}), f32[128,16,128]{2,1,0:T(8,128)S(1)}, u32[]{:S(2)}, u32[]{:S(2)}) async-start(f32[128,16,128]{2,1,0:T(8,128)} %broadcast_in_dim.3), calls=%async_computation.1 | async-start | bytes 2097152 | tf_op jit(solution)/shard_map/all_to_all | solution.py:465
  92.5 12.1 %collective-permute-start.4 = (bf16[8,64,128]{2,1,0:T(8,128)(2,1)S(1)}, bf16[8,64,128]{2,1,0:T(8,128)(2,1)S(1)}, u32[]{:S(2)}, u32[]{:S(2)}) collective-permute-start(bf16[8,64,128]{2,1,0:T(8,128)(2,1)S(1)} %copy-done.40), channel_id=1, source_target_pairs={{0,1},{1,2},{2,3},{3,4},{4,5},{5,6},{6,7},{8,9},{9,10},{10,11},{11... | collective-permute-start | bytes 393224 | tf_op jit(solution)/shard_map/ppermute | solution.py:386
  96.3 10.7 %collective-permute-start.5 = (bf16[8,64,128]{2,1,0:T(8,128)(2,1)S(1)}, bf16[8,64,128]{2,1,0:T(8,128)(2,1)S(1)}, u32[]{:S(2)}, u32[]{:S(2)}) collective-permute-start(bf16[8,64,128]{2,1,0:T(8,128)(2,1)S(1)} %copy-done.38), channel_id=1, source_target_pairs={{1,0},{2,1},{3,2},{4,3},{5,4},{6,5},{7,6},{9,8},{10,9},{11,10},{12... | collective-permute-start | bytes 393224 | tf_op jit(solution)/shard_map/ppermute | solution.py:386
  104.5 2.5 %copy-start.33 = (bf16[2,64,128]{2,1,0:T(8,128)(2,1)S(1)}, bf16[2,64,128]{2,1,0:T(8,128)(2,1)}, u32[]{:S(2)}) copy-start(bf16[2,64,128]{2,1,0:T(8,128)(2,1)} %copy-done.32) | copy-start | bytes 98308
  107.0 2.0 %copy-start.31 = (bf16[2,64,128]{2,1,0:T(8,128)(2,1)S(1)}, bf16[2,64,128]{2,1,0:T(8,128)(2,1)}, u32[]{:S(2)}) copy-start(bf16[2,64,128]{2,1,0:T(8,128)(2,1)} %copy-done.30) | copy-start | bytes 98308
  107.7 11.3 %collective-permute-start.7 = (bf16[6,64,128]{2,1,0:T(8,128)(2,1)}, bf16[6,64,128]{2,1,0:T(8,128)(2,1)}, u32[]{:S(2)}, u32[]{:S(2)}) collective-permute-start(bf16[6,64,128]{2,1,0:T(8,128)(2,1)} %pad_maximum_fusion.3), channel_id=1, source_target_pairs={{8,0},{9,1},{10,2},{11,3},{12,4},{13,5},{14,6},{15,7},{16,8},{17,9... | collective-permute-start | bytes 294920 | tf_op jit(solution)/shard_map/ppermute | solution.py:386
  109.6 9.3 %collective-permute-start.6 = (bf16[6,64,128]{2,1,0:T(8,128)(2,1)}, bf16[6,64,128]{2,1,0:T(8,128)(2,1)}, u32[]{:S(2)}, u32[]{:S(2)}) collective-permute-start(bf16[6,64,128]{2,1,0:T(8,128)(2,1)} %pad_maximum_fusion.2), channel_id=1, source_target_pairs={{0,8},{1,9},{2,10},{3,11},{4,12},{5,13},{6,14},{7,15},{8,16},{9,17... | collective-permute-start | bytes 294920 | tf_op jit(solution)/shard_map/ppermute | solution.py:386
  114.2 4.7 %copy-start = (bf16[512,1024]{1,0:T(8,128)(2,1)S(1)}, bf16[512,1024]{1,0:T(8,128)(2,1)}, u32[]{:S(2)}) copy-start(bf16[512,1024]{1,0:T(8,128)(2,1)} %constant.18.clone.e_yz) | copy-start | bytes 3145732
  117.7 1.2 copy-start.5
  117.7 1.3 copy-start.29
  119.6 1.0 copy-start.9
  122.3 0.9 copy-start.21
  (22 other events, 16.3 us)

commit v2 on v1

v2 whole, which is shorter than its diff:
```python
import jax
import jax.numpy as jnp
from jax import lax
from jax.experimental import pallas as pl
from jax.experimental.pallas import tpu as pltpu
from jax.sharding import PartitionSpec as P

AXES = ("region", "brick")
GRID_X = 8
ZERO_ROW = 44
ARRIVALS = {
    (-1, 0): (24, 4),
    (1, 0): (28, 4),
    (0, -1): (32, 2),
    (-1, -1): (34, 2),
    (1, -1): (36, 2),
    (0, 1): (38, 2),
    (-1, 1): (40, 2),
    (1, 1): (42, 2),
}
BF = jnp.bfloat16
F32 = jnp.float32


def direction_list():
    return [
        (a, b, c)
        for a in (-1, 0, 1)
        for b in (-1, 0, 1)
        for c in (-1, 0, 1)
        if (a, b, c) != (0, 0, 0)
    ]


DIRECTIONS = direction_list()


def face_of(vector):
    if vector[0] != 0:
        return 0 if vector[0] < 0 else 1
    if vector[1] != 0:
        return 2 if vector[1] < 0 else 3
    return 4 if vector[2] < 0 else 5


SEND_FACE = [face_of(d) for d in DIRECTIONS]
READ_FACE = [face_of(tuple(-t for t in d)) for d in DIRECTIONS]


YZ_GROUPS = [((0, 1, c), (0, -1, c)) for c in (-1, 0, 1)] + [((0, 0, 1), (0, 0, -1))]
X_GROUPS = [((1, b, c), (-1, b, c)) for b in (-1, 0, 1) for c in (-1, 0, 1)]


def one_hot(rows, source):
    at = lax.broadcasted_iota(jnp.int32, (rows, source.shape[1]), 0)
    return jnp.where(at == source, 1.0, 0.0).astype(BF)


def lanes(count):
    return lax.broadcasted_iota(jnp.int32, (1, count), 1)


def face_matrix():
    lane = lanes(768)
    face, u, v = lane >> 7, (lane >> 3) & 7, lane & 7
    first = jnp.where(face < 2, u * 8 + v, jnp.where(face < 4, u * 64 + v, u * 64 + v * 8))
    far = jnp.where(face == 1, 448, jnp.where(face == 3, 56, jnp.where(face == 5, 7, 0)))
    return one_hot(512, first + far)


def padded_lane(count):
    lane = lanes(count)
    cell = lane & 127
    y = (cell * 205) >> 11
    return lane >> 7, y, cell - y * 10


def spread_matrix(shift):
    plane, y, z = padded_lane(256)
    y, z = y - shift, z - shift
    inside = (y >= 0) & (y < 8) & (z >= 0) & (z < 8)
    return one_hot(128, jnp.where(inside, plane * 64 + y * 8 + z, -1))


def yz_matrix():
    x, y, z = padded_lane(1024)
    group = jnp.where(z == 0, 0, jnp.where(z == 9, 2, 1))
    y_edge, z_edge = (y == 0) | (y == 9), (z == 0) | (z == 9)
    z_cell = jnp.where(z == 0, 7, jnp.where(z == 9, 0, z - 1))
    from_y = group * 128 + jnp.where(y == 0, 64, 0) + x * 8 + z_cell
    from_z = 384 + jnp.where(z == 0, 64, 0) + x * 8 + y - 1
    source = jnp.where(y_edge, from_y, jnp.where(z_edge & (y < 9), from_z, -1))
    return one_hot(512, source)


def x_matrix():
    side, y, z = padded_lane(256)
    y_group = jnp.where(y == 0, 0, jnp.where(y == 9, 2, 1))
    z_group = jnp.where(z == 0, 0, jnp.where(z == 9, 2, 1))
    y_cell = jnp.where(y == 0, 7, jnp.where(y == 9, 0, y - 1))
    z_cell = jnp.where(z == 0, 7, jnp.where(z == 9, 0, z - 1))
    source = (y_group * 3 + z_group) * 128 + jnp.where(side == 0, 64, 0) + y_cell * 8 + z_cell
    return one_hot(1152, jnp.where(y < 10, source, -1))


def dot(a, b):
    return lax.dot_general(a, b, (((1,), (0,)), ((), ())), preferred_element_type=F32)


def dot_nt(a, b):
    return lax.dot_general(a, b, (((1,), (1,)), ((), ())), preferred_element_type=F32)


def low_half(shape):
    return lax.broadcasted_iota(jnp.int32, shape, len(shape) - 1) < 64


def place(n):
    mine = lax.axis_index("brick")
    owner = (n >> 2) - lax.axis_index("region") * 32
    dx = (owner & 7) - (mine & 7) + 1
    dy = (owner >> 3) - (mine >> 3) + 1
    return jnp.where(n >= 0, jnp.clip(dy * 3 + dx, 0, 8), 9)


def choose_sends(neighbours, send_ref):
    readers = []
    for b in range(4):
        for f in range(6):
            bits = 0
            for e in range(26):
                if SEND_FACE[e] == f:
                    bits = bits | jnp.left_shift(1, place(neighbours[b, e]))
            readers.append(bits)
    for x, y in ARRIVALS:
        s = (y + 1) * 3 + x + 1
        for t in range(8):
            send_ref[s * 8 + t] = 0
        sent = 0
        for f in range(24):
            send_ref[s * 8 + jnp.minimum(sent, 7)] = f
            sent = sent + ((readers[f] >> s) & 1)


def tables_kernel(neighbours_any, after_any, index_ref, neighbours, held, where_ref, rank_ref, sem):
    copy = pltpu.make_async_copy(neighbours_any, neighbours, sem)
    copy.start()
    copy.wait()
    for s in range(10):
        held[s] = 0

    def mark(b, carry):
        for e in range(26):
            n = neighbours[b, e]
            where = place(n)
            where_ref[b * 26 + e] = where
            held[where] = held[where] | jnp.left_shift(1, (n & 3) * 6 + READ_FACE[e])
        return carry

    lax.fori_loop(0, 4, mark, 0)
    for f in range(24):
        rank_ref[4 * 24 + f] = f
        rank_ref[9 * 24 + f] = ZERO_ROW
    for (x, y), (base, count) in ARRIVALS.items():
        s = (y + 1) * 3 + x + 1
        bits = held[s]
        got = 0
        for f in range(24):
            rank_ref[s * 24 + f] = base + jnp.minimum(got, count - 1)
            got = got + ((bits >> f) & 1)

    def index(b, carry):
        for e in range(26):
            row = where_ref[b * 26 + e] * 24 + (neighbours[b, e] & 3) * 6 + READ_FACE[e]
            index_ref[b * 26 + e] = rank_ref[row]
        return carry

    lax.fori_loop(0, 4, index, 0)


def send_slots(send_ref, x, y):
    s = (y + 1) * 3 + x + 1
    return [send_ref[s * 8 + t] for t in range(4 if y == 0 else 2)]


def pack(send_ref, tiles_of, right_ref, left_ref, up_ref, down_ref):
    for ref, x in ((right_ref, 1), (left_ref, -1)):
        ids = send_slots(send_ref, x, 0) + send_slots(send_ref, x, -1) + send_slots(send_ref, x, 1)
        for t, tile in enumerate(tiles_of(ids)):
            ref[t] = tile
    for ref, y in ((up_ref, 1), (down_ref, -1)):
        for t, tile in enumerate(tiles_of(send_slots(send_ref, 0, y))):
            ref[t] = tile


def first_kernel(
    neighbours_any, features_any, cotangent_any, active_any,
    values_ref, faces_ref, right_ref, left_ref, up_ref, down_ref, send_ref, active,
    neighbours, features, cotangent, sems,
):
    pairs = (
        (neighbours_any, neighbours), (features_any, features), (cotangent_any, cotangent),
        (active_any, active),
    )
    copies = [pltpu.make_async_copy(s, d, sems.at[t]) for t, (s, d) in enumerate(pairs)]
    for copy in copies:
        copy.start()
    copies[0].wait()
    choose_sends(neighbours, send_ref)
    for copy in copies[1:]:
        copy.wait()
    for b in range(4):
        mask = active[b : b + 1, :].astype(F32)
        f = features[b].astype(F32)
        values_ref[b * 64 : b * 64 + 64, :] = (mask * (f / (1.0 + jnp.exp(-f)))).astype(BF)
        values_ref[256 + b * 64 : 320 + b * 64, :] = (mask * cotangent[b].astype(F32)).astype(BF)
    faces = dot(values_ref[...], face_matrix()).astype(BF)
    for a in range(2):
        for b in range(4):
            for f in range(6):
                row = (a * 4 + b) * 64
                faces_ref[a, b * 6 + f] = faces[row : row + 64, f * 128 : f * 128 + 128]
    low = low_half((64, 128))
    pack(
        send_ref,
        lambda ids: [jnp.where(low, faces_ref[0, i], faces_ref[1, i]) for i in ids],
        right_ref, left_ref, up_ref, down_ref,
    )


def as_column(row):
    here = lax.broadcasted_iota(jnp.int32, (64, 64), 0)
    there = lax.broadcasted_iota(jnp.int32, (64, 64), 1)
    picked = jnp.where(here == there, jnp.broadcast_to(row, (64, 64)), 0.0)
    return jnp.broadcast_to(jnp.sum(picked, axis=1, keepdims=True), (64, 128))


def prepare_kernel(
    first, second, scale, shift,
    w_first, w_back, gain_ref, shift_ref, e_int, e_out, e_yz, e_x,
):
    e_int[...], e_out[...] = spread_matrix(1), spread_matrix(0)
    e_yz[...], e_x[...] = yz_matrix(), x_matrix()
    gain_ref[...] = 1.0 + as_column(scale[...])
    shift_ref[...] = as_column(shift[...])
    for i in range(3):
        for jl in range(9):
            k = 9 * i + jl
            rows, lanes = slice(i * 64, i * 64 + 64), slice(jl * 64, jl * 64 + 64)
            w_first[rows, lanes] = first[k]
            w_back[rows, lanes] = second[26 - k].T


def fill_table(table, faces, arrays, groups):
    low = low_half((64, 128))
    for a in range(arrays):
        for f in range(24):
            table[a, f] = faces[a, f] if arrays == 2 else faces[f]
        table[a, ZERO_ROW] = jnp.zeros((64, 128), BF)
    for ref, base, count in groups:
        for t in range(count * arrays // 2):
            tile = ref[t]
            swapped = jnp.concatenate([tile[:, 64:], tile[:, :64]], axis=1)
            first, second = jnp.where(low, tile, swapped), jnp.where(low, swapped, tile)
            if arrays == 2:
                table[0, base + t], table[1, base + t] = first, second
            else:
                table[0, base + 2 * t], table[0, base + 2 * t + 1] = first, second


def build_padded(index_ref, table, values, ext, side_yz, side_x, e_int, e_yz, e_x, arrays):
    low = low_half((64, 128))
    for a in range(arrays):
        for b in range(4):
            row = (a * 4 + b) * 64
            for side, pairs in ((side_yz, YZ_GROUPS), (side_x, X_GROUPS)):
                for g, (first, second) in enumerate(pairs):
                    lo = index_ref[b * 26 + DIRECTIONS.index(first)]
                    hi = index_ref[b * 26 + DIRECTIONS.index(second)]
                    side[row : row + 64, g * 128 : g * 128 + 128] = jnp.where(
                        low, table[a, lo], table[a, hi]
                    )
    outer = dot(side_x[...], e_x[...]).astype(BF)
    ext[:, 0:128] = outer[:, 0:128]
    ext[:, 1152:1280] = outer[:, 128:256]
    for m in range(4):
        inner = dot(values[:, m * 128 : m * 128 + 128], e_int[...])
        inner = inner + dot(side_yz[...], e_yz[:, m * 256 : m * 256 + 256])
        ext[:, 128 + m * 256 : 384 + m * 256] = inner.astype(BF)


def columns(ext, row, col):
    for p in range(10):
        plane = ext[row : row + 64, p * 128 : p * 128 + 128]
        for j in range(3):
            for l in range(3):
                s = 10 * j + l
                k = 3 * j + l
                moved = plane if s == 0 else pltpu.roll(plane, 128 - s, 1)
                col[k * 64 : k * 64 + 64, p * 128 : p * 128 + 128] = moved


def three_planes(product):
    return (
        product[0:64, 0:1024] + product[64:128, 128:1152] + product[128:192, 256:1280]
    )


def second_kernel(
    index_ref, values, faces, from_left, from_right, from_up, from_down, active,
    w_first, w_back, gain_ref, shift_ref, e_int, e_out, e_yz, e_x,
    hidden_ref, sums_ref, mask_ref,
    table, ext, side_yz, side_x, col_a, col_s, stack_h, stack_s, total_h, total_s,
):
    groups = ((from_left, 24, 4), (from_right, 28, 4), (from_up, 32, 6), (from_down, 38, 6))
    fill_table(table, faces, 2, groups)
    build_padded(index_ref, table, values, ext, side_yz, side_x, e_int, e_yz, e_x, 2)
    stack_h[...] = jnp.zeros_like(stack_h)
    stack_s[...] = jnp.zeros_like(stack_s)
    on = active[...].astype(F32).astype(BF)
    for m in range(4):
        mask_ref[:, m * 256 : m * 256 + 256] = dot(on[:, m * 128 : m * 128 + 128], e_out[...])
    gain = gain_ref[:, 0:1]
    shift = shift_ref[:, 0:1]
    for b in range(4):
        columns(ext, b * 64, col_a)
        columns(ext, 256 + b * 64, col_s)
        pre = three_planes(dot(w_first[...], col_a[...]))
        back = three_planes(dot(w_back[...], col_s[...]))
        mask = mask_ref[b : b + 1, :]
        shaped = pre * gain + shift
        gate = 1.0 / (1.0 + jnp.exp(-shaped))
        hidden = (mask * (shaped * gate)).astype(BF)
        slope = (back * mask * gate * (1.0 + shaped * (1.0 - gate)) * gain).astype(BF)
        for i in range(3):
            stack_h[i * 64 : i * 64 + 64, i * 128 : i * 128 + 1024] = hidden
            stack_s[i * 64 : i * 64 + 64, i * 128 : i * 128 + 1024] = slope
        for m in range(4):
            hidden_ref[b * 64 : b * 64 + 64, m * 128 : m * 128 + 128] = dot_nt(
                hidden[:, m * 256 : m * 256 + 256], e_out[...]
            ).astype(BF)
        part_h = dot_nt(col_s[...], stack_h[...])
        part_s = dot_nt(col_a[...], stack_s[...])
        total_h[...] = part_h if b == 0 else total_h[...] + part_h
        total_s[...] = part_s if b == 0 else total_s[...] + part_s
    pack_sums(total_h, total_s, sums_ref)


def faces_kernel(
    send_ref, hidden,
    hidden_faces, right_ref, left_ref, up_ref, down_ref,
):
    out = dot(hidden[...], face_matrix()).astype(BF)
    for b in range(4):
        for f in range(6):
            hidden_faces[b * 6 + f] = out[b * 64 : b * 64 + 64, f * 128 : f * 128 + 128]
    low = low_half((64, 128))
    pack(
        send_ref,
        lambda ids: [
            jnp.where(low, hidden_faces[i], hidden_faces[j]) for i, j in zip(ids[::2], ids[1::2])
        ],
        right_ref, left_ref, up_ref, down_ref,
    )


def pack_sums(total_h, total_s, sums_ref):
    for t, total in enumerate((total_h, total_s)):
        base = t * 864
        sums_ref[base : base + 576, :] = total[:, 0:128].astype(BF)
        sums_ref[base + 576 : base + 864, :] = jnp.concatenate(
            [total[0:288, 128:192], total[288:576, 128:192]], axis=1
        ).astype(BF)
    sums_ref[1728:2048, :] = jnp.zeros((320, 128), BF)


def third_kernel(
    index_ref, hidden_faces, from_left, from_right, from_up, from_down, mask_ref,
    hidden, features, weight,
    out_ref,
    table, ext, side_yz, side_x, col, w_second, e_int, e_out, e_yz, e_x,
):
    e_int[...], e_out[...] = spread_matrix(1), spread_matrix(0)
    e_yz[...], e_x[...] = yz_matrix(), x_matrix()
    for i in range(3):
        for jl in range(9):
            w_second[i * 64 : i * 64 + 64, jl * 64 : jl * 64 + 64] = weight[9 * i + jl]
    groups = ((from_left, 24, 4), (from_right, 28, 4), (from_up, 32, 6), (from_down, 38, 6))
    fill_table(table, hidden_faces, 1, groups)
    build_padded(index_ref, table, hidden, ext, side_yz, side_x, e_int, e_yz, e_x, 1)
    for b in range(4):
        columns(ext, b * 64, col)
        second = mask_ref[b : b + 1, :] * three_planes(dot(w_second[...], col[...]))
        for m in range(4):
            own = dot(features[b, :, m * 128 : m * 128 + 128], e_out[...])
            own = (own + second[:, m * 256 : m * 256 + 256]).astype(BF)
            out_ref[b, :, m * 128 : m * 128 + 128] = dot_nt(own, e_out[...]).astype(BF)


def share_kernel(parts, left_any, right_any, out_ref):
    total = parts[0].astype(F32)
    for d in range(1, 128):
        total = total + parts[d].astype(F32)
    total = total.astype(BF)
    for d in range(128):
        out_ref[d] = total


def unpack_kernel(sums, first_ref, second_ref):
    for t in range(2):
        base = t * 864
        for i in range(3):
            for jl in range(9):
                if i < 2:
                    block = sums[base + jl * 64 : base + jl * 64 + 64, i * 64 : i * 64 + 64]
                else:
                    pieces = []
                    for r in (jl * 64, jl * 64 + 32):
                        lane, at = (0, r) if r < 288 else (64, r - 288)
                        at += base + 576
                        pieces.append(sums[at : at + 32, lane : lane + 64])
                    block = jnp.concatenate(pieces, axis=0)
                block = block.astype(F32)
                k = 9 * i + jl
                if t == 0:
                    second_ref[26 - k] = block
                else:
                    first_ref[k] = block.T


def sent(array, step):
    pairs = []
    for i in range(32):
        j = i + step
        if 0 <= j < 32 and (abs(step) == GRID_X or i // GRID_X == j // GRID_X):
            pairs.append((i, j))
    return lax.ppermute(array, "brick", pairs)


def forward_kernel(from_left, from_right, up, down, after_any, up_ref, down_ref):
    n = up.shape[0]
    up_ref[0:n] = up[...]
    down_ref[0:n] = down[...]
    for t, ref in enumerate((from_left, from_right)):
        up_ref[n + t * n : 2 * n + t * n] = ref[3 * n :]
        down_ref[n + t * n : 2 * n + t * n] = ref[2 * n : 3 * n]


def first_round(right, left):
    return sent(right, 1), sent(left, -1)


def second_round(from_left, from_right, up, down, after):
    upward, downward = call(
        forward_kernel,
        [(VMEM, t) for t in (from_left, from_right, up, down)] + [(ANY, after)],
        [(VMEM, shape((3 * up.shape[0], 64, 128)))] * 2,
        [],
        8,
        0,
    )
    return from_left, from_right, sent(upward, GRID_X), sent(downward, -GRID_X)


def shape(dims, dtype=BF):
    return jax.ShapeDtypeStruct(dims, dtype)


SMEM = pl.BlockSpec(memory_space=pltpu.SMEM)
VMEM = pl.BlockSpec(memory_space=pltpu.VMEM)
ANY = pl.BlockSpec(memory_space=pl.ANY)
HBM = pl.BlockSpec(memory_space=pltpu.HBM)


def call(kernel, operands, outs, scratch, limit, us):
    return pl.pallas_call(
        kernel,
        out_shape=tuple(o for _, o in outs),
        in_specs=[s for s, _ in operands],
        out_specs=tuple(s for s, _ in outs),
        scratch_shapes=scratch,
        compiler_params=pltpu.CompilerParams(vmem_limit_bytes=limit << 20),
        cost_estimate=pl.CostEstimate(flops=us * 10**9, bytes_accessed=0, transcendentals=0),
        name=kernel.__name__,
    )(*(o for _, o in operands))


def shards(
    features, active, neighbours, first_weight, second_weight, film_scale, film_shift, cotangent
):
    def messages(arrays):
        return [(VMEM, shape((n * arrays, 64, 128))) for n in (4, 4, 1, 1)]


    values, faces, *outgoing, send_ids, on = call(
        first_kernel,
        [(HBM, t) for t in (neighbours, features, cotangent, active)],
        [(VMEM, shape((512, 512))), (VMEM, shape((2, 24, 64, 128)))]
        + messages(2)
        + [(SMEM, shape((80,), jnp.int32)), (VMEM, shape((4, 512), jnp.int32))],
        [
            pltpu.SMEM((4, 26), jnp.int32),
            pltpu.VMEM((4, 64, 512), BF),
            pltpu.VMEM((4, 64, 512), BF),
            pltpu.SemaphoreType.DMA((4,)),
        ],
        58,
        4,
    )
    arrived = second_round(*first_round(*outgoing[:2]), *outgoing[2:], neighbours)
    (index,) = call(
        tables_kernel,
        [(HBM, neighbours), (ANY, arrived[0])],
        [(SMEM, shape((104,), jnp.int32))],
        [
            pltpu.SMEM((4, 26), jnp.int32),
            pltpu.SMEM((10,), jnp.int32),
            pltpu.SMEM((104,), jnp.int32),
            pltpu.SMEM((240,), jnp.int32),
            pltpu.SemaphoreType.DMA,
        ],
        8,
        3,
    )
    spread_shapes = [(128, 256), (128, 256), (512, 1024), (1152, 256)]
    prepared = call(
        prepare_kernel,
        [
            (VMEM, t)
            for t in (
                first_weight,
                second_weight,
                film_scale.reshape(1, 64),
                film_shift.reshape(1, 64),
            )
        ],
        [(VMEM, shape((192, 576)))] * 2
        + [(VMEM, shape((64, 128), F32))] * 2
        + [(VMEM, shape(dims)) for dims in spread_shapes],
        [],
        16,
        3,
    )
    w_first, w_back, gain, shift, *spreads = prepared

    hidden, sums, mask = call(
        second_kernel,
        [(SMEM, index)]
        + [(VMEM, t) for t in (values, faces, *arrived, on, w_first, w_back, gain, shift)]
        + [(VMEM, t) for t in spreads],
        [
            (VMEM, shape((256, 512))),
            (VMEM, shape((2048, 128))),
            (VMEM, shape((4, 1024), F32)),
        ],
        [
            pltpu.VMEM((2, 45, 64, 128), BF),
            pltpu.VMEM((512, 1280), BF),
            pltpu.VMEM((512, 512), BF),
            pltpu.VMEM((512, 1152), BF),
            pltpu.VMEM((576, 1280), BF),
            pltpu.VMEM((576, 1280), BF),
            pltpu.VMEM((192, 1280), BF),
            pltpu.VMEM((192, 1280), BF),
            pltpu.VMEM((576, 192), F32),
            pltpu.VMEM((576, 192), F32),
        ],
        24,
        10,
    )
    parts = lax.all_to_all(sums.reshape(128, 16, 128), AXES, 0, 0, tiled=True)
    hidden_faces, *outgoing = call(
        faces_kernel,
        [(SMEM, send_ids), (VMEM, hidden)],
        [(VMEM, shape((24, 64, 128)))] + messages(1),
        [],
        16,
        8,
    )
    sides = first_round(*outgoing[:2])
    (shares,) = call(
        share_kernel, [(VMEM, parts)] + [(ANY, t) for t in sides], [(VMEM, shape((128, 16, 128)))], [], 16, 1
    )
    arrived = second_round(*sides, *outgoing[2:], shares)
    sums = lax.all_to_all(shares, AXES, 0, 0, tiled=True)
    (block_output,) = call(
        third_kernel,
        [(SMEM, index)]
        + [(VMEM, t) for t in (hidden_faces, *arrived, mask, hidden, features, second_weight)],
        [(VMEM, shape((4, 64, 512)))],
        [
            pltpu.VMEM((1, 45, 64, 128), BF),
            pltpu.VMEM((256, 1280), BF),
            pltpu.VMEM((256, 512), BF),
            pltpu.VMEM((256, 1152), BF),
            pltpu.VMEM((576, 1280), BF),
            pltpu.VMEM((192, 576), BF),
        ]
        + [pltpu.VMEM(dims, BF) for dims in spread_shapes],
        16,
        2,
    )
    grad_first, grad_second = call(
        unpack_kernel,
        [(VMEM, sums.reshape(2048, 128))],
        [(VMEM, shape((27, 64, 64), F32))] * 2,
        [],
        16,
        0,
    )
    return block_output, grad_first, grad_second


def solution(mesh):
    split = P(AXES, None, None)
    rows = P(AXES, None)
    return jax.shard_map(
        shards,
        mesh=mesh,
        in_specs=(split, rows, rows, P(), P(), P(), P(), split),
        out_specs=(split, P(), P()),
        check_vma=False,
    )
```

time: 131 us -> 83.2 us (0.64)
  local copies, waits for them, and re-layouts: 34.7 us -> 2 us
  blocking collectives: 28.5 us -> 0 us
  starting transfers between devices: 28.5 us -> 38.8 us
  Pallas kernels: 22 us -> 27.1 us
  other arithmetic: 2.1 us -> 0 us
    all_to_all x1 -> x0, blocking collectives: 28.5 us -> none  [shards(): parts = lax.all_to_all(sums.reshape(128, 16, 128), AXES, 0, 0, tiled=True)]
    unnamed x90 -> x24, local copies, waits for them, and re-layouts: 24 us -> 2 us
    all_to_all x1 -> x2, starting transfers between devices: 4.8 us -> 17.1 us  [the longest x1 10.8 us: shards(): parts = lax.all_to_all(sums.reshape(128, 16, 128), AXES, 0, 0, tiled=True)]
    reshape x11 -> x0, local copies, waits for them, and re-layouts: 9.53 us -> none  [the longest x9 8.74 us: stacked(): return weight.reshape(3, 9, 64, 64).transpose(0, 2, 1, 3).reshape(192, 576)]
    pallas_call x4 -> x10, Pallas kernels: 22 us -> 27.1 us  [call(): pl.pallas_call(kernel, out_shape=tuple((o for _, o in outs)), in_specs=[s...]
    all_to_all x1 -> x2, waiting for transfers between devices: 0.01 us -> 2.45 us  [the longest x1 2.45 us: shards(): parts = lax.all_to_all(sums.reshape(128, 16, 128), AXES, 0, 0, tiled=True)]
    ppermute x8, starting transfers between devices: 23.7 us -> 21.6 us  [sent(): return lax.ppermute(array, 'brick', pairs)]
    concatenate x4 -> x0, other arithmetic: 1.96 us -> none  [the longest x2 1.29 us: exchange(): jnp.concatenate([up, from_left[6:8], from_right[6:8]], axis=0)]
  transfers between devices with their start and end apart: 9 -> 10, of which waited for: 3 -> 7; matrix products, arithmetic and copies ran while one was open for 9% -> 0% of each run, Pallas kernels for 0% -> 12%
where the time goes in v2:
time: 83.2 us; the launch traced here: 82.7 us
  starting transfers between devices  38.8 us (47%)
  Pallas kernels  27.1 us (33%)
  waiting for transfers between devices  13.9 us (17%)
  local copies, waits for them, and re-layouts  2 us (2%)
  between operations  0.87 us (1%)
    pallas_call x10, Pallas kernels, call(): pl.pallas_call(kernel, out_shape=tuple((o for _, o in outs)), in_specs=[s...  27.1 us
    ppermute x8, starting transfers between devices, sent(): return lax.ppermute(array, 'brick', pairs)  21.6 us
    ppermute x8, waiting for transfers between devices, sent(): return lax.ppermute(array, 'brick', pairs)  11.5 us
    all_to_all x1, starting transfers between devices, shards(): parts = lax.all_to_all(sums.reshape(128, 16, 128), AXES, 0, 0, tiled=True)  10.8 us
    all_to_all x1, starting transfers between devices, shards(): sums = lax.all_to_all(shares, AXES, 0, 0, tiled=True)  6.34 us
    all_to_all x1, waiting for transfers between devices, shards(): parts = lax.all_to_all(sums.reshape(128, 16, 128), AXES, 0, 0, tiled=True)  2.45 us
    unnamed x24, local copies, waits for them, and re-layouts  2 us
  transfers between devices with their start and end apart: 10, of which 7 were waited for; matrix products, arithmetic and copies ran while one was open for 0% of the time, Pallas kernels for 12%

profile of v2, /device:TPU:1, one launch (start us, length us, event | category | flops | bytes accessed | tf_op | source)
XLA Modules:
  0.0 82.7 jit_solution(9224851387470222303)
XLA Ops:
  0.7 3.6 %first_kernel.1 = (bf16[512,512]{1,0:T(8,128)(2,1)}, bf16[2,24,64,128]{3,2,1,0:T(8,128)(2,1)}, bf16[8,64,128]{2,1,0:T(8,128)(2,1)}, bf16[8,64,128]{2,1,0:T(8,128...) custom-call(s32[4,26]{1,0:T(4,128)} %after_any.1, ...), custom_call_target="tpu_custom_call" | custom-call | flops 4000000000 | tf_op jit(solution)/shard_map/first_kernel/pallas_call | solution.py:476
  4.2 4.6 %collective-permute-start = (bf16[8,64,128]{2,1,0:T(8,128)(2,1)}, bf16[8,64,128]{2,1,0:T(8,128)(2,1)S(1)}, u32[]{:S(2)}, u32[]{:S(2)}) collective-permute-start(bf16[8,64,128]{2,1,0:T(8,128)(2,1)} %get-tuple-element.33), channel_id=1, source_target_pairs={{0,1},{1,2},{2,3},{3,4},{4,5},{5,6},{6,7},{8,9},{9,10},{10,11},{11... | collective-permute-start | bytes 393224 | tf_op jit(solution)/shard_map/ppermute | solution.py:437
  8.8 1.9 %collective-permute-start.1 = (bf16[8,64,128]{2,1,0:T(8,128)(2,1)}, bf16[8,64,128]{2,1,0:T(8,128)(2,1)S(1)}, u32[]{:S(2)}, u32[]{:S(2)}) collective-permute-start(bf16[8,64,128]{2,1,0:T(8,128)(2,1)} %get-tuple-element.37), channel_id=1, source_target_pairs={{1,0},{2,1},{3,2},{4,3},{5,4},{6,5},{7,6},{9,8},{10,9},{11,10},{12... | collective-permute-start | bytes 393224 | tf_op jit(solution)/shard_map/ppermute | solution.py:437
  10.8 0.6 copy-done.6
  11.4 0.0 copy-done.7
  11.4 1.1 %prepare_kernel.1 = (bf16[192,576]{1,0:T(8,128)(2,1)S(1)}, bf16[192,576]{1,0:T(8,128)(2,1)S(1)}, f32[64,128]{1,0:T(8,128)S(1)}, f32[64,128]{1,0:T(8,128)S(1)}, b...) custom-call(bf16[27,64,64]{2,1,0:T(8,128)(2,1)S(1)} %copy-done.3, ...), custom_call_target="tpu_custom_call" | custom-call | flops 3000000000 | tf_op jit(solution)/shard_map/prepare_kernel/pallas_call | solution.py:476
  12.6 0.0 copy-start.2
  12.6 2.7 %collective-permute-done.1.from_right = bf16[8,64,128]{2,1,0:T(8,128)(2,1)S(1)} collective-permute-done((bf16[8,64,128]{2,1,0:T(8,128)(2,1)}, bf16[8,64,128]{2,1,0:T(8,128)(2,1)S(1)}, u32[]{:S(2)}, u32[]{:S(2)}) %collective-permute-start.1) | collective-permute-done | bytes 131104 | tf_op jit(solution)/shard_map/ppermute | solution.py:437
  15.4 3.1 %collective-permute-start.2 = (bf16[6,64,128]{2,1,0:T(8,128)(2,1)S(1)}, bf16[6,64,128]{2,1,0:T(8,128)(2,1)S(1)}, u32[]{:S(2)}, u32[]{:S(2)}) collective-permute-start(bf16[6,64,128]{2,1,0:T(8,128)(2,1)S(1)} %get-tuple-element.40), channel_id=1, source_target_pairs={{0,8},{1,9},{2,10},{3,11},{4,12},{5,13},{6,14},{7,15},{8,16},{9,17... | collective-permute-start | bytes 294920 | tf_op jit(solution)/shard_map/ppermute | solution.py:437
  18.5 0.0 copy-start.8
  18.5 0.0 copy-start.9
  18.5 1.6 %collective-permute-start.3 = (bf16[6,64,128]{2,1,0:T(8,128)(2,1)S(1)}, bf16[6,64,128]{2,1,0:T(8,128)(2,1)S(1)}, u32[]{:S(2)}, u32[]{:S(2)}) collective-permute-start(bf16[6,64,128]{2,1,0:T(8,128)(2,1)S(1)} %get-tuple-element.41), channel_id=1, source_target_pairs={{8,0},{9,1},{10,2},{11,3},{12,4},{13,5},{14,6},{15,7},{16,8},{17,9... | collective-permute-start | bytes 294920 | tf_op jit(solution)/shard_map/ppermute | solution.py:437
  20.1 2.7 %tables_kernel.1.index_ref = s32[104]{0:T(128)S(1)} custom-call(s32[4,26]{1,0:T(4,128)S(1)} %copy-done.2, bf16[8,64,128]{2,1,0:T(8,128)(2,1)S(1)} %collective-permute-done.after_any.from_left), custom_call_target="tpu_custom_call" | custom-call | flops 3000000000 | tf_op jit(solution)/shard_map/tables_kernel/pallas_call | solution.py:476
  22.8 1.2 %collective-permute-done.3.from_down = bf16[6,64,128]{2,1,0:T(8,128)(2,1)S(1)} collective-permute-done((bf16[6,64,128]{2,1,0:T(8,128)(2,1)S(1)}, bf16[6,64,128]{2,1,0:T(8,128)(2,1)S(1)}, u32[]{:S(2)}, u32[]{:S(2)}) %collective-permute-start.3) | collective-permute-done | bytes 98336 | tf_op jit(solution)/shard_map/ppermute | solution.py:437
  24.0 0.7 copy-done.10
  24.7 10.7 %second_kernel.1 = (bf16[256,512]{1,0:T(8,128)(2,1)S(1)}, bf16[2048,128]{1,0:T(8,128)(2,1)}, f32[4,1024]{1,0:T(4,128)S(1)}) custom-call(s32[104]{0:T(128)S(1)} %tables_kernel.1.index_ref, bf16[512,512]{1,0:T(8,128)(2,1)S(1)} %copy-done.9, bf16[2,24,64,128]{3,2,1,0:T(8,128)(2,1)S(1)} %copy-done.8, ...), custom_call_target="tpu_custom_call" | custom-call | flops 10000000000 | tf_op jit(solution)/shard_map/second_kernel/pallas_call | solution.py:476
  35.5 10.8 %all-to-all-start = ((bf16[128,16,128]{2,1,0:T(8,128)(2,1)}), bf16[128,16,128]{2,1,0:T(8,128)(2,1)S(1)}, u32[]{:S(2)}, u32[]{:S(2)}) async-start(bf16[128,16,128]{2,1,0:T(8,128)(2,1)} %bitcast.2), calls=%async_computation | async-start | bytes 1048576 | tf_op jit(solution)/shard_map/all_to_all | solution.py:571
  46.3 0.6 copy-done.11
  46.9 1.0 %faces_kernel.1 = (bf16[24,64,128]{2,1,0:T(8,128)(2,1)S(1)}, bf16[4,64,128]{2,1,0:T(8,128)(2,1)S(1)}, bf16[4,64,128]{2,1,0:T(8,128)(2,1)S(1)}, bf16[1,64,128]{2,1,0:T(8,128)(2,1)S(1)}, bf16[1,64,128]{2,1,0:T(8,128)(2,1)S(1)}) custom-call(s32[80]{0:T(128)S(1)} %copy-done.11, bf16[256,512]{1,0:T(8,128)(2,1)S(1)} %get-tuple-element.51.hidden), custom_call_target="tpu_custom_call" | custom-call | flops 8000000000 | tf_op jit(solution)/shard_map/faces_kernel/pallas_call | solution.py:476
  47.9 3.5 %collective-permute-start.4 = (bf16[4,64,128]{2,1,0:T(8,128)(2,1)S(1)}, bf16[4,64,128]{2,1,0:T(8,128)(2,1)S(1)}, u32[]{:S(2)}, u32[]{:S(2)}) collective-permute-start(bf16[4,64,128]{2,1,0:T(8,128)(2,1)S(1)} %get-tuple-element.53), channel_id=1, source_target_pairs={{0,1},{1,2},{2,3},{3,4},{4,5},{5,6},{6,7},{8,9},{9,10},{10,11},{11... | collective-permute-start | bytes 196616 | tf_op jit(solution)/shard_map/ppermute | solution.py:437
  51.4 1.9 %collective-permute-start.5 = (bf16[4,64,128]{2,1,0:T(8,128)(2,1)S(1)}, bf16[4,64,128]{2,1,0:T(8,128)(2,1)S(1)}, u32[]{:S(2)}, u32[]{:S(2)}) collective-permute-start(bf16[4,64,128]{2,1,0:T(8,128)(2,1)S(1)} %get-tuple-element.54), channel_id=1, source_target_pairs={{1,0},{2,1},{3,2},{4,3},{5,4},{6,5},{7,6},{9,8},{10,9},{11,10},{12... | collective-permute-start | bytes 196616 | tf_op jit(solution)/shard_map/ppermute | solution.py:437
  53.4 0.3 collective-permute-done.4.left_any.from_left
  53.6 3.7 %collective-permute-done.5.right_any.from_right = bf16[4,64,128]{2,1,0:T(8,128)(2,1)S(1)} collective-permute-done((bf16[4,64,128]{2,1,0:T(8,128)(2,1)S(1)}, bf16[4,64,128]{2,1,0:T(8,128)(2,1)S(1)}, u32[]{:S(2)}, u32[]{:S(2)}) %collective-permute-start.5) | collective-permute-done | bytes 65568 | tf_op jit(solution)/shard_map/ppermute | solution.py:437
  57.3 2.5 %all-to-all-done.parts = bf16[128,16,128]{2,1,0:T(8,128)(2,1)S(1)} async-done(((bf16[128,16,128]{2,1,0:T(8,128)(2,1)}), bf16[128,16,128]{2,1,0:T(8,128)(2,1)S(1)}, u32[]{:S(2)}, u32[]{:S(2)}) %all-to-all-start) | async-done | bytes 524320 | tf_op jit(solution)/shard_map/all_to_all | solution.py:571
  59.8 1.0 %share_kernel.1.after_any = bf16[128,16,128]{2,1,0:T(8,128)(2,1)} custom-call(bf16[128,16,128]{2,1,0:T(8,128)(2,1)S(1)} %all-to-all-done.parts, bf16[4,64,128]{2,1,0:T(8,128)(2,1)S(1)} %collective-permute-done.4.left_any.from_left, bf16[4,64,128]{2,1,0:T(8,128)(2,1)S(1)} %collective-permute-done.5.right_any.from_right), custom_call_target="tpu_custom_call" | custom-call | flops 1000000000 | tf_op jit(solution)/shard_map/share_kernel/pallas_call | solution.py:476
  60.7 6.3 %all-to-all-start.1 = ((bf16[128,16,128]{2,1,0:T(8,128)(2,1)}), bf16[128,16,128]{2,1,0:T(8,128)(2,1)S(1)}, u32[]{:S(2)}, u32[]{:S(2)}) async-start(bf16[128,16,128]{2,1,0:T(8,128)(2,1)} %share_kernel.1.after_any), calls=%async_computation.1 | async-start | bytes 1048576 | tf_op jit(solution)/shard_map/all_to_all | solution.py:585
  67.1 3.4 %collective-permute-start.6 = (bf16[3,64,128]{2,1,0:T(8,128)(2,1)S(1)}, bf16[3,64,128]{2,1,0:T(8,128)(2,1)S(1)}, u32[]{:S(2)}, u32[]{:S(2)}) collective-permute-start(bf16[3,64,128]{2,1,0:T(8,128)(2,1)S(1)} %get-tuple-element.58), channel_id=1, source_target_pairs={{0,8},{1,9},{2,10},{3,11},{4,12},{5,13},{6,14},{7,15},{8,16},{9,17... | collective-permute-start | bytes 147464 | tf_op jit(solution)/shard_map/ppermute | solution.py:437
  70.5 1.5 %collective-permute-start.7 = (bf16[3,64,128]{2,1,0:T(8,128)(2,1)S(1)}, bf16[3,64,128]{2,1,0:T(8,128)(2,1)S(1)}, u32[]{:S(2)}, u32[]{:S(2)}) collective-permute-start(bf16[3,64,128]{2,1,0:T(8,128)(2,1)S(1)} %get-tuple-element.59), channel_id=1, source_target_pairs={{8,0},{9,1},{10,2},{11,3},{12,4},{13,5},{14,6},{15,7},{16,8},{17,9... | collective-permute-start | bytes 147464 | tf_op jit(solution)/shard_map/ppermute | solution.py:437
  72.1 0.4 collective-permute-done.6.from_up
  72.4 3.2 %collective-permute-done.7.from_down = bf16[3,64,128]{2,1,0:T(8,128)(2,1)S(1)} collective-permute-done((bf16[3,64,128]{2,1,0:T(8,128)(2,1)S(1)}, bf16[3,64,128]{2,1,0:T(8,128)(2,1)S(1)}, u32[]{:S(2)}, u32[]{:S(2)}) %collective-permute-start.7) | collective-permute-done | bytes 49184 | tf_op jit(solution)/shard_map/ppermute | solution.py:437
  75.7 5.4 %third_kernel.1 = bf16[4,64,512]{2,1,0:T(8,128)(2,1)} custom-call(s32[104]{0:T(128)S(1)} %tables_kernel.1.index_ref, bf16[24,64,128]{2,1,0:T(8,128)(2,1)S(1)} %get-tuple-element.52.hidden_faces, bf16[4,64,128]{2,1,0:T(8,128)(2,1)S(1)} %collective-permute-done.4.left_any.from_left, bf16[4,64,128]{2,1,0:T(8,128)(2,1)S(1)} %collective-permute-done.5.right_any.from_right, ...), custom_call_target="tpu_custom_call" | custom-call | flops 2000000000 | tf_op jit(solution)/shard_map/third_kernel/pallas_call | solution.py:476
  81.1 1.6 %unpack_kernel.1 = (f32[27,64,64]{2,1,0:T(8,128)}, f32[27,64,64]{2,1,0:T(8,128)}) custom-call(bf16[2048,128]{1,0:T(8,128)(2,1)S(1)} %bitcast.4), custom_call_target="tpu_custom_call" | custom-call | tf_op jit(solution)/shard_map/unpack_kernel/pallas_call | solution.py:476
  (22 shorter events, 0.1 us)
Async XLA Ops:
  0.6 10.2 %copy-start.4 = (bf16[27,64,64]{2,1,0:T(8,128)(2,1)S(1)}, bf16[27,64,64]{2,1,0:T(8,128)(2,1)}, u32[]{:S(2)}) copy-start(bf16[27,64,64]{2,1,0:T(8,128)(2,1)} %weight.1) | copy-start | bytes 663556
  0.6 10.2 %copy-start.3 = (bf16[27,64,64]{2,1,0:T(8,128)(2,1)S(1)}, bf16[27,64,64]{2,1,0:T(8,128)(2,1)}, u32[]{:S(2)}) copy-start(bf16[27,64,64]{2,1,0:T(8,128)(2,1)} %first.1) | copy-start | bytes 663556
  4.2 8.4 %collective-permute-start = (bf16[8,64,128]{2,1,0:T(8,128)(2,1)}, bf16[8,64,128]{2,1,0:T(8,128)(2,1)S(1)}, u32[]{:S(2)}, u32[]{:S(2)}) collective-permute-start(bf16[8,64,128]{2,1,0:T(8,128)(2,1)} %get-tuple-element.33), channel_id=1, source_target_pairs={{0,1},{1,2},{2,3},{3,4},{4,5},{5,6},{6,7},{8,9},{9,10},{10,11},{11... | collective-permute-start | bytes 393224 | tf_op jit(solution)/shard_map/ppermute | solution.py:437
  8.8 6.5 %collective-permute-start.1 = (bf16[8,64,128]{2,1,0:T(8,128)(2,1)}, bf16[8,64,128]{2,1,0:T(8,128)(2,1)S(1)}, u32[]{:S(2)}, u32[]{:S(2)}) collective-permute-start(bf16[8,64,128]{2,1,0:T(8,128)(2,1)} %get-tuple-element.37), channel_id=1, source_target_pairs={{1,0},{2,1},{3,2},{4,3},{5,4},{6,5},{7,6},{9,8},{10,9},{11,10},{12... | collective-permute-start | bytes 393224 | tf_op jit(solution)/shard_map/ppermute | solution.py:437
  10.8 0.7 copy-start.6
  10.8 0.7 copy-start.7
  11.4 3.9 %copy-start = (bf16[2,64,128]{2,1,0:T(8,128)(2,1)S(1)}, bf16[2,64,128]{2,1,0:T(8,128)(2,1)}, u32[]{:S(2)}) copy-start(bf16[2,64,128]{2,1,0:T(8,128)(2,1)} %get-tuple-element.38.up) | copy-start | bytes 98308
  11.4 3.9 %copy-start.1 = (bf16[2,64,128]{2,1,0:T(8,128)(2,1)S(1)}, bf16[2,64,128]{2,1,0:T(8,128)(2,1)}, u32[]{:S(2)}) copy-start(bf16[2,64,128]{2,1,0:T(8,128)(2,1)} %get-tuple-element.39.down) | copy-start | bytes 98308
  12.6 2.8 %copy-start.2 = (s32[4,26]{1,0:T(4,128)S(1)}, s32[4,26]{1,0:T(4,128)}, u32[]{:S(2)}) copy-start(s32[4,26]{1,0:T(4,128)} %after_any.1) | copy-start | bytes 1252
  15.4 7.5 %collective-permute-start.2 = (bf16[6,64,128]{2,1,0:T(8,128)(2,1)S(1)}, bf16[6,64,128]{2,1,0:T(8,128)(2,1)S(1)}, u32[]{:S(2)}, u32[]{:S(2)}) collective-permute-start(bf16[6,64,128]{2,1,0:T(8,128)(2,1)S(1)} %get-tuple-element.40), channel_id=1, source_target_pairs={{0,8},{1,9},{2,10},{3,11},{4,12},{5,13},{6,14},{7,15},{8,16},{9,17... | collective-permute-start | bytes 294920 | tf_op jit(solution)/shard_map/ppermute | solution.py:437
  18.5 5.5 %copy-start.8 = (bf16[2,24,64,128]{3,2,1,0:T(8,128)(2,1)S(1)}, bf16[2,24,64,128]{3,2,1,0:T(8,128)(2,1)}, u32[]{:S(2)}) copy-start(bf16[2,24,64,128]{3,2,1,0:T(8,128)(2,1)} %get-tuple-element.36.faces) | copy-start | bytes 2359300
  18.5 5.5 %copy-start.9 = (bf16[512,512]{1,0:T(8,128)(2,1)S(1)}, bf16[512,512]{1,0:T(8,128)(2,1)}, u32[]{:S(2)}) copy-start(bf16[512,512]{1,0:T(8,128)(2,1)} %get-tuple-element.35.values) | copy-start | bytes 1572868
  18.5 5.5 %collective-permute-start.3 = (bf16[6,64,128]{2,1,0:T(8,128)(2,1)S(1)}, bf16[6,64,128]{2,1,0:T(8,128)(2,1)S(1)}, u32[]{:S(2)}, u32[]{:S(2)}) collective-permute-start(bf16[6,64,128]{2,1,0:T(8,128)(2,1)S(1)} %get-tuple-element.41), channel_id=1, source_target_pairs={{8,0},{9,1},{10,2},{11,3},{12,4},{13,5},{14,6},{15,7},{16,8},{17,9... | collective-permute-start | bytes 294920 | tf_op jit(solution)/shard_map/ppermute | solution.py:437
  24.0 0.7 copy-start.10
  35.5 24.3 %all-to-all-start = ((bf16[128,16,128]{2,1,0:T(8,128)(2,1)}), bf16[128,16,128]{2,1,0:T(8,128)(2,1)S(1)}, u32[]{:S(2)}, u32[]{:S(2)}) async-start(bf16[128,16,128]{2,1,0:T(8,128)(2,1)} %bitcast.2), calls=%async_computation | async-start | bytes 1048576 | tf_op jit(solution)/shard_map/all_to_all | solution.py:571
  46.3 0.6 copy-start.11
  47.9 5.8 %collective-permute-start.4 = (bf16[4,64,128]{2,1,0:T(8,128)(2,1)S(1)}, bf16[4,64,128]{2,1,0:T(8,128)(2,1)S(1)}, u32[]{:S(2)}, u32[]{:S(2)}) collective-permute-start(bf16[4,64,128]{2,1,0:T(8,128)(2,1)S(1)} %get-tuple-element.53), channel_id=1, source_target_pairs={{0,1},{1,2},{2,3},{3,4},{4,5},{5,6},{6,7},{8,9},{9,10},{10,11},{11... | collective-permute-start | bytes 196616 | tf_op jit(solution)/shard_map/ppermute | solution.py:437
  51.4 5.9 %collective-permute-start.5 = (bf16[4,64,128]{2,1,0:T(8,128)(2,1)S(1)}, bf16[4,64,128]{2,1,0:T(8,128)(2,1)S(1)}, u32[]{:S(2)}, u32[]{:S(2)}) collective-permute-start(bf16[4,64,128]{2,1,0:T(8,128)(2,1)S(1)} %get-tuple-element.54), channel_id=1, source_target_pairs={{1,0},{2,1},{3,2},{4,3},{5,4},{6,5},{7,6},{9,8},{10,9},{11,10},{12... | collective-permute-start | bytes 196616 | tf_op jit(solution)/shard_map/ppermute | solution.py:437
  60.7 20.4 %all-to-all-start.1 = ((bf16[128,16,128]{2,1,0:T(8,128)(2,1)}), bf16[128,16,128]{2,1,0:T(8,128)(2,1)S(1)}, u32[]{:S(2)}, u32[]{:S(2)}) async-start(bf16[128,16,128]{2,1,0:T(8,128)(2,1)} %share_kernel.1.after_any), calls=%async_computation.1 | async-start | bytes 1048576 | tf_op jit(solution)/shard_map/all_to_all | solution.py:585
  67.1 8.6 %copy-start.5 = (bf16[4,64,512]{2,1,0:T(8,128)(2,1)S(1)}, bf16[4,64,512]{2,1,0:T(8,128)(2,1)}, u32[]{:S(2)}) copy-start(bf16[4,64,512]{2,1,0:T(8,128)(2,1)} %features.1) | copy-start | bytes 786436
  67.1 5.3 %collective-permute-start.6 = (bf16[3,64,128]{2,1,0:T(8,128)(2,1)S(1)}, bf16[3,64,128]{2,1,0:T(8,128)(2,1)S(1)}, u32[]{:S(2)}, u32[]{:S(2)}) collective-permute-start(bf16[3,64,128]{2,1,0:T(8,128)(2,1)S(1)} %get-tuple-element.58), channel_id=1, source_target_pairs={{0,8},{1,9},{2,10},{3,11},{4,12},{5,13},{6,14},{7,15},{8,16},{9,17... | collective-permute-start | bytes 147464 | tf_op jit(solution)/shard_map/ppermute | solution.py:437
  70.5 5.1 %collective-permute-start.7 = (bf16[3,64,128]{2,1,0:T(8,128)(2,1)S(1)}, bf16[3,64,128]{2,1,0:T(8,128)(2,1)S(1)}, u32[]{:S(2)}, u32[]{:S(2)}) collective-permute-start(bf16[3,64,128]{2,1,0:T(8,128)(2,1)S(1)} %get-tuple-element.59), channel_id=1, source_target_pairs={{8,0},{9,1},{10,2},{11,3},{12,4},{13,5},{14,6},{15,7},{16,8},{17,9... | collective-permute-start | bytes 147464 | tf_op jit(solution)/shard_map/ppermute | solution.py:437

commit v3 on v2

--- a/solution.py
+++ b/solution.py
@@ -75,11 +75,18 @@
     return lane >> 7, y, cell - y * 10
 
 
-def spread_matrix(shift):
+def spread_matrix():
     plane, y, z = padded_lane(256)
-    y, z = y - shift, z - shift
+    y, z = y - 1, z - 1
     inside = (y >= 0) & (y < 8) & (z >= 0) & (z < 8)
     return one_hot(128, jnp.where(inside, plane * 64 + y * 8 + z, -1))
+
+
+def window_matrix():
+    lane = lanes(1152)
+    tap, plane, y, z = lane >> 7, (lane >> 6) & 1, (lane >> 3) & 7, lane & 7
+    j = jnp.where(tap < 3, 0, jnp.where(tap < 6, 1, 2))
+    return one_hot(256, plane * 128 + (y + j) * 10 + z + tap - 3 * j)
 
 
 def yz_matrix():
@@ -142,10 +149,13 @@
             sent = sent + ((readers[f] >> s) & 1)
 
 
-def tables_kernel(neighbours_any, after_any, index_ref, neighbours, held, where_ref, rank_ref, sem):
+def tables_kernel(
+    neighbours_any, after_any, index_ref, send_ref, neighbours, held, where_ref, rank_ref, sem
+):
     copy = pltpu.make_async_copy(neighbours_any, neighbours, sem)
     copy.start()
     copy.wait()
+    choose_sends(neighbours, send_ref)
     for s in range(10):
         held[s] = 0
 
@@ -195,8 +205,8 @@
 
 def first_kernel(
     neighbours_any, features_any, cotangent_any, active_any,
-    values_ref, faces_ref, right_ref, left_ref, up_ref, down_ref, send_ref, active,
-    neighbours, features, cotangent, sems,
+    values_ref, faces_ref, right_ref, left_ref, up_ref, down_ref,
+    neighbours, features, cotangent, active, send_ref, sems,
 ):
     pairs = (
         (neighbours_any, neighbours), (features_any, features), (cotangent_any, cotangent),
@@ -205,10 +215,9 @@
     copies = [pltpu.make_async_copy(s, d, sems.at[t]) for t, (s, d) in enumerate(pairs)]
     for copy in copies:
         copy.start()
-    copies[0].wait()
+    for copy in copies:
+        copy.wait()
     choose_sends(neighbours, send_ref)
-    for copy in copies[1:]:
-        copy.wait()
     for b in range(4):
         mask = active[b : b + 1, :].astype(F32)
         f = features[b].astype(F32)
@@ -236,11 +245,12 @@
 
 
 def prepare_kernel(
-    first, second, scale, shift,
-    w_first, w_back, gain_ref, shift_ref, e_int, e_out, e_yz, e_x,
+    active, first, second, scale, shift,
+    mask_ref, w_first, w_back, gain_ref, shift_ref, e_int, e_yz, e_x, windows,
 ):
-    e_int[...], e_out[...] = spread_matrix(1), spread_matrix(0)
-    e_yz[...], e_x[...] = yz_matrix(), x_matrix()
+    mask_ref[...] = active[...].astype(F32)
+    e_int[...], e_yz[...], e_x[...] = spread_matrix(), yz_matrix(), x_matrix()
+    windows[...] = window_matrix()
     gain_ref[...] = 1.0 + as_column(scale[...])
     shift_ref[...] = as_column(shift[...])
     for i in range(3):
@@ -289,60 +299,64 @@
         ext[:, 128 + m * 256 : 384 + m * 256] = inner.astype(BF)
 
 
-def columns(ext, row, col):
-    for p in range(10):
-        plane = ext[row : row + 64, p * 128 : p * 128 + 128]
-        for j in range(3):
-            for l in range(3):
-                s = 10 * j + l
-                k = 3 * j + l
-                moved = plane if s == 0 else pltpu.roll(plane, 128 - s, 1)
-                col[k * 64 : k * 64 + 64, p * 128 : p * 128 + 128] = moved
-
-
-def three_planes(product):
+def columns(ext, windows, cols):
+    for m in range(5):
+        moved = dot(ext[:, m * 256 : m * 256 + 256], windows[...]).astype(BF)
+        for a, col in enumerate(cols):
+            for b in range(4):
+                row = (a * 4 + b) * 64
+                lane = b * 640 + m * 128
+                for k in range(9):
+                    col[k * 64 : k * 64 + 64, lane : lane + 128] = moved[
+                        row : row + 64, k * 128 : k * 128 + 128
+                    ]
+
+
+def three_planes(product, lane):
     return (
-        product[0:64, 0:1024] + product[64:128, 128:1152] + product[128:192, 256:1280]
-    )
+        product[0:64, lane : lane + 512]
+        + product[64:128, lane + 64 : lane + 576]
+        + product[128:192, lane + 128 : lane + 640]
+    )
+
+
+def stack_planes(stack, lane, values):
+    none = jnp.zeros((64, 64), BF)
+    wide = jnp.zeros((64, 128), BF)
+    stack[0:64, lane : lane + 640] = jnp.concatenate([values, wide], axis=1)
+    stack[64:128, lane : lane + 640] = jnp.concatenate([none, values, none], axis=1)
+    stack[128:192, lane : lane + 640] = jnp.concatenate([wide, values], axis=1)
 
 
 def second_kernel(
-    index_ref, values, faces, from_left, from_right, from_up, from_down, active,
-    w_first, w_back, gain_ref, shift_ref, e_int, e_out, e_yz, e_x,
-    hidden_ref, sums_ref, mask_ref,
-    table, ext, side_yz, side_x, col_a, col_s, stack_h, stack_s, total_h, total_s,
+    index_ref, values, faces, from_left, from_right, from_up, from_down, mask_ref,
+    w_first, w_back, gain_ref, shift_ref, e_int, e_yz, e_x, windows,
+    hidden_ref, sums_ref,
+    table, ext, side_yz, side_x, col_a, col_s, stack_h, stack_s,
 ):
     groups = ((from_left, 24, 4), (from_right, 28, 4), (from_up, 32, 6), (from_down, 38, 6))
     fill_table(table, faces, 2, groups)
     build_padded(index_ref, table, values, ext, side_yz, side_x, e_int, e_yz, e_x, 2)
-    stack_h[...] = jnp.zeros_like(stack_h)
-    stack_s[...] = jnp.zeros_like(stack_s)
-    on = active[...].astype(F32).astype(BF)
-    for m in range(4):
-        mask_ref[:, m * 256 : m * 256 + 256] = dot(on[:, m * 128 : m * 128 + 128], e_out[...])
+    columns(ext, windows, (col_a, col_s))
     gain = gain_ref[:, 0:1]
     shift = shift_ref[:, 0:1]
-    for b in range(4):
-        columns(ext, b * 64, col_a)
-        columns(ext, 256 + b * 64, col_s)
-        pre = three_planes(dot(w_first[...], col_a[...]))
-        back = three_planes(dot(w_back[...], col_s[...]))
-        mask = mask_ref[b : b + 1, :]
-        shaped = pre * gain + shift
-        gate = 1.0 / (1.0 + jnp.exp(-shaped))
-        hidden = (mask * (shaped * gate)).astype(BF)
-        slope = (back * mask * gate * (1.0 + shaped * (1.0 - gate)) * gain).astype(BF)
-        for i in range(3):
-            stack_h[i * 64 : i * 64 + 64, i * 128 : i * 128 + 1024] = hidden
-            stack_s[i * 64 : i * 64 + 64, i * 128 : i * 128 + 1024] = slope
-        for m in range(4):
-            hidden_ref[b * 64 : b * 64 + 64, m * 128 : m * 128 + 128] = dot_nt(
-                hidden[:, m * 256 : m * 256 + 256], e_out[...]
-            ).astype(BF)
-        part_h = dot_nt(col_s[...], stack_h[...])
-        part_s = dot_nt(col_a[...], stack_s[...])
-        total_h[...] = part_h if b == 0 else total_h[...] + part_h
-        total_s[...] = part_s if b == 0 else total_s[...] + part_s
+    for pair in range(2):
+        these = slice(pair * 1280, pair * 1280 + 1280)
+        first = dot(w_first[...], col_a[:, these])
+        second = dot(w_back[...], col_s[:, these])
+        for half in range(2):
+            b = 2 * pair + half
+            pre, back = three_planes(first, half * 640), three_planes(second, half * 640)
+            mask = mask_ref[b : b + 1, :]
+            shaped = pre * gain + shift
+            gate = 1.0 / (1.0 + jnp.exp(-shaped))
+            hidden = (mask * (shaped * gate)).astype(BF)
+            slope = (back * mask * gate * (1.0 + shaped * (1.0 - gate)) * gain).astype(BF)
+            hidden_ref[b * 64 : b * 64 + 64, :] = hidden
+            stack_planes(stack_h, b * 640, hidden)
+            stack_planes(stack_s, b * 640, slope)
+    total_h = dot_nt(col_s[...], stack_h[...])
+    total_s = dot_nt(col_a[...], stack_s[...])
     pack_sums(total_h, total_s, sums_ref)
 
 
@@ -375,26 +389,26 @@
 
 
 def third_kernel(
-    index_ref, hidden_faces, from_left, from_right, from_up, from_down, mask_ref,
-    hidden, features, weight,
+    index_ref, hidden_faces, from_left, from_right, from_up, from_down, hidden,
+    active, features, weight,
     out_ref,
-    table, ext, side_yz, side_x, col, w_second, e_int, e_out, e_yz, e_x,
+    table, ext, side_yz, side_x, col, w_second, e_int, e_yz, e_x, windows,
 ):
-    e_int[...], e_out[...] = spread_matrix(1), spread_matrix(0)
-    e_yz[...], e_x[...] = yz_matrix(), x_matrix()
+    e_int[...], e_yz[...], e_x[...] = spread_matrix(), yz_matrix(), x_matrix()
+    windows[...] = window_matrix()
     for i in range(3):
         for jl in range(9):
             w_second[i * 64 : i * 64 + 64, jl * 64 : jl * 64 + 64] = weight[9 * i + jl]
     groups = ((from_left, 24, 4), (from_right, 28, 4), (from_up, 32, 6), (from_down, 38, 6))
     fill_table(table, hidden_faces, 1, groups)
     build_padded(index_ref, table, hidden, ext, side_yz, side_x, e_int, e_yz, e_x, 1)
-    for b in range(4):
-        columns(ext, b * 64, col)
-        second = mask_ref[b : b + 1, :] * three_planes(dot(w_second[...], col[...]))
-        for m in range(4):
-            own = dot(features[b, :, m * 128 : m * 128 + 128], e_out[...])
-            own = (own + second[:, m * 256 : m * 256 + 256]).astype(BF)
-            out_ref[b, :, m * 128 : m * 128 + 128] = dot_nt(own, e_out[...]).astype(BF)
+    columns(ext, windows, (col,))
+    for pair in range(2):
+        product = dot(w_second[...], col[:, pair * 1280 : pair * 1280 + 1280])
+        for half in range(2):
+            b = 2 * pair + half
+            second = active[b : b + 1, :].astype(F32) * three_planes(product, half * 640)
+            out_ref[b] = (features[b].astype(F32) + second).astype(BF)
 
 
 def share_kernel(parts, left_any, right_any, out_ref):
@@ -492,26 +506,27 @@
         return [(VMEM, shape((n * arrays, 64, 128))) for n in (4, 4, 1, 1)]
 
 
-    values, faces, *outgoing, send_ids, on = call(
+    values, faces, *outgoing = call(
         first_kernel,
         [(HBM, t) for t in (neighbours, features, cotangent, active)],
         [(VMEM, shape((512, 512))), (VMEM, shape((2, 24, 64, 128)))]
-        + messages(2)
-        + [(SMEM, shape((80,), jnp.int32)), (VMEM, shape((4, 512), jnp.int32))],
+        + messages(2),
         [
             pltpu.SMEM((4, 26), jnp.int32),
             pltpu.VMEM((4, 64, 512), BF),
             pltpu.VMEM((4, 64, 512), BF),
+            pltpu.VMEM((4, 512), jnp.int32),
+            pltpu.SMEM((80,), jnp.int32),
             pltpu.SemaphoreType.DMA((4,)),
         ],
         58,
         4,
     )
     arrived = second_round(*first_round(*outgoing[:2]), *outgoing[2:], neighbours)
-    (index,) = call(
+    index, send_ids = call(
         tables_kernel,
         [(HBM, neighbours), (ANY, arrived[0])],
-        [(SMEM, shape((104,), jnp.int32))],
+        [(SMEM, shape((104,), jnp.int32)), (SMEM, shape((80,), jnp.int32))],
         [
             pltpu.SMEM((4, 26), jnp.int32),
             pltpu.SMEM((10,), jnp.int32),
@@ -522,50 +537,49 @@
         8,
         3,
     )
-    spread_shapes = [(128, 256), (128, 256), (512, 1024), (1152, 256)]
+    spread_shapes = [(128, 256), (512, 1024), (1152, 256), (256, 1152)]
     prepared = call(
         prepare_kernel,
         [
             (VMEM, t)
             for t in (
+                active,
                 first_weight,
                 second_weight,
                 film_scale.reshape(1, 64),
                 film_shift.reshape(1, 64),
             )
         ],
-        [(VMEM, shape((192, 576)))] * 2
+        [(VMEM, shape((4, 512), F32))]
+        + [(VMEM, shape((192, 576)))] * 2
         + [(VMEM, shape((64, 128), F32))] * 2
         + [(VMEM, shape(dims)) for dims in spread_shapes],
         [],
         16,
         3,
     )
-    w_first, w_back, gain, shift, *spreads = prepared
-
-    hidden, sums, mask = call(
+    mask, w_first, w_back, gain, shift, *spreads = prepared
+
+    hidden, sums = call(
         second_kernel,
         [(SMEM, index)]
-        + [(VMEM, t) for t in (values, faces, *arrived, on, w_first, w_back, gain, shift)]
+        + [(VMEM, t) for t in (values, faces, *arrived, mask, w_first, w_back, gain, shift)]
         + [(VMEM, t) for t in spreads],
         [
             (VMEM, shape((256, 512))),
             (VMEM, shape((2048, 128))),
-            (VMEM, shape((4, 1024), F32)),
         ],
         [
             pltpu.VMEM((2, 45, 64, 128), BF),
             pltpu.VMEM((512, 1280), BF),
             pltpu.VMEM((512, 512), BF),
             pltpu.VMEM((512, 1152), BF),
-            pltpu.VMEM((576, 1280), BF),
-            pltpu.VMEM((576, 1280), BF),
-            pltpu.VMEM((192, 1280), BF),
-            pltpu.VMEM((192, 1280), BF),
-            pltpu.VMEM((576, 192), F32),
-            pltpu.VMEM((576, 192), F32),
+            pltpu.VMEM((576, 2560), BF),
+            pltpu.VMEM((576, 2560), BF),
+            pltpu.VMEM((192, 2560), BF),
+            pltpu.VMEM((192, 2560), BF),
         ],
-        24,
+        32,
         10,
     )
     parts = lax.all_to_all(sums.reshape(128, 16, 128), AXES, 0, 0, tiled=True)
@@ -586,14 +600,14 @@
     (block_output,) = call(
         third_kernel,
         [(SMEM, index)]
-        + [(VMEM, t) for t in (hidden_faces, *arrived, mask, hidden, features, second_weight)],
+        + [(VMEM, t) for t in (hidden_faces, *arrived, hidden, active, features, second_weight)],
         [(VMEM, shape((4, 64, 512)))],
         [
             pltpu.VMEM((1, 45, 64, 128), BF),
             pltpu.VMEM((256, 1280), BF),
             pltpu.VMEM((256, 512), BF),
             pltpu.VMEM((256, 1152), BF),
-            pltpu.VMEM((576, 1280), BF),
+            pltpu.VMEM((576, 2560), BF),
             pltpu.VMEM((192, 576), BF),
         ]
         + [pltpu.VMEM(dims, BF) for dims in spread_shapes],

time: 83.2 us -> 78.4 us (0.942)
  Pallas kernels: 27.1 us -> 23.9 us
  local copies, waits for them, and re-layouts: 2 us -> 0.67 us
  starting transfers between devices: 38.8 us -> 37.9 us
    pallas_call x10, Pallas kernels: 27.1 us -> 23.9 us  [call(): pl.pallas_call(kernel, out_shape=tuple((o for _, o in outs)), in_specs=[s...]
    unnamed x24 -> x22, local copies, waits for them, and re-layouts: 2 us -> 0.67 us
    ppermute x8, waiting for transfers between devices: 11.5 us -> 10.5 us  [sent(): return lax.ppermute(array, 'brick', pairs)]
    all_to_all x1, waiting for transfers between devices: 0.01 us -> 0.92 us  [shards(): sums = lax.all_to_all(shares, AXES, 0, 0, tiled=True)]
  transfers between devices with their start and end apart: 10 -> 10, of which waited for: 7 -> 8; matrix products, arithmetic and copies ran while one was open for 0% -> 0% of each run, Pallas kernels for 12% -> 13%
where the time goes in v3:
time: 78.4 us; the launch traced here: 77.9 us
  starting transfers between devices  37.9 us (48%)
  Pallas kernels  23.9 us (30%)
  waiting for transfers between devices  14.5 us (18%)
  between operations  0.88 us (1%)
    pallas_call x10, Pallas kernels, call(): pl.pallas_call(kernel, out_shape=tuple((o for _, o in outs)), in_specs=[s...  23.9 us
    ppermute x8, starting transfers between devices, sent(): return lax.ppermute(array, 'brick', pairs)  21.4 us
    all_to_all x1, starting transfers between devices, shards(): parts = lax.all_to_all(sums.reshape(128, 16, 128), AXES, 0, 0, tiled=True)  10.8 us
    ppermute x8, waiting for transfers between devices, sent(): return lax.ppermute(array, 'brick', pairs)  10.5 us
    all_to_all x1, starting transfers between devices, shards(): sums = lax.all_to_all(shares, AXES, 0, 0, tiled=True)  5.71 us
    all_to_all x1, waiting for transfers between devices, shards(): parts = lax.all_to_all(sums.reshape(128, 16, 128), AXES, 0, 0, tiled=True)  3.03 us
  transfers between devices with their start and end apart: 10, of which 8 were waited for; matrix products, arithmetic and copies ran while one was open for 0% of the time, Pallas kernels for 13%

profile of v3, /device:TPU:1, one launch (start us, length us, event | category | flops | bytes accessed | tf_op | source)
XLA Modules:
  0.0 77.9 jit_solution(9352191628600373556)
XLA Ops:
  0.7 3.3 %first_kernel.1 = (bf16[512,512]{1,0:T(8,128)(2,1)}, bf16[2,24,64,128]{3,2,1,0:T(8,128)(2,1)}, bf16[8,64,128]{2,1,0:T(8,128)(2,1)}, bf16[8,64,128]{2,1,0:T(8,128...) custom-call(s32[4,26]{1,0:T(4,128)} %after_any.1, bf16[4,64,512]{2,1,0:T(8,128)(2,1)} %features.1, ...), custom_call_target="tpu_custom_call" | custom-call | flops 4000000000 | tf_op jit(solution)/shard_map/first_kernel/pallas_call | solution.py:490
  4.0 4.6 %collective-permute-start = (bf16[8,64,128]{2,1,0:T(8,128)(2,1)}, bf16[8,64,128]{2,1,0:T(8,128)(2,1)S(1)}, u32[]{:S(2)}, u32[]{:S(2)}) collective-permute-start(bf16[8,64,128]{2,1,0:T(8,128)(2,1)} %get-tuple-element.33), channel_id=1, source_target_pairs={{0,1},{1,2},{2,3},{3,4},{4,5},{5,6},{6,7},{8,9},{9,10},{10,11},{11... | collective-permute-start | bytes 393224 | tf_op jit(solution)/shard_map/ppermute | solution.py:451
  8.6 1.9 %collective-permute-start.1 = (bf16[8,64,128]{2,1,0:T(8,128)(2,1)}, bf16[8,64,128]{2,1,0:T(8,128)(2,1)S(1)}, u32[]{:S(2)}, u32[]{:S(2)}) collective-permute-start(bf16[8,64,128]{2,1,0:T(8,128)(2,1)} %get-tuple-element.38), channel_id=1, source_target_pairs={{1,0},{2,1},{3,2},{4,3},{5,4},{6,5},{7,6},{9,8},{10,9},{11,10},{12... | collective-permute-start | bytes 393224 | tf_op jit(solution)/shard_map/ppermute | solution.py:451
  10.5 0.0 copy-start.7
  10.5 0.0 copy-start.8
  10.6 0.6 copy-done.7
  11.2 0.0 copy-done.8
  11.2 1.4 %prepare_kernel.1 = (f32[4,512]{1,0:T(4,128)S(1)}, bf16[192,576]{1,0:T(8,128)(2,1)S(1)}, bf16[192,576]{1,0:T(8,128)(2,1)S(1)}, f32[64,128]{1,0:T(8,128)S(1)}, f3...) custom-call(s32[4,512]{1,0:T(4,128)S(1)} %copy-done.6, ...), custom_call_target="tpu_custom_call" | custom-call | flops 3000000000 | tf_op jit(solution)/shard_map/prepare_kernel/pallas_call | solution.py:490
  12.6 0.0 copy-start.2
  12.6 2.5 %collective-permute-done.1.from_right = bf16[8,64,128]{2,1,0:T(8,128)(2,1)S(1)} collective-permute-done((bf16[8,64,128]{2,1,0:T(8,128)(2,1)}, bf16[8,64,128]{2,1,0:T(8,128)(2,1)S(1)}, u32[]{:S(2)}, u32[]{:S(2)}) %collective-permute-start.1) | collective-permute-done | bytes 131104 | tf_op jit(solution)/shard_map/ppermute | solution.py:451
  15.1 3.1 %collective-permute-start.2 = (bf16[6,64,128]{2,1,0:T(8,128)(2,1)S(1)}, bf16[6,64,128]{2,1,0:T(8,128)(2,1)S(1)}, u32[]{:S(2)}, u32[]{:S(2)}) collective-permute-start(bf16[6,64,128]{2,1,0:T(8,128)(2,1)S(1)} %get-tuple-element.41), channel_id=1, source_target_pairs={{0,8},{1,9},{2,10},{3,11},{4,12},{5,13},{6,14},{7,15},{8,16},{9,17... | collective-permute-start | bytes 294920 | tf_op jit(solution)/shard_map/ppermute | solution.py:451
  18.3 1.4 %collective-permute-start.3 = (bf16[6,64,128]{2,1,0:T(8,128)(2,1)S(1)}, bf16[6,64,128]{2,1,0:T(8,128)(2,1)S(1)}, u32[]{:S(2)}, u32[]{:S(2)}) collective-permute-start(bf16[6,64,128]{2,1,0:T(8,128)(2,1)S(1)} %get-tuple-element.42), channel_id=1, source_target_pairs={{8,0},{9,1},{10,2},{11,3},{12,4},{13,5},{14,6},{15,7},{16,8},{17,9... | collective-permute-start | bytes 294920 | tf_op jit(solution)/shard_map/ppermute | solution.py:451
  19.7 3.7 %tables_kernel.1 = (s32[104]{0:T(128)S(1)}, s32[80]{0:T(128)S(1)}) custom-call(s32[4,26]{1,0:T(4,128)S(1)} %copy-done.2, bf16[8,64,128]{2,1,0:T(8,128)(2,1)S(1)} %collective-permute-done.after_any.from_left), custom_call_target="tpu_custom_call" | custom-call | flops 3000000000 | tf_op jit(solution)/shard_map/tables_kernel/pallas_call | solution.py:490
  23.4 0.4 collective-permute-done.3.from_down
  23.8 8.1 %second_kernel.1 = (bf16[256,512]{1,0:T(8,128)(2,1)S(1)}, bf16[2048,128]{1,0:T(8,128)(2,1)}) custom-call(s32[104]{0:T(128)S(1)} %get-tuple-element.34.index_ref, bf16[512,512]{1,0:T(8,128)(2,1)S(1)} %copy-done.10, bf16[2,24,64,128]{3,2,1,0:T(8,128)(2,1)S(1)} %copy-done.9, bf16[8,64,128]{2,1,0:T(8,128)(2,1)S(1)} %collective-permute-done.after_any.from_left, ...), custom_call_target="tpu_custom_call" | custom-call | flops 10000000000 | tf_op jit(solution)/shard_map/second_kernel/pallas_call | solution.py:490
  31.8 10.8 %all-to-all-start = ((bf16[128,16,128]{2,1,0:T(8,128)(2,1)}), bf16[128,16,128]{2,1,0:T(8,128)(2,1)S(1)}, u32[]{:S(2)}, u32[]{:S(2)}) async-start(bf16[128,16,128]{2,1,0:T(8,128)(2,1)} %bitcast.2), calls=%async_computation | async-start | bytes 1048576 | tf_op jit(solution)/shard_map/all_to_all | solution.py:585
  42.6 1.0 %faces_kernel.1 = (bf16[24,64,128]{2,1,0:T(8,128)(2,1)S(1)}, bf16[4,64,128]{2,1,0:T(8,128)(2,1)S(1)}, bf16[4,64,128]{2,1,0:T(8,128)(2,1)S(1)}, bf16[1,64,128]{2,1,0:T(8,128)(2,1)S(1)}, bf16[1,64,128]{2,1,0:T(8,128)(2,1)S(1)}) custom-call(s32[80]{0:T(128)S(1)} %get-tuple-element.35.send_ref, bf16[256,512]{1,0:T(8,128)(2,1)S(1)} %get-tuple-element.52.hidden), custom_call_target="tpu_custom_call" | custom-call | flops 8000000000 | tf_op jit(solution)/shard_map/faces_kernel/pallas_call | solution.py:490
  43.6 3.5 %collective-permute-start.4 = (bf16[4,64,128]{2,1,0:T(8,128)(2,1)S(1)}, bf16[4,64,128]{2,1,0:T(8,128)(2,1)S(1)}, u32[]{:S(2)}, u32[]{:S(2)}) collective-permute-start(bf16[4,64,128]{2,1,0:T(8,128)(2,1)S(1)} %get-tuple-element.54), channel_id=1, source_target_pairs={{0,1},{1,2},{2,3},{3,4},{4,5},{5,6},{6,7},{8,9},{9,10},{10,11},{11... | collective-permute-start | bytes 196616 | tf_op jit(solution)/shard_map/ppermute | solution.py:451
  47.2 2.1 %collective-permute-start.5 = (bf16[4,64,128]{2,1,0:T(8,128)(2,1)S(1)}, bf16[4,64,128]{2,1,0:T(8,128)(2,1)S(1)}, u32[]{:S(2)}, u32[]{:S(2)}) collective-permute-start(bf16[4,64,128]{2,1,0:T(8,128)(2,1)S(1)} %get-tuple-element.55), channel_id=1, source_target_pairs={{1,0},{2,1},{3,2},{4,3},{5,4},{6,5},{7,6},{9,8},{10,9},{11,10},{12... | collective-permute-start | bytes 196616 | tf_op jit(solution)/shard_map/ppermute | solution.py:451
  49.3 0.4 collective-permute-done.4.left_any.from_left
  49.7 3.4 %collective-permute-done.5.right_any.from_right = bf16[4,64,128]{2,1,0:T(8,128)(2,1)S(1)} collective-permute-done((bf16[4,64,128]{2,1,0:T(8,128)(2,1)S(1)}, bf16[4,64,128]{2,1,0:T(8,128)(2,1)S(1)}, u32[]{:S(2)}, u32[]{:S(2)}) %collective-permute-start.5) | collective-permute-done | bytes 65568 | tf_op jit(solution)/shard_map/ppermute | solution.py:451
  53.1 3.0 %all-to-all-done.parts = bf16[128,16,128]{2,1,0:T(8,128)(2,1)S(1)} async-done(((bf16[128,16,128]{2,1,0:T(8,128)(2,1)}), bf16[128,16,128]{2,1,0:T(8,128)(2,1)S(1)}, u32[]{:S(2)}, u32[]{:S(2)}) %all-to-all-start) | async-done | bytes 524320 | tf_op jit(solution)/shard_map/all_to_all | solution.py:585
  56.1 1.0 %share_kernel.1.after_any = bf16[128,16,128]{2,1,0:T(8,128)(2,1)} custom-call(bf16[128,16,128]{2,1,0:T(8,128)(2,1)S(1)} %all-to-all-done.parts, bf16[4,64,128]{2,1,0:T(8,128)(2,1)S(1)} %collective-permute-done.4.left_any.from_left, bf16[4,64,128]{2,1,0:T(8,128)(2,1)S(1)} %collective-permute-done.5.right_any.from_right), custom_call_target="tpu_custom_call" | custom-call | flops 1000000000 | tf_op jit(solution)/shard_map/share_kernel/pallas_call | solution.py:490
  57.1 5.7 %all-to-all-start.1 = ((bf16[128,16,128]{2,1,0:T(8,128)(2,1)}), bf16[128,16,128]{2,1,0:T(8,128)(2,1)S(1)}, u32[]{:S(2)}, u32[]{:S(2)}) async-start(bf16[128,16,128]{2,1,0:T(8,128)(2,1)} %share_kernel.1.after_any), calls=%async_computation.1 | async-start | bytes 1048576 | tf_op jit(solution)/shard_map/all_to_all | solution.py:599
  62.8 0.0 copy-start.5
  62.8 3.4 %collective-permute-start.6 = (bf16[3,64,128]{2,1,0:T(8,128)(2,1)S(1)}, bf16[3,64,128]{2,1,0:T(8,128)(2,1)S(1)}, u32[]{:S(2)}, u32[]{:S(2)}) collective-permute-start(bf16[3,64,128]{2,1,0:T(8,128)(2,1)S(1)} %get-tuple-element.59), channel_id=1, source_target_pairs={{0,8},{1,9},{2,10},{3,11},{4,12},{5,13},{6,14},{7,15},{8,16},{9,17... | collective-permute-start | bytes 147464 | tf_op jit(solution)/shard_map/ppermute | solution.py:451
  66.3 1.3 %collective-permute-start.7 = (bf16[3,64,128]{2,1,0:T(8,128)(2,1)S(1)}, bf16[3,64,128]{2,1,0:T(8,128)(2,1)S(1)}, u32[]{:S(2)}, u32[]{:S(2)}) collective-permute-start(bf16[3,64,128]{2,1,0:T(8,128)(2,1)S(1)} %get-tuple-element.60), channel_id=1, source_target_pairs={{8,0},{9,1},{10,2},{11,3},{12,4},{13,5},{14,6},{15,7},{16,8},{17,9... | collective-permute-start | bytes 147464 | tf_op jit(solution)/shard_map/ppermute | solution.py:451
  67.6 0.6 collective-permute-done.6.from_up
  68.2 3.2 %collective-permute-done.7.from_down = bf16[3,64,128]{2,1,0:T(8,128)(2,1)S(1)} collective-permute-done((bf16[3,64,128]{2,1,0:T(8,128)(2,1)S(1)}, bf16[3,64,128]{2,1,0:T(8,128)(2,1)S(1)}, u32[]{:S(2)}, u32[]{:S(2)}) %collective-permute-start.7) | collective-permute-done | bytes 49184 | tf_op jit(solution)/shard_map/ppermute | solution.py:451
  71.4 4.0 %third_kernel.1 = bf16[4,64,512]{2,1,0:T(8,128)(2,1)} custom-call(s32[104]{0:T(128)S(1)} %get-tuple-element.34.index_ref, bf16[24,64,128]{2,1,0:T(8,128)(2,1)S(1)} %get-tuple-element.53.hidden_faces, bf16[4,64,128]{2,1,0:T(8,128)(2,1)S(1)} %collective-permute-done.4.left_any.from_left, bf16[4,64,128]{2,1,0:T(8,128)(2,1)S(1)} %collective-permute-done.5.right_any.from_right, ...), custom_call_target="tpu_custom_call" | custom-call | flops 2000000000 | tf_op jit(solution)/shard_map/third_kernel/pallas_call | solution.py:490
  75.4 0.9 %all-to-all-done.1 = bf16[128,16,128]{2,1,0:T(8,128)(2,1)S(1)} async-done(((bf16[128,16,128]{2,1,0:T(8,128)(2,1)}), bf16[128,16,128]{2,1,0:T(8,128)(2,1)S(1)}, u32[]{:S(2)}, u32[]{:S(2)}) %all-to-all-start.1) | async-done | bytes 524320 | tf_op jit(solution)/shard_map/all_to_all | solution.py:599
  76.3 1.6 %unpack_kernel.1 = (f32[27,64,64]{2,1,0:T(8,128)}, f32[27,64,64]{2,1,0:T(8,128)}) custom-call(bf16[2048,128]{1,0:T(8,128)(2,1)S(1)} %bitcast.4), custom_call_target="tpu_custom_call" | custom-call | tf_op jit(solution)/shard_map/unpack_kernel/pallas_call | solution.py:490
  (20 shorter events, 0.1 us)
Async XLA Ops:
  0.6 9.9 %copy-start.6 = (s32[4,512]{1,0:T(4,128)S(1)}, s32[4,512]{1,0:T(4,128)}, u32[]{:S(2)}) copy-start(s32[4,512]{1,0:T(4,128)} %active.3) | copy-start | bytes 24580
  0.6 9.9 %copy-start.4 = (bf16[27,64,64]{2,1,0:T(8,128)(2,1)S(1)}, bf16[27,64,64]{2,1,0:T(8,128)(2,1)}, u32[]{:S(2)}) copy-start(bf16[27,64,64]{2,1,0:T(8,128)(2,1)} %weight.1) | copy-start | bytes 663556
  0.7 9.9 %copy-start.3 = (bf16[27,64,64]{2,1,0:T(8,128)(2,1)S(1)}, bf16[27,64,64]{2,1,0:T(8,128)(2,1)}, u32[]{:S(2)}) copy-start(bf16[27,64,64]{2,1,0:T(8,128)(2,1)} %first.1) | copy-start | bytes 663556
  4.0 8.6 %collective-permute-start = (bf16[8,64,128]{2,1,0:T(8,128)(2,1)}, bf16[8,64,128]{2,1,0:T(8,128)(2,1)S(1)}, u32[]{:S(2)}, u32[]{:S(2)}) collective-permute-start(bf16[8,64,128]{2,1,0:T(8,128)(2,1)} %get-tuple-element.33), channel_id=1, source_target_pairs={{0,1},{1,2},{2,3},{3,4},{4,5},{5,6},{6,7},{8,9},{9,10},{10,11},{11... | collective-permute-start | bytes 393224 | tf_op jit(solution)/shard_map/ppermute | solution.py:451
  8.6 6.5 %collective-permute-start.1 = (bf16[8,64,128]{2,1,0:T(8,128)(2,1)}, bf16[8,64,128]{2,1,0:T(8,128)(2,1)S(1)}, u32[]{:S(2)}, u32[]{:S(2)}) collective-permute-start(bf16[8,64,128]{2,1,0:T(8,128)(2,1)} %get-tuple-element.38), channel_id=1, source_target_pairs={{1,0},{2,1},{3,2},{4,3},{5,4},{6,5},{7,6},{9,8},{10,9},{11,10},{12... | collective-permute-start | bytes 393224 | tf_op jit(solution)/shard_map/ppermute | solution.py:451
  10.5 0.7 copy-start.7
  10.5 0.7 copy-start.8
  11.2 3.9 %copy-start = (bf16[2,64,128]{2,1,0:T(8,128)(2,1)S(1)}, bf16[2,64,128]{2,1,0:T(8,128)(2,1)}, u32[]{:S(2)}) copy-start(bf16[2,64,128]{2,1,0:T(8,128)(2,1)} %get-tuple-element.39.up) | copy-start | bytes 98308
  11.2 3.9 %copy-start.1 = (bf16[2,64,128]{2,1,0:T(8,128)(2,1)S(1)}, bf16[2,64,128]{2,1,0:T(8,128)(2,1)}, u32[]{:S(2)}) copy-start(bf16[2,64,128]{2,1,0:T(8,128)(2,1)} %get-tuple-element.40.down) | copy-start | bytes 98308
  12.6 2.5 %copy-start.2 = (s32[4,26]{1,0:T(4,128)S(1)}, s32[4,26]{1,0:T(4,128)}, u32[]{:S(2)}) copy-start(s32[4,26]{1,0:T(4,128)} %after_any.1) | copy-start | bytes 1252
  15.1 8.3 %collective-permute-start.2 = (bf16[6,64,128]{2,1,0:T(8,128)(2,1)S(1)}, bf16[6,64,128]{2,1,0:T(8,128)(2,1)S(1)}, u32[]{:S(2)}, u32[]{:S(2)}) collective-permute-start(bf16[6,64,128]{2,1,0:T(8,128)(2,1)S(1)} %get-tuple-element.41), channel_id=1, source_target_pairs={{0,8},{1,9},{2,10},{3,11},{4,12},{5,13},{6,14},{7,15},{8,16},{9,17... | collective-permute-start | bytes 294920 | tf_op jit(solution)/shard_map/ppermute | solution.py:451
  18.2 5.5 %copy-start.9 = (bf16[2,24,64,128]{3,2,1,0:T(8,128)(2,1)S(1)}, bf16[2,24,64,128]{3,2,1,0:T(8,128)(2,1)}, u32[]{:S(2)}) copy-start(bf16[2,24,64,128]{3,2,1,0:T(8,128)(2,1)} %get-tuple-element.37.faces) | copy-start | bytes 2359300
  18.2 5.5 %copy-start.10 = (bf16[512,512]{1,0:T(8,128)(2,1)S(1)}, bf16[512,512]{1,0:T(8,128)(2,1)}, u32[]{:S(2)}) copy-start(bf16[512,512]{1,0:T(8,128)(2,1)} %get-tuple-element.36.values) | copy-start | bytes 1572868
  18.3 5.5 %collective-permute-start.3 = (bf16[6,64,128]{2,1,0:T(8,128)(2,1)S(1)}, bf16[6,64,128]{2,1,0:T(8,128)(2,1)S(1)}, u32[]{:S(2)}, u32[]{:S(2)}) collective-permute-start(bf16[6,64,128]{2,1,0:T(8,128)(2,1)S(1)} %get-tuple-element.42), channel_id=1, source_target_pairs={{8,0},{9,1},{10,2},{11,3},{12,4},{13,5},{14,6},{15,7},{16,8},{17,9... | collective-permute-start | bytes 294920 | tf_op jit(solution)/shard_map/ppermute | solution.py:451
  31.8 24.3 %all-to-all-start = ((bf16[128,16,128]{2,1,0:T(8,128)(2,1)}), bf16[128,16,128]{2,1,0:T(8,128)(2,1)S(1)}, u32[]{:S(2)}, u32[]{:S(2)}) async-start(bf16[128,16,128]{2,1,0:T(8,128)(2,1)} %bitcast.2), calls=%async_computation | async-start | bytes 1048576 | tf_op jit(solution)/shard_map/all_to_all | solution.py:585
  43.6 6.1 %collective-permute-start.4 = (bf16[4,64,128]{2,1,0:T(8,128)(2,1)S(1)}, bf16[4,64,128]{2,1,0:T(8,128)(2,1)S(1)}, u32[]{:S(2)}, u32[]{:S(2)}) collective-permute-start(bf16[4,64,128]{2,1,0:T(8,128)(2,1)S(1)} %get-tuple-element.54), channel_id=1, source_target_pairs={{0,1},{1,2},{2,3},{3,4},{4,5},{5,6},{6,7},{8,9},{9,10},{10,11},{11... | collective-permute-start | bytes 196616 | tf_op jit(solution)/shard_map/ppermute | solution.py:451
  47.2 5.9 %collective-permute-start.5 = (bf16[4,64,128]{2,1,0:T(8,128)(2,1)S(1)}, bf16[4,64,128]{2,1,0:T(8,128)(2,1)S(1)}, u32[]{:S(2)}, u32[]{:S(2)}) collective-permute-start(bf16[4,64,128]{2,1,0:T(8,128)(2,1)S(1)} %get-tuple-element.55), channel_id=1, source_target_pairs={{1,0},{2,1},{3,2},{4,3},{5,4},{6,5},{7,6},{9,8},{10,9},{11,10},{12... | collective-permute-start | bytes 196616 | tf_op jit(solution)/shard_map/ppermute | solution.py:451
  57.1 19.2 %all-to-all-start.1 = ((bf16[128,16,128]{2,1,0:T(8,128)(2,1)}), bf16[128,16,128]{2,1,0:T(8,128)(2,1)S(1)}, u32[]{:S(2)}, u32[]{:S(2)}) async-start(bf16[128,16,128]{2,1,0:T(8,128)(2,1)} %share_kernel.1.after_any), calls=%async_computation.1 | async-start | bytes 1048576 | tf_op jit(solution)/shard_map/all_to_all | solution.py:599
  62.8 8.6 %copy-start.5 = (bf16[4,64,512]{2,1,0:T(8,128)(2,1)S(1)}, bf16[4,64,512]{2,1,0:T(8,128)(2,1)}, u32[]{:S(2)}) copy-start(bf16[4,64,512]{2,1,0:T(8,128)(2,1)} %features.1) | copy-start | bytes 786436
  62.8 5.3 %collective-permute-start.6 = (bf16[3,64,128]{2,1,0:T(8,128)(2,1)S(1)}, bf16[3,64,128]{2,1,0:T(8,128)(2,1)S(1)}, u32[]{:S(2)}, u32[]{:S(2)}) collective-permute-start(bf16[3,64,128]{2,1,0:T(8,128)(2,1)S(1)} %get-tuple-element.59), channel_id=1, source_target_pairs={{0,8},{1,9},{2,10},{3,11},{4,12},{5,13},{6,14},{7,15},{8,16},{9,17... | collective-permute-start | bytes 147464 | tf_op jit(solution)/shard_map/ppermute | solution.py:451
  66.3 5.1 %collective-permute-start.7 = (bf16[3,64,128]{2,1,0:T(8,128)(2,1)S(1)}, bf16[3,64,128]{2,1,0:T(8,128)(2,1)S(1)}, u32[]{:S(2)}, u32[]{:S(2)}) collective-permute-start(bf16[3,64,128]{2,1,0:T(8,128)(2,1)S(1)} %get-tuple-element.60), channel_id=1, source_target_pairs={{8,0},{9,1},{10,2},{11,3},{12,4},{13,5},{14,6},{15,7},{16,8},{17,9... | collective-permute-start | bytes 147464 | tf_op jit(solution)/shard_map/ppermute | solution.py:451

commit v4 on v3

--- a/solution.py
+++ b/solution.py
@@ -47,8 +47,8 @@
 READ_FACE = [face_of(tuple(-t for t in d)) for d in DIRECTIONS]
 
 
-YZ_GROUPS = [((0, 1, c), (0, -1, c)) for c in (-1, 0, 1)] + [((0, 0, 1), (0, 0, -1))]
-X_GROUPS = [((1, b, c), (-1, b, c)) for b in (-1, 0, 1) for c in (-1, 0, 1)]
+X_TILES = [(0, 0), (0, None), (None, 0), (None, None)]
+Y_TILES = [(0, 0), (0, None)]
 
 
 def one_hot(rows, source):
@@ -75,13 +75,6 @@
     return lane >> 7, y, cell - y * 10
 
 
-def spread_matrix():
-    plane, y, z = padded_lane(256)
-    y, z = y - 1, z - 1
-    inside = (y >= 0) & (y < 8) & (z >= 0) & (z < 8)
-    return one_hot(128, jnp.where(inside, plane * 64 + y * 8 + z, -1))
-
-
 def window_matrix():
     lane = lanes(1152)
     tap, plane, y, z = lane >> 7, (lane >> 6) & 1, (lane >> 3) & 7, lane & 7
@@ -91,23 +84,23 @@
 
 def yz_matrix():
     x, y, z = padded_lane(1024)
-    group = jnp.where(z == 0, 0, jnp.where(z == 9, 2, 1))
     y_edge, z_edge = (y == 0) | (y == 9), (z == 0) | (z == 9)
     z_cell = jnp.where(z == 0, 7, jnp.where(z == 9, 0, z - 1))
-    from_y = group * 128 + jnp.where(y == 0, 64, 0) + x * 8 + z_cell
-    from_z = 384 + jnp.where(z == 0, 64, 0) + x * 8 + y - 1
-    source = jnp.where(y_edge, from_y, jnp.where(z_edge & (y < 9), from_z, -1))
-    return one_hot(512, source)
+    from_y = jnp.where(z_edge, 128, 0) + jnp.where(y == 0, 64, 0) + x * 8 + z_cell
+    from_z = 256 + jnp.where(z == 0, 64, 0) + x * 8 + y - 1
+    own = 384 + (x & 1) * 64 + (y - 1) * 8 + z - 1
+    source = jnp.where(y_edge, from_y, jnp.where(z_edge, from_z, own))
+    return one_hot(512, jnp.where(y < 10, source, -1))
 
 
 def x_matrix():
     side, y, z = padded_lane(256)
-    y_group = jnp.where(y == 0, 0, jnp.where(y == 9, 2, 1))
-    z_group = jnp.where(z == 0, 0, jnp.where(z == 9, 2, 1))
+    y_edge, z_edge = (y == 0) | (y == 9), (z == 0) | (z == 9)
     y_cell = jnp.where(y == 0, 7, jnp.where(y == 9, 0, y - 1))
     z_cell = jnp.where(z == 0, 7, jnp.where(z == 9, 0, z - 1))
-    source = (y_group * 3 + z_group) * 128 + jnp.where(side == 0, 64, 0) + y_cell * 8 + z_cell
-    return one_hot(1152, jnp.where(y < 10, source, -1))
+    tile = jnp.where(y_edge, 256, 0) + jnp.where(z_edge, 128, 0)
+    source = tile + jnp.where(side == 0, 64, 0) + y_cell * 8 + z_cell
+    return one_hot(512, jnp.where(y < 10, source, -1))
 
 
 def dot(a, b):
@@ -122,75 +115,70 @@
     return lax.broadcasted_iota(jnp.int32, shape, len(shape) - 1) < 64
 
 
-def place(n):
+def place(n, origin):
+    return jnp.where(n >= 0, ((n >> 5) & 3) * 3 + ((n >> 2) & 7) + origin, 9)
+
+
+def own_origin():
     mine = lax.axis_index("brick")
-    owner = (n >> 2) - lax.axis_index("region") * 32
-    dx = (owner & 7) - (mine & 7) + 1
-    dy = (owner >> 3) - (mine >> 3) + 1
-    return jnp.where(n >= 0, jnp.clip(dy * 3 + dx, 0, 8), 9)
-
-
-def choose_sends(neighbours, send_ref):
+    return 4 - (mine >> 3) * 3 - (mine & 7)
+
+
+def choose_sends(neighbours, send_ref, seen=None):
+    origin = own_origin()
     readers = []
     for b in range(4):
-        for f in range(6):
-            bits = 0
-            for e in range(26):
-                if SEND_FACE[e] == f:
-                    bits = bits | jnp.left_shift(1, place(neighbours[b, e]))
-            readers.append(bits)
+        bits = [0] * 6
+        for e in range(26):
+            n = neighbours[b, e]
+            where = place(n, origin)
+            bits[SEND_FACE[e]] = bits[SEND_FACE[e]] | jnp.left_shift(1, where)
+            if seen is not None:
+                seen(b, e, n, where)
+        readers += bits
     for x, y in ARRIVALS:
         s = (y + 1) * 3 + x + 1
-        for t in range(8):
-            send_ref[s * 8 + t] = 0
-        sent = 0
+        for t in range(4):
+            send_ref[s * 32 + t] = 0
+        sent = s * 32
         for f in range(24):
-            send_ref[s * 8 + jnp.minimum(sent, 7)] = f
+            send_ref[sent] = f
             sent = sent + ((readers[f] >> s) & 1)
 
 
 def tables_kernel(
-    neighbours_any, after_any, index_ref, send_ref, neighbours, held, where_ref, rank_ref, sem
+    neighbours_any, after_any, index_ref, send_ref, neighbours, held, rank_ref, sem
 ):
     copy = pltpu.make_async_copy(neighbours_any, neighbours, sem)
     copy.start()
-    copy.wait()
-    choose_sends(neighbours, send_ref)
     for s in range(10):
         held[s] = 0
-
-    def mark(b, carry):
-        for e in range(26):
-            n = neighbours[b, e]
-            where = place(n)
-            where_ref[b * 26 + e] = where
-            held[where] = held[where] | jnp.left_shift(1, (n & 3) * 6 + READ_FACE[e])
-        return carry
-
-    lax.fori_loop(0, 4, mark, 0)
     for f in range(24):
         rank_ref[4 * 24 + f] = f
         rank_ref[9 * 24 + f] = ZERO_ROW
+    rows = {}
+
+    def mark(b, e, n, where):
+        face = (n & 3) * 6 + READ_FACE[e]
+        rows[b, e] = where * 24 + face
+        held[where] = held[where] | jnp.left_shift(1, face)
+
+    copy.wait()
+    choose_sends(neighbours, send_ref, mark)
     for (x, y), (base, count) in ARRIVALS.items():
         s = (y + 1) * 3 + x + 1
         bits = held[s]
-        got = 0
+        got = base
         for f in range(24):
-            rank_ref[s * 24 + f] = base + jnp.minimum(got, count - 1)
+            rank_ref[s * 24 + f] = jnp.minimum(got, base + count - 1)
             got = got + ((bits >> f) & 1)
-
-    def index(b, carry):
-        for e in range(26):
-            row = where_ref[b * 26 + e] * 24 + (neighbours[b, e] & 3) * 6 + READ_FACE[e]
-            index_ref[b * 26 + e] = rank_ref[row]
-        return carry
-
-    lax.fori_loop(0, 4, index, 0)
+    for (b, e), row in rows.items():
+        index_ref[b * 26 + e] = rank_ref[row]
 
 
 def send_slots(send_ref, x, y):
     s = (y + 1) * 3 + x + 1
-    return [send_ref[s * 8 + t] for t in range(4 if y == 0 else 2)]
+    return [send_ref[s * 32 + t] for t in range(4 if y == 0 else 2)]
 
 
 def pack(send_ref, tiles_of, right_ref, left_ref, up_ref, down_ref):
@@ -246,11 +234,10 @@
 
 def prepare_kernel(
     active, first, second, scale, shift,
-    mask_ref, w_first, w_back, gain_ref, shift_ref, e_int, e_yz, e_x, windows,
+    mask_ref, w_first, w_back, gain_ref, shift_ref, e_yz, e_x, windows,
 ):
     mask_ref[...] = active[...].astype(F32)
-    e_int[...], e_yz[...], e_x[...] = spread_matrix(), yz_matrix(), x_matrix()
-    windows[...] = window_matrix()
+    e_yz[...], e_x[...], windows[...] = yz_matrix(), x_matrix(), window_matrix()
     gain_ref[...] = 1.0 + as_column(scale[...])
     shift_ref[...] = as_column(shift[...])
     for i in range(3):
@@ -278,24 +265,47 @@
                 table[0, base + 2 * t], table[0, base + 2 * t + 1] = first, second
 
 
-def build_padded(index_ref, table, values, ext, side_yz, side_x, e_int, e_yz, e_x, arrays):
-    low = low_half((64, 128))
+def build_padded(index_ref, table, values, ext, side_yz, side_x, e_yz, e_x, arrays):
+    lane = lax.broadcasted_iota(jnp.int32, (64, 128), 1)
+    low, u_far, v_far = lane < 64, (lane & 32) != 0, (lane & 4) != 0
     for a in range(arrays):
         for b in range(4):
             row = (a * 4 + b) * 64
-            for side, pairs in ((side_yz, YZ_GROUPS), (side_x, X_GROUPS)):
-                for g, (first, second) in enumerate(pairs):
-                    lo = index_ref[b * 26 + DIRECTIONS.index(first)]
-                    hi = index_ref[b * 26 + DIRECTIONS.index(second)]
-                    side[row : row + 64, g * 128 : g * 128 + 128] = jnp.where(
-                        low, table[a, lo], table[a, hi]
-                    )
+
+            def face(*offset):
+                return table[a, index_ref[b * 26 + DIRECTIONS.index(offset)]]
+
+            def both(low_face, high_face):
+                return jnp.where(low, low_face, high_face)
+
+            def along_v(u, v, make):
+                if v is None:
+                    return jnp.where(v_far, make(u, -1), make(u, 1))
+                return make(u, v)
+
+            def tile(u, v, make):
+                if u is None:
+                    return jnp.where(u_far, along_v(-1, v, make), along_v(1, v, make))
+                return along_v(u, v, make)
+
+            def x_faces(y, z):
+                return both(face(1, y, z), face(-1, y, z))
+
+            for t, (y, z) in enumerate(X_TILES):
+                side_x[row : row + 64, t * 128 : t * 128 + 128] = tile(y, z, x_faces)
+
+            def y_faces(_, z):
+                return both(face(0, 1, z), face(0, -1, z))
+
+            for t, (_, z) in enumerate(Y_TILES):
+                side_yz[row : row + 64, t * 128 : t * 128 + 128] = along_v(0, z, y_faces)
+            side_yz[row : row + 64, 256:384] = both(face(0, 0, 1), face(0, 0, -1))
     outer = dot(side_x[...], e_x[...]).astype(BF)
     ext[:, 0:128] = outer[:, 0:128]
     ext[:, 1152:1280] = outer[:, 128:256]
     for m in range(4):
-        inner = dot(values[:, m * 128 : m * 128 + 128], e_int[...])
-        inner = inner + dot(side_yz[...], e_yz[:, m * 256 : m * 256 + 256])
+        known = jnp.concatenate([side_yz[...], values[:, m * 128 : m * 128 + 128]], axis=1)
+        inner = dot(known, e_yz[:, m * 256 : m * 256 + 256])
         ext[:, 128 + m * 256 : 384 + m * 256] = inner.astype(BF)
 
 
@@ -330,13 +340,13 @@
 
 def second_kernel(
     index_ref, values, faces, from_left, from_right, from_up, from_down, mask_ref,
-    w_first, w_back, gain_ref, shift_ref, e_int, e_yz, e_x, windows,
+    w_first, w_back, gain_ref, shift_ref, e_yz, e_x, windows,
     hidden_ref, sums_ref,
     table, ext, side_yz, side_x, col_a, col_s, stack_h, stack_s,
 ):
     groups = ((from_left, 24, 4), (from_right, 28, 4), (from_up, 32, 6), (from_down, 38, 6))
     fill_table(table, faces, 2, groups)
-    build_padded(index_ref, table, values, ext, side_yz, side_x, e_int, e_yz, e_x, 2)
+    build_padded(index_ref, table, values, ext, side_yz, side_x, e_yz, e_x, 2)
     columns(ext, windows, (col_a, col_s))
     gain = gain_ref[:, 0:1]
     shift = shift_ref[:, 0:1]
@@ -392,16 +402,15 @@
     index_ref, hidden_faces, from_left, from_right, from_up, from_down, hidden,
     active, features, weight,
     out_ref,
-    table, ext, side_yz, side_x, col, w_second, e_int, e_yz, e_x, windows,
+    table, ext, side_yz, side_x, col, w_second, e_yz, e_x, windows,
 ):
-    e_int[...], e_yz[...], e_x[...] = spread_matrix(), yz_matrix(), x_matrix()
-    windows[...] = window_matrix()
+    e_yz[...], e_x[...], windows[...] = yz_matrix(), x_matrix(), window_matrix()
     for i in range(3):
         for jl in range(9):
             w_second[i * 64 : i * 64 + 64, jl * 64 : jl * 64 + 64] = weight[9 * i + jl]
     groups = ((from_left, 24, 4), (from_right, 28, 4), (from_up, 32, 6), (from_down, 38, 6))
     fill_table(table, hidden_faces, 1, groups)
-    build_padded(index_ref, table, hidden, ext, side_yz, side_x, e_int, e_yz, e_x, 1)
+    build_padded(index_ref, table, hidden, ext, side_yz, side_x, e_yz, e_x, 1)
     columns(ext, windows, (col,))
     for pair in range(2):
         product = dot(w_second[...], col[:, pair * 1280 : pair * 1280 + 1280])
@@ -412,16 +421,17 @@
 
 
 def share_kernel(parts, left_any, right_any, out_ref):
-    total = parts[0].astype(F32)
-    for d in range(1, 128):
-        total = total + parts[d].astype(F32)
-    total = total.astype(BF)
+    totals = [parts[d].astype(F32) for d in range(4)]
+    for d in range(4, 128):
+        totals[d % 4] = totals[d % 4] + parts[d].astype(F32)
+    total = ((totals[0] + totals[1]) + (totals[2] + totals[3])).astype(BF)
     for d in range(128):
         out_ref[d] = total
 
 
-def unpack_kernel(sums, first_ref, second_ref):
-    for t in range(2):
+def unpack_kernel(sums, first_any, second_any, first, second, sems):
+    copies = []
+    for t, (grad, grad_any) in enumerate(((second, second_any), (first, first_any))):
         base = t * 864
         for i in range(3):
             for jl in range(9):
@@ -437,9 +447,16 @@
                 block = block.astype(F32)
                 k = 9 * i + jl
                 if t == 0:
-                    second_ref[26 - k] = block
+                    grad[26 - k] = block
                 else:
-                    first_ref[k] = block.T
+                    grad[k] = block.T
+            nine = pl.ds(18 - 9 * i if t == 0 else 9 * i, 9)
+            copies.append(
+                pltpu.make_async_copy(grad.at[nine], grad_any.at[nine], sems.at[3 * t + i])
+            )
+            copies[-1].start()
+    for copy in copies:
+        copy.wait()
 
 
 def sent(array, step):
@@ -516,28 +533,27 @@
             pltpu.VMEM((4, 64, 512), BF),
             pltpu.VMEM((4, 64, 512), BF),
             pltpu.VMEM((4, 512), jnp.int32),
-            pltpu.SMEM((80,), jnp.int32),
+            pltpu.SMEM((288,), jnp.int32),
             pltpu.SemaphoreType.DMA((4,)),
         ],
         58,
         4,
     )
-    arrived = second_round(*first_round(*outgoing[:2]), *outgoing[2:], neighbours)
+    arrived = second_round(*first_round(*outgoing[:2]), *outgoing[2:], outgoing[2])
     index, send_ids = call(
         tables_kernel,
         [(HBM, neighbours), (ANY, arrived[0])],
-        [(SMEM, shape((104,), jnp.int32)), (SMEM, shape((80,), jnp.int32))],
+        [(SMEM, shape((104,), jnp.int32)), (SMEM, shape((288,), jnp.int32))],
         [
             pltpu.SMEM((4, 26), jnp.int32),
             pltpu.SMEM((10,), jnp.int32),
-            pltpu.SMEM((104,), jnp.int32),
             pltpu.SMEM((240,), jnp.int32),
             pltpu.SemaphoreType.DMA,
         ],
         8,
         3,
     )
-    spread_shapes = [(128, 256), (512, 1024), (1152, 256), (256, 1152)]
+    spread_shapes = [(512, 1024), (512, 256), (256, 1152)]
     prepared = call(
         prepare_kernel,
         [
@@ -572,8 +588,8 @@
         [
             pltpu.VMEM((2, 45, 64, 128), BF),
             pltpu.VMEM((512, 1280), BF),
+            pltpu.VMEM((512, 384), BF),
             pltpu.VMEM((512, 512), BF),
-            pltpu.VMEM((512, 1152), BF),
             pltpu.VMEM((576, 2560), BF),
             pltpu.VMEM((576, 2560), BF),
             pltpu.VMEM((192, 2560), BF),
@@ -605,8 +621,8 @@
         [
             pltpu.VMEM((1, 45, 64, 128), BF),
             pltpu.VMEM((256, 1280), BF),
+            pltpu.VMEM((256, 384), BF),
             pltpu.VMEM((256, 512), BF),
-            pltpu.VMEM((256, 1152), BF),
             pltpu.VMEM((576, 2560), BF),
             pltpu.VMEM((192, 576), BF),
         ]
@@ -617,8 +633,12 @@
     grad_first, grad_second = call(
         unpack_kernel,
         [(VMEM, sums.reshape(2048, 128))],
-        [(VMEM, shape((27, 64, 64), F32))] * 2,
-        [],
+        [(ANY, shape((27, 64, 64), F32))] * 2,
+        [
+            pltpu.VMEM((27, 64, 64), F32),
+            pltpu.VMEM((27, 64, 64), F32),
+            pltpu.SemaphoreType.DMA((6,)),
+        ],
         16,
         0,
     )

time: 78.4 us -> 77.6 us (0.990)
  Pallas kernels: 23.9 us -> 21.7 us
  waiting for transfers between devices: 14.5 us -> 15.9 us
    pallas_call x10, Pallas kernels: 23.9 us -> 21.7 us  [call(): pl.pallas_call(kernel, out_shape=tuple((o for _, o in outs)), in_specs=[s...]
    ppermute x8, waiting for transfers between devices: 10.5 us -> 11.8 us  [sent(): return lax.ppermute(array, 'brick', pairs)]
  transfers between devices with their start and end apart: 10 -> 10, of which waited for: 8 -> 8; matrix products, arithmetic and copies ran while one was open for 0% -> 0% of each run, Pallas kernels for 13% -> 11%
where the time goes in v4:
time: 77.6 us; the launch traced here: 77.1 us
  starting transfers between devices  37.8 us (49%)
  Pallas kernels  21.7 us (28%)
  waiting for transfers between devices  15.9 us (20%)
  between operations  1.04 us (1%)
    pallas_call x10, Pallas kernels, call(): pl.pallas_call(kernel, out_shape=tuple((o for _, o in outs)), in_specs=[s...  21.7 us
    ppermute x8, starting transfers between devices, sent(): return lax.ppermute(array, 'brick', pairs)  21.2 us
    ppermute x8, waiting for transfers between devices, sent(): return lax.ppermute(array, 'brick', pairs)  11.8 us
    all_to_all x1, starting transfers between devices, shards(): parts = lax.all_to_all(sums.reshape(128, 16, 128), AXES, 0, 0, tiled=True)  10.8 us
    all_to_all x1, starting transfers between devices, shards(): sums = lax.all_to_all(shares, AXES, 0, 0, tiled=True)  5.72 us
    all_to_all x1, waiting for transfers between devices, shards(): parts = lax.all_to_all(sums.reshape(128, 16, 128), AXES, 0, 0, tiled=True)  3.03 us
  transfers between devices with their start and end apart: 10, of which 8 were waited for; matrix products, arithmetic and copies ran while one was open for 0% of the time, Pallas kernels for 11%

profile of v4, /device:TPU:1, one launch (start us, length us, event | category | flops | bytes accessed | tf_op | source)
XLA Modules:
  0.0 77.1 jit_solution(5478722568991803375)
XLA Ops:
  0.7 3.0 %first_kernel.1 = (bf16[512,512]{1,0:T(8,128)(2,1)}, bf16[2,24,64,128]{3,2,1,0:T(8,128)(2,1)}, bf16[8,64,128]{2,1,0:T(8,128)(2,1)}, bf16[8,64,128]{2,1,0:T(8,128...) custom-call(s32[4,26]{1,0:T(4,128)} %neighbours_any.3, bf16[4,64,512]{2,1,0:T(8,128)(2,1)} %features.1, ...), custom_call_target="tpu_custom_call" | custom-call | flops 4000000000 | tf_op jit(solution)/shard_map/first_kernel/pallas_call | solution.py:507
  3.7 4.6 %collective-permute-start = (bf16[8,64,128]{2,1,0:T(8,128)(2,1)}, bf16[8,64,128]{2,1,0:T(8,128)(2,1)S(1)}, u32[]{:S(2)}, u32[]{:S(2)}) collective-permute-start(bf16[8,64,128]{2,1,0:T(8,128)(2,1)} %get-tuple-element.32), channel_id=1, source_target_pairs={{0,1},{1,2},{2,3},{3,4},{4,5},{5,6},{6,7},{8,9},{9,10},{10,11},{11... | collective-permute-start | bytes 393224 | tf_op jit(solution)/shard_map/ppermute | solution.py:468
  8.3 1.9 %collective-permute-start.1 = (bf16[8,64,128]{2,1,0:T(8,128)(2,1)}, bf16[8,64,128]{2,1,0:T(8,128)(2,1)S(1)}, u32[]{:S(2)}, u32[]{:S(2)}) collective-permute-start(bf16[8,64,128]{2,1,0:T(8,128)(2,1)} %get-tuple-element.37), channel_id=1, source_target_pairs={{1,0},{2,1},{3,2},{4,3},{5,4},{6,5},{7,6},{9,8},{10,9},{11,10},{12... | collective-permute-start | bytes 393224 | tf_op jit(solution)/shard_map/ppermute | solution.py:468
  10.2 0.0 copy-start.7
  10.3 0.6 copy-done.7
  10.9 0.0 copy-done.8
  10.9 1.2 %prepare_kernel.1 = (f32[4,512]{1,0:T(4,128)S(1)}, bf16[192,576]{1,0:T(8,128)(2,1)S(1)}, bf16[192,576]{1,0:T(8,128)(2,1)S(1)}, f32[64,128]{1,0:T(8,128)S(1)}, f3...) custom-call(s32[4,512]{1,0:T(4,128)S(1)} %copy-done.5, ...), custom_call_target="tpu_custom_call" | custom-call | flops 3000000000 | tf_op jit(solution)/shard_map/prepare_kernel/pallas_call | solution.py:507
  12.1 2.7 %collective-permute-done.1.from_right = bf16[8,64,128]{2,1,0:T(8,128)(2,1)S(1)} collective-permute-done((bf16[8,64,128]{2,1,0:T(8,128)(2,1)}, bf16[8,64,128]{2,1,0:T(8,128)(2,1)S(1)}, u32[]{:S(2)}, u32[]{:S(2)}) %collective-permute-start.1) | collective-permute-done | bytes 131104 | tf_op jit(solution)/shard_map/ppermute | solution.py:468
  14.8 0.0 copy-start.6
  14.8 3.1 %collective-permute-start.2 = (bf16[6,64,128]{2,1,0:T(8,128)(2,1)S(1)}, bf16[6,64,128]{2,1,0:T(8,128)(2,1)S(1)}, u32[]{:S(2)}, u32[]{:S(2)}) collective-permute-start(bf16[6,64,128]{2,1,0:T(8,128)(2,1)S(1)} %get-tuple-element.40), channel_id=1, source_target_pairs={{0,8},{1,9},{2,10},{3,11},{4,12},{5,13},{6,14},{7,15},{8,16},{9,17... | collective-permute-start | bytes 294920 | tf_op jit(solution)/shard_map/ppermute | solution.py:468
  18.0 0.0 copy-start.9
  18.0 0.0 copy-start.10
  18.0 1.4 %collective-permute-start.3 = (bf16[6,64,128]{2,1,0:T(8,128)(2,1)S(1)}, bf16[6,64,128]{2,1,0:T(8,128)(2,1)S(1)}, u32[]{:S(2)}, u32[]{:S(2)}) collective-permute-start(bf16[6,64,128]{2,1,0:T(8,128)(2,1)S(1)} %get-tuple-element.41), channel_id=1, source_target_pairs={{8,0},{9,1},{10,2},{11,3},{12,4},{13,5},{14,6},{15,7},{16,8},{17,9... | collective-permute-start | bytes 294920 | tf_op jit(solution)/shard_map/ppermute | solution.py:468
  19.4 2.7 %tables_kernel.1 = (s32[104]{0:T(128)S(1)}, s32[288]{0:T(512)S(1)}) custom-call(s32[4,26]{1,0:T(4,128)S(1)} %copy-done.6, bf16[8,64,128]{2,1,0:T(8,128)(2,1)S(1)} %collective-permute-done.after_any.from_left), custom_call_target="tpu_custom_call" | custom-call | flops 3000000000 | tf_op jit(solution)/shard_map/tables_kernel/pallas_call | solution.py:507
  22.2 1.3 %collective-permute-done.3.from_down = bf16[6,64,128]{2,1,0:T(8,128)(2,1)S(1)} collective-permute-done((bf16[6,64,128]{2,1,0:T(8,128)(2,1)S(1)}, bf16[6,64,128]{2,1,0:T(8,128)(2,1)S(1)}, u32[]{:S(2)}, u32[]{:S(2)}) %collective-permute-start.3) | collective-permute-done | bytes 98336 | tf_op jit(solution)/shard_map/ppermute | solution.py:468
  23.5 7.7 %second_kernel.1 = (bf16[256,512]{1,0:T(8,128)(2,1)S(1)}, bf16[2048,128]{1,0:T(8,128)(2,1)}) custom-call(s32[104]{0:T(128)S(1)} %get-tuple-element.33.index_ref, bf16[512,512]{1,0:T(8,128)(2,1)S(1)} %copy-done.10, bf16[2,24,64,128]{3,2,1,0:T(8,128)(2,1)S(1)} %copy-done.9, bf16[8,64,128]{2,1,0:T(8,128)(2,1)S(1)} %collective-permute-done.after_any.from_left, ...), custom_call_target="tpu_custom_call" | custom-call | flops 10000000000 | tf_op jit(solution)/shard_map/second_kernel/pallas_call | solution.py:507
  31.2 10.8 %all-to-all-start = ((bf16[128,16,128]{2,1,0:T(8,128)(2,1)}), bf16[128,16,128]{2,1,0:T(8,128)(2,1)S(1)}, u32[]{:S(2)}, u32[]{:S(2)}) async-start(bf16[128,16,128]{2,1,0:T(8,128)(2,1)} %bitcast.2), calls=%async_computation | async-start | bytes 1048576 | tf_op jit(solution)/shard_map/all_to_all | solution.py:601
  42.0 1.0 %faces_kernel.1 = (bf16[24,64,128]{2,1,0:T(8,128)(2,1)S(1)}, bf16[4,64,128]{2,1,0:T(8,128)(2,1)S(1)}, bf16[4,64,128]{2,1,0:T(8,128)(2,1)S(1)}, bf16[1,64,128]{2,1,0:T(8,128)(2,1)S(1)}, bf16[1,64,128]{2,1,0:T(8,128)(2,1)S(1)}) custom-call(s32[288]{0:T(512)S(1)} %get-tuple-element.34.send_ref, bf16[256,512]{1,0:T(8,128)(2,1)S(1)} %get-tuple-element.50.hidden), custom_call_target="tpu_custom_call" | custom-call | flops 8000000000 | tf_op jit(solution)/shard_map/faces_kernel/pallas_call | solution.py:507
  43.0 3.5 %collective-permute-start.4 = (bf16[4,64,128]{2,1,0:T(8,128)(2,1)S(1)}, bf16[4,64,128]{2,1,0:T(8,128)(2,1)S(1)}, u32[]{:S(2)}, u32[]{:S(2)}) collective-permute-start(bf16[4,64,128]{2,1,0:T(8,128)(2,1)S(1)} %get-tuple-element.52), channel_id=1, source_target_pairs={{0,1},{1,2},{2,3},{3,4},{4,5},{5,6},{6,7},{8,9},{9,10},{10,11},{11... | collective-permute-start | bytes 196616 | tf_op jit(solution)/shard_map/ppermute | solution.py:468
  46.6 1.9 %collective-permute-start.5 = (bf16[4,64,128]{2,1,0:T(8,128)(2,1)S(1)}, bf16[4,64,128]{2,1,0:T(8,128)(2,1)S(1)}, u32[]{:S(2)}, u32[]{:S(2)}) collective-permute-start(bf16[4,64,128]{2,1,0:T(8,128)(2,1)S(1)} %get-tuple-element.53), channel_id=1, source_target_pairs={{1,0},{2,1},{3,2},{4,3},{5,4},{6,5},{7,6},{9,8},{10,9},{11,10},{12... | collective-permute-start | bytes 196616 | tf_op jit(solution)/shard_map/ppermute | solution.py:468
  48.5 0.7 collective-permute-done.4.left_any.from_left
  49.2 3.3 %collective-permute-done.5.right_any.from_right = bf16[4,64,128]{2,1,0:T(8,128)(2,1)S(1)} collective-permute-done((bf16[4,64,128]{2,1,0:T(8,128)(2,1)S(1)}, bf16[4,64,128]{2,1,0:T(8,128)(2,1)S(1)}, u32[]{:S(2)}, u32[]{:S(2)}) %collective-permute-start.5) | collective-permute-done | bytes 65568 | tf_op jit(solution)/shard_map/ppermute | solution.py:468
  52.5 3.0 %all-to-all-done.parts = bf16[128,16,128]{2,1,0:T(8,128)(2,1)S(1)} async-done(((bf16[128,16,128]{2,1,0:T(8,128)(2,1)}), bf16[128,16,128]{2,1,0:T(8,128)(2,1)S(1)}, u32[]{:S(2)}, u32[]{:S(2)}) %all-to-all-start) | async-done | bytes 524320 | tf_op jit(solution)/shard_map/all_to_all | solution.py:601
  55.5 0.9 %share_kernel.1.after_any = bf16[128,16,128]{2,1,0:T(8,128)(2,1)} custom-call(bf16[128,16,128]{2,1,0:T(8,128)(2,1)S(1)} %all-to-all-done.parts, bf16[4,64,128]{2,1,0:T(8,128)(2,1)S(1)} %collective-permute-done.4.left_any.from_left, bf16[4,64,128]{2,1,0:T(8,128)(2,1)S(1)} %collective-permute-done.5.right_any.from_right), custom_call_target="tpu_custom_call" | custom-call | flops 1000000000 | tf_op jit(solution)/shard_map/share_kernel/pallas_call | solution.py:507
  56.4 5.7 %all-to-all-start.1 = ((bf16[128,16,128]{2,1,0:T(8,128)(2,1)}), bf16[128,16,128]{2,1,0:T(8,128)(2,1)S(1)}, u32[]{:S(2)}, u32[]{:S(2)}) async-start(bf16[128,16,128]{2,1,0:T(8,128)(2,1)} %share_kernel.1.after_any), calls=%async_computation.1 | async-start | bytes 1048576 | tf_op jit(solution)/shard_map/all_to_all | solution.py:615
  62.2 3.4 %collective-permute-start.6 = (bf16[3,64,128]{2,1,0:T(8,128)(2,1)S(1)}, bf16[3,64,128]{2,1,0:T(8,128)(2,1)S(1)}, u32[]{:S(2)}, u32[]{:S(2)}) collective-permute-start(bf16[3,64,128]{2,1,0:T(8,128)(2,1)S(1)} %get-tuple-element.57), channel_id=1, source_target_pairs={{0,8},{1,9},{2,10},{3,11},{4,12},{5,13},{6,14},{7,15},{8,16},{9,17... | collective-permute-start | bytes 147464 | tf_op jit(solution)/shard_map/ppermute | solution.py:468
  65.6 1.3 %collective-permute-start.7 = (bf16[3,64,128]{2,1,0:T(8,128)(2,1)S(1)}, bf16[3,64,128]{2,1,0:T(8,128)(2,1)S(1)}, u32[]{:S(2)}, u32[]{:S(2)}) collective-permute-start(bf16[3,64,128]{2,1,0:T(8,128)(2,1)S(1)} %get-tuple-element.58), channel_id=1, source_target_pairs={{8,0},{9,1},{10,2},{11,3},{12,4},{13,5},{14,6},{15,7},{16,8},{17,9... | collective-permute-start | bytes 147464 | tf_op jit(solution)/shard_map/ppermute | solution.py:468
  66.9 0.6 collective-permute-done.6.from_up
  67.5 3.2 %collective-permute-done.7.from_down = bf16[3,64,128]{2,1,0:T(8,128)(2,1)S(1)} collective-permute-done((bf16[3,64,128]{2,1,0:T(8,128)(2,1)S(1)}, bf16[3,64,128]{2,1,0:T(8,128)(2,1)S(1)}, u32[]{:S(2)}, u32[]{:S(2)}) %collective-permute-start.7) | collective-permute-done | bytes 49184 | tf_op jit(solution)/shard_map/ppermute | solution.py:468
  70.8 3.9 %third_kernel.1 = bf16[4,64,512]{2,1,0:T(8,128)(2,1)} custom-call(s32[104]{0:T(128)S(1)} %get-tuple-element.33.index_ref, bf16[24,64,128]{2,1,0:T(8,128)(2,1)S(1)} %get-tuple-element.51.hidden_faces, bf16[4,64,128]{2,1,0:T(8,128)(2,1)S(1)} %collective-permute-done.4.left_any.from_left, bf16[4,64,128]{2,1,0:T(8,128)(2,1)S(1)} %collective-permute-done.5.right_any.from_right, ...), custom_call_target="tpu_custom_call" | custom-call | flops 2000000000 | tf_op jit(solution)/shard_map/third_kernel/pallas_call | solution.py:507
  74.6 1.0 %all-to-all-done.1 = bf16[128,16,128]{2,1,0:T(8,128)(2,1)S(1)} async-done(((bf16[128,16,128]{2,1,0:T(8,128)(2,1)}), bf16[128,16,128]{2,1,0:T(8,128)(2,1)S(1)}, u32[]{:S(2)}, u32[]{:S(2)}) %all-to-all-start.1) | async-done | bytes 524320 | tf_op jit(solution)/shard_map/all_to_all | solution.py:615
  75.7 1.3 %unpack_kernel.1 = (f32[27,64,64]{2,1,0:T(8,128)}, f32[27,64,64]{2,1,0:T(8,128)}) custom-call(bf16[2048,128]{1,0:T(8,128)(2,1)S(1)} %bitcast.4), custom_call_target="tpu_custom_call" | custom-call | tf_op jit(solution)/shard_map/unpack_kernel/pallas_call | solution.py:507
  (20 shorter events, 0.1 us)
Async XLA Ops:
  0.6 9.6 %copy-start.5 = (s32[4,512]{1,0:T(4,128)S(1)}, s32[4,512]{1,0:T(4,128)}, u32[]{:S(2)}) copy-start(s32[4,512]{1,0:T(4,128)} %active.3) | copy-start | bytes 24580
  0.6 9.6 %copy-start.3 = (bf16[27,64,64]{2,1,0:T(8,128)(2,1)S(1)}, bf16[27,64,64]{2,1,0:T(8,128)(2,1)}, u32[]{:S(2)}) copy-start(bf16[27,64,64]{2,1,0:T(8,128)(2,1)} %weight.1) | copy-start | bytes 663556
  0.7 9.6 %copy-start.2 = (bf16[27,64,64]{2,1,0:T(8,128)(2,1)S(1)}, bf16[27,64,64]{2,1,0:T(8,128)(2,1)}, u32[]{:S(2)}) copy-start(bf16[27,64,64]{2,1,0:T(8,128)(2,1)} %first.1) | copy-start | bytes 663556
  3.7 8.4 %collective-permute-start = (bf16[8,64,128]{2,1,0:T(8,128)(2,1)}, bf16[8,64,128]{2,1,0:T(8,128)(2,1)S(1)}, u32[]{:S(2)}, u32[]{:S(2)}) collective-permute-start(bf16[8,64,128]{2,1,0:T(8,128)(2,1)} %get-tuple-element.32), channel_id=1, source_target_pairs={{0,1},{1,2},{2,3},{3,4},{4,5},{5,6},{6,7},{8,9},{9,10},{10,11},{11... | collective-permute-start | bytes 393224 | tf_op jit(solution)/shard_map/ppermute | solution.py:468
  8.3 6.5 %collective-permute-start.1 = (bf16[8,64,128]{2,1,0:T(8,128)(2,1)}, bf16[8,64,128]{2,1,0:T(8,128)(2,1)S(1)}, u32[]{:S(2)}, u32[]{:S(2)}) collective-permute-start(bf16[8,64,128]{2,1,0:T(8,128)(2,1)} %get-tuple-element.37), channel_id=1, source_target_pairs={{1,0},{2,1},{3,2},{4,3},{5,4},{6,5},{7,6},{9,8},{10,9},{11,10},{12... | collective-permute-start | bytes 393224 | tf_op jit(solution)/shard_map/ppermute | solution.py:468
  10.2 0.7 copy-start.7
  10.2 0.7 copy-start.8
  10.9 3.9 %copy-start = (bf16[2,64,128]{2,1,0:T(8,128)(2,1)S(1)}, bf16[2,64,128]{2,1,0:T(8,128)(2,1)}, u32[]{:S(2)}) copy-start(bf16[2,64,128]{2,1,0:T(8,128)(2,1)} %get-tuple-element.38.up.after_any) | copy-start | bytes 98308
  10.9 3.9 %copy-start.1 = (bf16[2,64,128]{2,1,0:T(8,128)(2,1)S(1)}, bf16[2,64,128]{2,1,0:T(8,128)(2,1)}, u32[]{:S(2)}) copy-start(bf16[2,64,128]{2,1,0:T(8,128)(2,1)} %get-tuple-element.39.down) | copy-start | bytes 98308
  14.8 4.6 %copy-start.6 = (s32[4,26]{1,0:T(4,128)S(1)}, s32[4,26]{1,0:T(4,128)}, u32[]{:S(2)}) copy-start(s32[4,26]{1,0:T(4,128)} %neighbours_any.3) | copy-start | bytes 1252
  14.8 7.3 %collective-permute-start.2 = (bf16[6,64,128]{2,1,0:T(8,128)(2,1)S(1)}, bf16[6,64,128]{2,1,0:T(8,128)(2,1)S(1)}, u32[]{:S(2)}, u32[]{:S(2)}) collective-permute-start(bf16[6,64,128]{2,1,0:T(8,128)(2,1)S(1)} %get-tuple-element.40), channel_id=1, source_target_pairs={{0,8},{1,9},{2,10},{3,11},{4,12},{5,13},{6,14},{7,15},{8,16},{9,17... | collective-permute-start | bytes 294920 | tf_op jit(solution)/shard_map/ppermute | solution.py:468
  18.0 5.5 %copy-start.9 = (bf16[2,24,64,128]{3,2,1,0:T(8,128)(2,1)S(1)}, bf16[2,24,64,128]{3,2,1,0:T(8,128)(2,1)}, u32[]{:S(2)}) copy-start(bf16[2,24,64,128]{3,2,1,0:T(8,128)(2,1)} %get-tuple-element.36.faces) | copy-start | bytes 2359300
  18.0 5.5 %copy-start.10 = (bf16[512,512]{1,0:T(8,128)(2,1)S(1)}, bf16[512,512]{1,0:T(8,128)(2,1)}, u32[]{:S(2)}) copy-start(bf16[512,512]{1,0:T(8,128)(2,1)} %get-tuple-element.35.values) | copy-start | bytes 1572868
  18.0 5.5 %collective-permute-start.3 = (bf16[6,64,128]{2,1,0:T(8,128)(2,1)S(1)}, bf16[6,64,128]{2,1,0:T(8,128)(2,1)S(1)}, u32[]{:S(2)}, u32[]{:S(2)}) collective-permute-start(bf16[6,64,128]{2,1,0:T(8,128)(2,1)S(1)} %get-tuple-element.41), channel_id=1, source_target_pairs={{8,0},{9,1},{10,2},{11,3},{12,4},{13,5},{14,6},{15,7},{16,8},{17,9... | collective-permute-start | bytes 294920 | tf_op jit(solution)/shard_map/ppermute | solution.py:468
  31.2 24.3 %all-to-all-start = ((bf16[128,16,128]{2,1,0:T(8,128)(2,1)}), bf16[128,16,128]{2,1,0:T(8,128)(2,1)S(1)}, u32[]{:S(2)}, u32[]{:S(2)}) async-start(bf16[128,16,128]{2,1,0:T(8,128)(2,1)} %bitcast.2), calls=%async_computation | async-start | bytes 1048576 | tf_op jit(solution)/shard_map/all_to_all | solution.py:601
  43.0 6.2 %collective-permute-start.4 = (bf16[4,64,128]{2,1,0:T(8,128)(2,1)S(1)}, bf16[4,64,128]{2,1,0:T(8,128)(2,1)S(1)}, u32[]{:S(2)}, u32[]{:S(2)}) collective-permute-start(bf16[4,64,128]{2,1,0:T(8,128)(2,1)S(1)} %get-tuple-element.52), channel_id=1, source_target_pairs={{0,1},{1,2},{2,3},{3,4},{4,5},{5,6},{6,7},{8,9},{9,10},{10,11},{11... | collective-permute-start | bytes 196616 | tf_op jit(solution)/shard_map/ppermute | solution.py:468
  46.6 5.9 %collective-permute-start.5 = (bf16[4,64,128]{2,1,0:T(8,128)(2,1)S(1)}, bf16[4,64,128]{2,1,0:T(8,128)(2,1)S(1)}, u32[]{:S(2)}, u32[]{:S(2)}) collective-permute-start(bf16[4,64,128]{2,1,0:T(8,128)(2,1)S(1)} %get-tuple-element.53), channel_id=1, source_target_pairs={{1,0},{2,1},{3,2},{4,3},{5,4},{6,5},{7,6},{9,8},{10,9},{11,10},{12... | collective-permute-start | bytes 196616 | tf_op jit(solution)/shard_map/ppermute | solution.py:468
  56.4 19.2 %all-to-all-start.1 = ((bf16[128,16,128]{2,1,0:T(8,128)(2,1)}), bf16[128,16,128]{2,1,0:T(8,128)(2,1)S(1)}, u32[]{:S(2)}, u32[]{:S(2)}) async-start(bf16[128,16,128]{2,1,0:T(8,128)(2,1)} %share_kernel.1.after_any), calls=%async_computation.1 | async-start | bytes 1048576 | tf_op jit(solution)/shard_map/all_to_all | solution.py:615
  62.2 8.6 %copy-start.4 = (bf16[4,64,512]{2,1,0:T(8,128)(2,1)S(1)}, bf16[4,64,512]{2,1,0:T(8,128)(2,1)}, u32[]{:S(2)}) copy-start(bf16[4,64,512]{2,1,0:T(8,128)(2,1)} %features.1) | copy-start | bytes 786436
  62.2 5.3 %collective-permute-start.6 = (bf16[3,64,128]{2,1,0:T(8,128)(2,1)S(1)}, bf16[3,64,128]{2,1,0:T(8,128)(2,1)S(1)}, u32[]{:S(2)}, u32[]{:S(2)}) collective-permute-start(bf16[3,64,128]{2,1,0:T(8,128)(2,1)S(1)} %get-tuple-element.57), channel_id=1, source_target_pairs={{0,8},{1,9},{2,10},{3,11},{4,12},{5,13},{6,14},{7,15},{8,16},{9,17... | collective-permute-start | bytes 147464 | tf_op jit(solution)/shard_map/ppermute | solution.py:468
  65.6 5.1 %collective-permute-start.7 = (bf16[3,64,128]{2,1,0:T(8,128)(2,1)S(1)}, bf16[3,64,128]{2,1,0:T(8,128)(2,1)S(1)}, u32[]{:S(2)}, u32[]{:S(2)}) collective-permute-start(bf16[3,64,128]{2,1,0:T(8,128)(2,1)S(1)} %get-tuple-element.58), channel_id=1, source_target_pairs={{8,0},{9,1},{10,2},{11,3},{12,4},{13,5},{14,6},{15,7},{16,8},{17,9... | collective-permute-start | bytes 147464 | tf_op jit(solution)/shard_map/ppermute | solution.py:468

commit v5 on v4

--- a/solution.py
+++ b/solution.py
@@ -191,10 +191,19 @@
             ref[t] = tile
 
 
+def own_faces(values, faces_ref):
+    faces = dot(values[...], face_matrix()).astype(BF)
+    for a in range(2):
+        for b in range(4):
+            for f in range(6):
+                row = (a * 4 + b) * 64
+                faces_ref[a, b * 6 + f] = faces[row : row + 64, f * 128 : f * 128 + 128]
+
+
 def first_kernel(
     neighbours_any, features_any, cotangent_any, active_any,
-    values_ref, faces_ref, right_ref, left_ref, up_ref, down_ref,
-    neighbours, features, cotangent, active, send_ref, sems,
+    values_ref, right_ref, left_ref, up_ref, down_ref,
+    faces_ref, neighbours, features, cotangent, active, send_ref, sems,
 ):
     pairs = (
         (neighbours_any, neighbours), (features_any, features), (cotangent_any, cotangent),
@@ -211,12 +220,7 @@
         f = features[b].astype(F32)
         values_ref[b * 64 : b * 64 + 64, :] = (mask * (f / (1.0 + jnp.exp(-f)))).astype(BF)
         values_ref[256 + b * 64 : 320 + b * 64, :] = (mask * cotangent[b].astype(F32)).astype(BF)
-    faces = dot(values_ref[...], face_matrix()).astype(BF)
-    for a in range(2):
-        for b in range(4):
-            for f in range(6):
-                row = (a * 4 + b) * 64
-                faces_ref[a, b * 6 + f] = faces[row : row + 64, f * 128 : f * 128 + 128]
+    own_faces(values_ref, faces_ref)
     low = low_half((64, 128))
     pack(
         send_ref,
@@ -233,9 +237,10 @@
 
 
 def prepare_kernel(
-    active, first, second, scale, shift,
-    mask_ref, w_first, w_back, gain_ref, shift_ref, e_yz, e_x, windows,
+    values, active, first, second, scale, shift,
+    faces_ref, mask_ref, w_first, w_back, gain_ref, shift_ref, e_yz, e_x, windows,
 ):
+    own_faces(values, faces_ref)
     mask_ref[...] = active[...].astype(F32)
     e_yz[...], e_x[...], windows[...] = yz_matrix(), x_matrix(), window_matrix()
     gain_ref[...] = 1.0 + as_column(scale[...])
@@ -341,9 +346,18 @@
 def second_kernel(
     index_ref, values, faces, from_left, from_right, from_up, from_down, mask_ref,
     w_first, w_back, gain_ref, shift_ref, e_yz, e_x, windows,
-    hidden_ref, sums_ref,
-    table, ext, side_yz, side_x, col_a, col_s, stack_h, stack_s,
+    hidden_ref, sums_any,
+    table, ext, side_yz, side_x, col_a, col_s, stack_h, stack_s, sums_ref, sems,
 ):
+    copies = []
+
+    def send(start, stop, t):
+        rows = pl.ds(start, stop - start)
+        copies.append(pltpu.make_async_copy(sums_ref.at[rows], sums_any.at[rows], sems.at[t]))
+        copies[-1].start()
+
+    sums_ref[1728:2048, :] = jnp.zeros((320, 128), BF)
+    send(1728, 2048, 0)
     groups = ((from_left, 24, 4), (from_right, 28, 4), (from_up, 32, 6), (from_down, 38, 6))
     fill_table(table, faces, 2, groups)
     build_padded(index_ref, table, values, ext, side_yz, side_x, e_yz, e_x, 2)
@@ -365,9 +379,12 @@
             hidden_ref[b * 64 : b * 64 + 64, :] = hidden
             stack_planes(stack_h, b * 640, hidden)
             stack_planes(stack_s, b * 640, slope)
-    total_h = dot_nt(col_s[...], stack_h[...])
-    total_s = dot_nt(col_a[...], stack_s[...])
-    pack_sums(total_h, total_s, sums_ref)
+    pack_sums(dot_nt(col_s[...], stack_h[...]), sums_ref, 0)
+    send(0, 864, 1)
+    pack_sums(dot_nt(col_a[...], stack_s[...]), sums_ref, 864)
+    send(864, 1728, 2)
+    for copy in copies:
+        copy.wait()
 
 
 def faces_kernel(
@@ -388,14 +405,11 @@
     )
 
 
-def pack_sums(total_h, total_s, sums_ref):
-    for t, total in enumerate((total_h, total_s)):
-        base = t * 864
-        sums_ref[base : base + 576, :] = total[:, 0:128].astype(BF)
-        sums_ref[base + 576 : base + 864, :] = jnp.concatenate(
-            [total[0:288, 128:192], total[288:576, 128:192]], axis=1
-        ).astype(BF)
-    sums_ref[1728:2048, :] = jnp.zeros((320, 128), BF)
+def pack_sums(total, sums_ref, base):
+    sums_ref[base : base + 576, :] = total[:, 0:128].astype(BF)
+    sums_ref[base + 576 : base + 864, :] = jnp.concatenate(
+        [total[0:288, 128:192], total[288:576, 128:192]], axis=1
+    ).astype(BF)
 
 
 def third_kernel(
@@ -523,12 +537,12 @@
         return [(VMEM, shape((n * arrays, 64, 128))) for n in (4, 4, 1, 1)]
 
 
-    values, faces, *outgoing = call(
+    values, *outgoing = call(
         first_kernel,
         [(HBM, t) for t in (neighbours, features, cotangent, active)],
-        [(VMEM, shape((512, 512))), (VMEM, shape((2, 24, 64, 128)))]
-        + messages(2),
+        [(VMEM, shape((512, 512)))] + messages(2),
         [
+            pltpu.VMEM((2, 24, 64, 128), BF),
             pltpu.SMEM((4, 26), jnp.int32),
             pltpu.VMEM((4, 64, 512), BF),
             pltpu.VMEM((4, 64, 512), BF),
@@ -536,7 +550,7 @@
             pltpu.SMEM((288,), jnp.int32),
             pltpu.SemaphoreType.DMA((4,)),
         ],
-        58,
+        56,
         4,
     )
     arrived = second_round(*first_round(*outgoing[:2]), *outgoing[2:], outgoing[2])
@@ -559,6 +573,7 @@
         [
             (VMEM, t)
             for t in (
+                values,
                 active,
                 first_weight,
                 second_weight,
@@ -566,7 +581,7 @@
                 film_shift.reshape(1, 64),
             )
         ],
-        [(VMEM, shape((4, 512), F32))]
+        [(VMEM, shape((2, 24, 64, 128))), (VMEM, shape((4, 512), F32))]
         + [(VMEM, shape((192, 576)))] * 2
         + [(VMEM, shape((64, 128), F32))] * 2
         + [(VMEM, shape(dims)) for dims in spread_shapes],
@@ -574,7 +589,7 @@
         16,
         3,
     )
-    mask, w_first, w_back, gain, shift, *spreads = prepared
+    faces, mask, w_first, w_back, gain, shift, *spreads = prepared
 
     hidden, sums = call(
         second_kernel,
@@ -583,7 +598,7 @@
         + [(VMEM, t) for t in spreads],
         [
             (VMEM, shape((256, 512))),
-            (VMEM, shape((2048, 128))),
+            (ANY, shape((2048, 128))),
         ],
         [
             pltpu.VMEM((2, 45, 64, 128), BF),
@@ -594,6 +609,8 @@
             pltpu.VMEM((576, 2560), BF),
             pltpu.VMEM((192, 2560), BF),
             pltpu.VMEM((192, 2560), BF),
+            pltpu.VMEM((2048, 128), BF),
+            pltpu.SemaphoreType.DMA((3,)),
         ],
         32,
         10,

time: 77.6 us -> 77.5 us (level)
  waiting for transfers between devices: 15.9 us -> 14.8 us
  local copies, waits for them, and re-layouts: 0.67 us -> 1.71 us
    ppermute x8, waiting for transfers between devices: 11.8 us -> 10.7 us  [sent(): return lax.ppermute(array, 'brick', pairs)]
    unnamed x22, local copies, waits for them, and re-layouts: 0.67 us -> 1.71 us
where the time goes in v5:
time: 77.5 us; the launch traced here: 76.9 us
  starting transfers between devices  38 us (49%)
  Pallas kernels  21.4 us (28%)
  waiting for transfers between devices  14.8 us (19%)
  local copies, waits for them, and re-layouts  1.71 us (2%)
  between operations  1.04 us (1%)
    ppermute x8, starting transfers between devices, sent(): return lax.ppermute(array, 'brick', pairs)  21.4 us
    pallas_call x10, Pallas kernels, call(): pl.pallas_call(kernel, out_shape=tuple((o for _, o in outs)), in_specs=[s...  21.4 us
    all_to_all x1, starting transfers between devices, shards(): parts = lax.all_to_all(sums.reshape(128, 16, 128), AXES, 0, 0, tiled=True)  10.8 us
    ppermute x8, waiting for transfers between devices, sent(): return lax.ppermute(array, 'brick', pairs)  10.7 us
    all_to_all x1, starting transfers between devices, shards(): sums = lax.all_to_all(shares, AXES, 0, 0, tiled=True)  5.72 us
    all_to_all x1, waiting for transfers between devices, shards(): parts = lax.all_to_all(sums.reshape(128, 16, 128), AXES, 0, 0, tiled=True)  3.03 us
    unnamed x22, local copies, waits for them, and re-layouts  1.71 us
  transfers between devices with their start and end apart: 10, of which 8 were waited for; matrix products, arithmetic and copies ran while one was open for 0% of the time, Pallas kernels for 11%

profile of v5, /device:TPU:1, one launch (start us, length us, event | category | flops | bytes accessed | tf_op | source)
XLA Modules:
  0.0 76.9 jit_solution(6552525796622894963)
XLA Ops:
  0.7 2.8 %first_kernel.1 = (bf16[512,512]{1,0:T(8,128)(2,1)}, bf16[8,64,128]{2,1,0:T(8,128)(2,1)}, bf16[8,64,128]{2,1,0:T(8,128)(2,1)}, bf16[2,64,128]{2,1,0:T(8,128)(2,1)}, bf16[2,64,128]{2,1,0:T(8,128)(2,1)}) custom-call(s32[4,26]{1,0:T(4,128)} %neighbours_any.3, bf16[4,64,512]{2,1,0:T(8,128)(2,1)} %features.1, bf16[4,64,512]{2,1,0:T(8,128)(2,1)} %cotangent_any.1, ...), custom_call_target="tpu_custom_call" | custom-call | flops 4000000000 | tf_op jit(solution)/shard_map/first_kernel/pallas_call | solution.py:521
  3.5 4.6 %collective-permute-start = (bf16[8,64,128]{2,1,0:T(8,128)(2,1)}, bf16[8,64,128]{2,1,0:T(8,128)(2,1)S(1)}, u32[]{:S(2)}, u32[]{:S(2)}) collective-permute-start(bf16[8,64,128]{2,1,0:T(8,128)(2,1)} %get-tuple-element.32), channel_id=1, source_target_pairs={{0,1},{1,2},{2,3},{3,4},{4,5},{5,6},{6,7},{8,9},{9,10},{10,11},{11... | collective-permute-start | bytes 393224 | tf_op jit(solution)/shard_map/ppermute | solution.py:482
  8.1 1.9 %collective-permute-start.1 = (bf16[8,64,128]{2,1,0:T(8,128)(2,1)}, bf16[8,64,128]{2,1,0:T(8,128)(2,1)S(1)}, u32[]{:S(2)}, u32[]{:S(2)}) collective-permute-start(bf16[8,64,128]{2,1,0:T(8,128)(2,1)} %get-tuple-element.37), channel_id=1, source_target_pairs={{1,0},{2,1},{3,2},{4,3},{5,4},{6,5},{7,6},{9,8},{10,9},{11,10},{12... | collective-permute-start | bytes 393224 | tf_op jit(solution)/shard_map/ppermute | solution.py:482
  10.0 0.0 copy-start.7
  10.0 0.0 copy-start.8
  10.1 0.6 copy-done.7
  10.7 0.0 copy-done.8
  10.7 1.0 %copy-done.9 = bf16[512,512]{1,0:T(8,128)(2,1)S(1)} copy-done((bf16[512,512]{1,0:T(8,128)(2,1)S(1)}, bf16[512,512]{1,0:T(8,128)(2,1)}, u32[]{:S(2)}) %copy-start.9) | copy-done | bytes 524312
  11.7 1.0 %prepare_kernel.1 = (bf16[2,24,64,128]{3,2,1,0:T(8,128)(2,1)S(1)}, f32[4,512]{1,0:T(4,128)S(1)}, bf16[192,576]{1,0:T(8,128)(2,1)S(1)}, bf16[192,576]{1,0:T(8,128...) custom-call(bf16[512,512]{1,0:T(8,128)(2,1)S(1)} %copy-done.9, ...), custom_call_target="tpu_custom_call" | custom-call | flops 3000000000 | tf_op jit(solution)/shard_map/prepare_kernel/pallas_call | solution.py:521
  12.8 1.8 %collective-permute-done.1.from_right = bf16[8,64,128]{2,1,0:T(8,128)(2,1)S(1)} collective-permute-done((bf16[8,64,128]{2,1,0:T(8,128)(2,1)}, bf16[8,64,128]{2,1,0:T(8,128)(2,1)S(1)}, u32[]{:S(2)}, u32[]{:S(2)}) %collective-permute-start.1) | collective-permute-done | bytes 131104 | tf_op jit(solution)/shard_map/ppermute | solution.py:482
  14.6 0.0 copy-start.6
  14.6 3.1 %collective-permute-start.2 = (bf16[6,64,128]{2,1,0:T(8,128)(2,1)S(1)}, bf16[6,64,128]{2,1,0:T(8,128)(2,1)S(1)}, u32[]{:S(2)}, u32[]{:S(2)}) collective-permute-start(bf16[6,64,128]{2,1,0:T(8,128)(2,1)S(1)} %get-tuple-element.40), channel_id=1, source_target_pairs={{0,8},{1,9},{2,10},{3,11},{4,12},{5,13},{6,14},{7,15},{8,16},{9,17... | collective-permute-start | bytes 294920 | tf_op jit(solution)/shard_map/ppermute | solution.py:482
  17.8 1.4 %collective-permute-start.3 = (bf16[6,64,128]{2,1,0:T(8,128)(2,1)S(1)}, bf16[6,64,128]{2,1,0:T(8,128)(2,1)S(1)}, u32[]{:S(2)}, u32[]{:S(2)}) collective-permute-start(bf16[6,64,128]{2,1,0:T(8,128)(2,1)S(1)} %get-tuple-element.41), channel_id=1, source_target_pairs={{8,0},{9,1},{10,2},{11,3},{12,4},{13,5},{14,6},{15,7},{16,8},{17,9... | collective-permute-start | bytes 294920 | tf_op jit(solution)/shard_map/ppermute | solution.py:482
  19.2 2.7 %tables_kernel.1 = (s32[104]{0:T(128)S(1)}, s32[288]{0:T(512)S(1)}) custom-call(s32[4,26]{1,0:T(4,128)S(1)} %copy-done.6, bf16[8,64,128]{2,1,0:T(8,128)(2,1)S(1)} %collective-permute-done.after_any.from_left), custom_call_target="tpu_custom_call" | custom-call | flops 3000000000 | tf_op jit(solution)/shard_map/tables_kernel/pallas_call | solution.py:521
  21.9 1.3 %collective-permute-done.3.from_down = bf16[6,64,128]{2,1,0:T(8,128)(2,1)S(1)} collective-permute-done((bf16[6,64,128]{2,1,0:T(8,128)(2,1)S(1)}, bf16[6,64,128]{2,1,0:T(8,128)(2,1)S(1)}, u32[]{:S(2)}, u32[]{:S(2)}) %collective-permute-start.3) | collective-permute-done | bytes 98336 | tf_op jit(solution)/shard_map/ppermute | solution.py:482
  23.3 7.7 %second_kernel.1 = (bf16[256,512]{1,0:T(8,128)(2,1)S(1)}, bf16[2048,128]{1,0:T(8,128)(2,1)}) custom-call(s32[104]{0:T(128)S(1)} %get-tuple-element.33.index_ref, bf16[512,512]{1,0:T(8,128)(2,1)S(1)} %copy-done.10, bf16[2,24,64,128]{3,2,1,0:T(8,128)(2,1)S(1)} %get-tuple-element.36.faces, bf16[8,64,128]{2,1,0:T(8,128)(2,1)S(1)} %collective-permute-done.after_any.from_left, ...), custom_call_target="tpu_custom_call" | custom-call | flops 10000000000 | tf_op jit(solution)/shard_map/second_kernel/pallas_call | solution.py:521
  31.0 10.8 %all-to-all-start = ((bf16[128,16,128]{2,1,0:T(8,128)(2,1)}), bf16[128,16,128]{2,1,0:T(8,128)(2,1)S(1)}, u32[]{:S(2)}, u32[]{:S(2)}) async-start(bf16[128,16,128]{2,1,0:T(8,128)(2,1)} %bitcast.2), calls=%async_computation | async-start | bytes 1048576 | tf_op jit(solution)/shard_map/all_to_all | solution.py:618
  41.8 1.0 %faces_kernel.1 = (bf16[24,64,128]{2,1,0:T(8,128)(2,1)S(1)}, bf16[4,64,128]{2,1,0:T(8,128)(2,1)S(1)}, bf16[4,64,128]{2,1,0:T(8,128)(2,1)S(1)}, bf16[1,64,128]{2,1,0:T(8,128)(2,1)S(1)}, bf16[1,64,128]{2,1,0:T(8,128)(2,1)S(1)}) custom-call(s32[288]{0:T(512)S(1)} %get-tuple-element.34.send_ref, bf16[256,512]{1,0:T(8,128)(2,1)S(1)} %get-tuple-element.50.hidden), custom_call_target="tpu_custom_call" | custom-call | flops 8000000000 | tf_op jit(solution)/shard_map/faces_kernel/pallas_call | solution.py:521
  42.8 3.5 %collective-permute-start.4 = (bf16[4,64,128]{2,1,0:T(8,128)(2,1)S(1)}, bf16[4,64,128]{2,1,0:T(8,128)(2,1)S(1)}, u32[]{:S(2)}, u32[]{:S(2)}) collective-permute-start(bf16[4,64,128]{2,1,0:T(8,128)(2,1)S(1)} %get-tuple-element.52), channel_id=1, source_target_pairs={{0,1},{1,2},{2,3},{3,4},{4,5},{5,6},{6,7},{8,9},{9,10},{10,11},{11... | collective-permute-start | bytes 196616 | tf_op jit(solution)/shard_map/ppermute | solution.py:482
  46.4 1.9 %collective-permute-start.5 = (bf16[4,64,128]{2,1,0:T(8,128)(2,1)S(1)}, bf16[4,64,128]{2,1,0:T(8,128)(2,1)S(1)}, u32[]{:S(2)}, u32[]{:S(2)}) collective-permute-start(bf16[4,64,128]{2,1,0:T(8,128)(2,1)S(1)} %get-tuple-element.53), channel_id=1, source_target_pairs={{1,0},{2,1},{3,2},{4,3},{5,4},{6,5},{7,6},{9,8},{10,9},{11,10},{12... | collective-permute-start | bytes 196616 | tf_op jit(solution)/shard_map/ppermute | solution.py:482
  48.3 0.7 collective-permute-done.4.left_any.from_left
  49.0 3.3 %collective-permute-done.5.right_any.from_right = bf16[4,64,128]{2,1,0:T(8,128)(2,1)S(1)} collective-permute-done((bf16[4,64,128]{2,1,0:T(8,128)(2,1)S(1)}, bf16[4,64,128]{2,1,0:T(8,128)(2,1)S(1)}, u32[]{:S(2)}, u32[]{:S(2)}) %collective-permute-start.5) | collective-permute-done | bytes 65568 | tf_op jit(solution)/shard_map/ppermute | solution.py:482
  52.3 3.0 %all-to-all-done.parts = bf16[128,16,128]{2,1,0:T(8,128)(2,1)S(1)} async-done(((bf16[128,16,128]{2,1,0:T(8,128)(2,1)}), bf16[128,16,128]{2,1,0:T(8,128)(2,1)S(1)}, u32[]{:S(2)}, u32[]{:S(2)}) %all-to-all-start) | async-done | bytes 524320 | tf_op jit(solution)/shard_map/all_to_all | solution.py:618
  55.3 0.9 %share_kernel.1.after_any = bf16[128,16,128]{2,1,0:T(8,128)(2,1)} custom-call(bf16[128,16,128]{2,1,0:T(8,128)(2,1)S(1)} %all-to-all-done.parts, bf16[4,64,128]{2,1,0:T(8,128)(2,1)S(1)} %collective-permute-done.4.left_any.from_left, bf16[4,64,128]{2,1,0:T(8,128)(2,1)S(1)} %collective-permute-done.5.right_any.from_right), custom_call_target="tpu_custom_call" | custom-call | flops 1000000000 | tf_op jit(solution)/shard_map/share_kernel/pallas_call | solution.py:521
  56.2 5.7 %all-to-all-start.1 = ((bf16[128,16,128]{2,1,0:T(8,128)(2,1)}), bf16[128,16,128]{2,1,0:T(8,128)(2,1)S(1)}, u32[]{:S(2)}, u32[]{:S(2)}) async-start(bf16[128,16,128]{2,1,0:T(8,128)(2,1)} %share_kernel.1.after_any), calls=%async_computation.1 | async-start | bytes 1048576 | tf_op jit(solution)/shard_map/all_to_all | solution.py:632
  62.0 3.4 %collective-permute-start.6 = (bf16[3,64,128]{2,1,0:T(8,128)(2,1)S(1)}, bf16[3,64,128]{2,1,0:T(8,128)(2,1)S(1)}, u32[]{:S(2)}, u32[]{:S(2)}) collective-permute-start(bf16[3,64,128]{2,1,0:T(8,128)(2,1)S(1)} %get-tuple-element.57), channel_id=1, source_target_pairs={{0,8},{1,9},{2,10},{3,11},{4,12},{5,13},{6,14},{7,15},{8,16},{9,17... | collective-permute-start | bytes 147464 | tf_op jit(solution)/shard_map/ppermute | solution.py:482
  65.4 1.5 %collective-permute-start.7 = (bf16[3,64,128]{2,1,0:T(8,128)(2,1)S(1)}, bf16[3,64,128]{2,1,0:T(8,128)(2,1)S(1)}, u32[]{:S(2)}, u32[]{:S(2)}) collective-permute-start(bf16[3,64,128]{2,1,0:T(8,128)(2,1)S(1)} %get-tuple-element.58), channel_id=1, source_target_pairs={{8,0},{9,1},{10,2},{11,3},{12,4},{13,5},{14,6},{15,7},{16,8},{17,9... | collective-permute-start | bytes 147464 | tf_op jit(solution)/shard_map/ppermute | solution.py:482
  66.9 0.4 collective-permute-done.6.from_up
  67.3 3.2 %collective-permute-done.7.from_down = bf16[3,64,128]{2,1,0:T(8,128)(2,1)S(1)} collective-permute-done((bf16[3,64,128]{2,1,0:T(8,128)(2,1)S(1)}, bf16[3,64,128]{2,1,0:T(8,128)(2,1)S(1)}, u32[]{:S(2)}, u32[]{:S(2)}) %collective-permute-start.7) | collective-permute-done | bytes 49184 | tf_op jit(solution)/shard_map/ppermute | solution.py:482
  70.5 3.9 %third_kernel.1 = bf16[4,64,512]{2,1,0:T(8,128)(2,1)} custom-call(s32[104]{0:T(128)S(1)} %get-tuple-element.33.index_ref, bf16[24,64,128]{2,1,0:T(8,128)(2,1)S(1)} %get-tuple-element.51.hidden_faces, bf16[4,64,128]{2,1,0:T(8,128)(2,1)S(1)} %collective-permute-done.4.left_any.from_left, bf16[4,64,128]{2,1,0:T(8,128)(2,1)S(1)} %collective-permute-done.5.right_any.from_right, ...), custom_call_target="tpu_custom_call" | custom-call | flops 2000000000 | tf_op jit(solution)/shard_map/third_kernel/pallas_call | solution.py:521
  74.4 1.0 %all-to-all-done.1 = bf16[128,16,128]{2,1,0:T(8,128)(2,1)S(1)} async-done(((bf16[128,16,128]{2,1,0:T(8,128)(2,1)}), bf16[128,16,128]{2,1,0:T(8,128)(2,1)S(1)}, u32[]{:S(2)}, u32[]{:S(2)}) %all-to-all-start.1) | async-done | bytes 524320 | tf_op jit(solution)/shard_map/all_to_all | solution.py:632
  75.4 1.3 %unpack_kernel.1 = (f32[27,64,64]{2,1,0:T(8,128)}, f32[27,64,64]{2,1,0:T(8,128)}) custom-call(bf16[2048,128]{1,0:T(8,128)(2,1)S(1)} %bitcast.4), custom_call_target="tpu_custom_call" | custom-call | tf_op jit(solution)/shard_map/unpack_kernel/pallas_call | solution.py:521
  (20 shorter events, 0.1 us)
Async XLA Ops:
  0.6 9.4 %copy-start.3 = (bf16[27,64,64]{2,1,0:T(8,128)(2,1)S(1)}, bf16[27,64,64]{2,1,0:T(8,128)(2,1)}, u32[]{:S(2)}) copy-start(bf16[27,64,64]{2,1,0:T(8,128)(2,1)} %weight.1) | copy-start | bytes 663556
  0.6 9.4 %copy-start.2 = (bf16[27,64,64]{2,1,0:T(8,128)(2,1)S(1)}, bf16[27,64,64]{2,1,0:T(8,128)(2,1)}, u32[]{:S(2)}) copy-start(bf16[27,64,64]{2,1,0:T(8,128)(2,1)} %first.1) | copy-start | bytes 663556
  3.5 6.6 %copy-start.5 = (s32[4,512]{1,0:T(4,128)S(1)}, s32[4,512]{1,0:T(4,128)}, u32[]{:S(2)}) copy-start(s32[4,512]{1,0:T(4,128)} %active.3) | copy-start | bytes 24580
  3.5 9.3 %collective-permute-start = (bf16[8,64,128]{2,1,0:T(8,128)(2,1)}, bf16[8,64,128]{2,1,0:T(8,128)(2,1)S(1)}, u32[]{:S(2)}, u32[]{:S(2)}) collective-permute-start(bf16[8,64,128]{2,1,0:T(8,128)(2,1)} %get-tuple-element.32), channel_id=1, source_target_pairs={{0,1},{1,2},{2,3},{3,4},{4,5},{5,6},{6,7},{8,9},{9,10},{10,11},{11... | collective-permute-start | bytes 393224 | tf_op jit(solution)/shard_map/ppermute | solution.py:482
  8.1 6.5 %collective-permute-start.1 = (bf16[8,64,128]{2,1,0:T(8,128)(2,1)}, bf16[8,64,128]{2,1,0:T(8,128)(2,1)S(1)}, u32[]{:S(2)}, u32[]{:S(2)}) collective-permute-start(bf16[8,64,128]{2,1,0:T(8,128)(2,1)} %get-tuple-element.37), channel_id=1, source_target_pairs={{1,0},{2,1},{3,2},{4,3},{5,4},{6,5},{7,6},{9,8},{10,9},{11,10},{12... | collective-permute-start | bytes 393224 | tf_op jit(solution)/shard_map/ppermute | solution.py:482
  10.0 0.7 copy-start.7
  10.0 0.7 copy-start.8
  10.7 1.0 %copy-start.9 = (bf16[512,512]{1,0:T(8,128)(2,1)S(1)}, bf16[512,512]{1,0:T(8,128)(2,1)}, u32[]{:S(2)}) copy-start(bf16[512,512]{1,0:T(8,128)(2,1)} %get-tuple-element.35.values) | copy-start | bytes 1572868
  11.7 2.9 %copy-start = (bf16[2,64,128]{2,1,0:T(8,128)(2,1)S(1)}, bf16[2,64,128]{2,1,0:T(8,128)(2,1)}, u32[]{:S(2)}) copy-start(bf16[2,64,128]{2,1,0:T(8,128)(2,1)} %get-tuple-element.38.up.after_any) | copy-start | bytes 98308
  11.7 2.9 %copy-start.1 = (bf16[2,64,128]{2,1,0:T(8,128)(2,1)S(1)}, bf16[2,64,128]{2,1,0:T(8,128)(2,1)}, u32[]{:S(2)}) copy-start(bf16[2,64,128]{2,1,0:T(8,128)(2,1)} %get-tuple-element.39.down) | copy-start | bytes 98308
  14.6 4.6 %copy-start.6 = (s32[4,26]{1,0:T(4,128)S(1)}, s32[4,26]{1,0:T(4,128)}, u32[]{:S(2)}) copy-start(s32[4,26]{1,0:T(4,128)} %neighbours_any.3) | copy-start | bytes 1252
  14.6 7.3 %collective-permute-start.2 = (bf16[6,64,128]{2,1,0:T(8,128)(2,1)S(1)}, bf16[6,64,128]{2,1,0:T(8,128)(2,1)S(1)}, u32[]{:S(2)}, u32[]{:S(2)}) collective-permute-start(bf16[6,64,128]{2,1,0:T(8,128)(2,1)S(1)} %get-tuple-element.40), channel_id=1, source_target_pairs={{0,8},{1,9},{2,10},{3,11},{4,12},{5,13},{6,14},{7,15},{8,16},{9,17... | collective-permute-start | bytes 294920 | tf_op jit(solution)/shard_map/ppermute | solution.py:482
  17.7 5.5 %copy-start.10 = (bf16[512,512]{1,0:T(8,128)(2,1)S(1)}, bf16[512,512]{1,0:T(8,128)(2,1)}, u32[]{:S(2)}) copy-start(bf16[512,512]{1,0:T(8,128)(2,1)} %get-tuple-element.35.values) | copy-start | bytes 1572868
  17.8 5.5 %collective-permute-start.3 = (bf16[6,64,128]{2,1,0:T(8,128)(2,1)S(1)}, bf16[6,64,128]{2,1,0:T(8,128)(2,1)S(1)}, u32[]{:S(2)}, u32[]{:S(2)}) collective-permute-start(bf16[6,64,128]{2,1,0:T(8,128)(2,1)S(1)} %get-tuple-element.41), channel_id=1, source_target_pairs={{8,0},{9,1},{10,2},{11,3},{12,4},{13,5},{14,6},{15,7},{16,8},{17,9... | collective-permute-start | bytes 294920 | tf_op jit(solution)/shard_map/ppermute | solution.py:482
  31.0 24.3 %all-to-all-start = ((bf16[128,16,128]{2,1,0:T(8,128)(2,1)}), bf16[128,16,128]{2,1,0:T(8,128)(2,1)S(1)}, u32[]{:S(2)}, u32[]{:S(2)}) async-start(bf16[128,16,128]{2,1,0:T(8,128)(2,1)} %bitcast.2), calls=%async_computation | async-start | bytes 1048576 | tf_op jit(solution)/shard_map/all_to_all | solution.py:618
  42.8 6.2 %collective-permute-start.4 = (bf16[4,64,128]{2,1,0:T(8,128)(2,1)S(1)}, bf16[4,64,128]{2,1,0:T(8,128)(2,1)S(1)}, u32[]{:S(2)}, u32[]{:S(2)}) collective-permute-start(bf16[4,64,128]{2,1,0:T(8,128)(2,1)S(1)} %get-tuple-element.52), channel_id=1, source_target_pairs={{0,1},{1,2},{2,3},{3,4},{4,5},{5,6},{6,7},{8,9},{9,10},{10,11},{11... | collective-permute-start | bytes 196616 | tf_op jit(solution)/shard_map/ppermute | solution.py:482
  46.4 5.9 %collective-permute-start.5 = (bf16[4,64,128]{2,1,0:T(8,128)(2,1)S(1)}, bf16[4,64,128]{2,1,0:T(8,128)(2,1)S(1)}, u32[]{:S(2)}, u32[]{:S(2)}) collective-permute-start(bf16[4,64,128]{2,1,0:T(8,128)(2,1)S(1)} %get-tuple-element.53), channel_id=1, source_target_pairs={{1,0},{2,1},{3,2},{4,3},{5,4},{6,5},{7,6},{9,8},{10,9},{11,10},{12... | collective-permute-start | bytes 196616 | tf_op jit(solution)/shard_map/ppermute | solution.py:482
  56.2 19.2 %all-to-all-start.1 = ((bf16[128,16,128]{2,1,0:T(8,128)(2,1)}), bf16[128,16,128]{2,1,0:T(8,128)(2,1)S(1)}, u32[]{:S(2)}, u32[]{:S(2)}) async-start(bf16[128,16,128]{2,1,0:T(8,128)(2,1)} %share_kernel.1.after_any), calls=%async_computation.1 | async-start | bytes 1048576 | tf_op jit(solution)/shard_map/all_to_all | solution.py:632
  61.9 8.6 %copy-start.4 = (bf16[4,64,512]{2,1,0:T(8,128)(2,1)S(1)}, bf16[4,64,512]{2,1,0:T(8,128)(2,1)}, u32[]{:S(2)}) copy-start(bf16[4,64,512]{2,1,0:T(8,128)(2,1)} %features.1) | copy-start | bytes 786436
  62.0 5.3 %collective-permute-start.6 = (bf16[3,64,128]{2,1,0:T(8,128)(2,1)S(1)}, bf16[3,64,128]{2,1,0:T(8,128)(2,1)S(1)}, u32[]{:S(2)}, u32[]{:S(2)}) collective-permute-start(bf16[3,64,128]{2,1,0:T(8,128)(2,1)S(1)} %get-tuple-element.57), channel_id=1, source_target_pairs={{0,8},{1,9},{2,10},{3,11},{4,12},{5,13},{6,14},{7,15},{8,16},{9,17... | collective-permute-start | bytes 147464 | tf_op jit(solution)/shard_map/ppermute | solution.py:482
  65.4 5.1 %collective-permute-start.7 = (bf16[3,64,128]{2,1,0:T(8,128)(2,1)S(1)}, bf16[3,64,128]{2,1,0:T(8,128)(2,1)S(1)}, u32[]{:S(2)}, u32[]{:S(2)}) collective-permute-start(bf16[3,64,128]{2,1,0:T(8,128)(2,1)S(1)} %get-tuple-element.58), channel_id=1, source_target_pairs={{8,0},{9,1},{10,2},{11,3},{12,4},{13,5},{14,6},{15,7},{16,8},{17,9... | collective-permute-start | bytes 147464 | tf_op jit(solution)/shard_map/ppermute | solution.py:482

commit v6 on v5

--- a/solution.py
+++ b/solution.py
@@ -191,8 +191,8 @@
             ref[t] = tile
 
 
-def own_faces(values, faces_ref):
-    faces = dot(values[...], face_matrix()).astype(BF)
+def own_faces(values, matrix, faces_ref):
+    faces = dot(values[...], matrix).astype(BF)
     for a in range(2):
         for b in range(4):
             for f in range(6):
@@ -203,7 +203,7 @@
 def first_kernel(
     neighbours_any, features_any, cotangent_any, active_any,
     values_ref, right_ref, left_ref, up_ref, down_ref,
-    faces_ref, neighbours, features, cotangent, active, send_ref, sems,
+    faces_ref, face_mat, neighbours, features, cotangent, active, send_ref, sems,
 ):
     pairs = (
         (neighbours_any, neighbours), (features_any, features), (cotangent_any, cotangent),
@@ -212,6 +212,7 @@
     copies = [pltpu.make_async_copy(s, d, sems.at[t]) for t, (s, d) in enumerate(pairs)]
     for copy in copies:
         copy.start()
+    face_mat[...] = face_matrix()
     for copy in copies:
         copy.wait()
     choose_sends(neighbours, send_ref)
@@ -220,7 +221,7 @@
         f = features[b].astype(F32)
         values_ref[b * 64 : b * 64 + 64, :] = (mask * (f / (1.0 + jnp.exp(-f)))).astype(BF)
         values_ref[256 + b * 64 : 320 + b * 64, :] = (mask * cotangent[b].astype(F32)).astype(BF)
-    own_faces(values_ref, faces_ref)
+    own_faces(values_ref, face_mat[...], faces_ref)
     low = low_half((64, 128))
     pack(
         send_ref,
@@ -240,7 +241,7 @@
     values, active, first, second, scale, shift,
     faces_ref, mask_ref, w_first, w_back, gain_ref, shift_ref, e_yz, e_x, windows,
 ):
-    own_faces(values, faces_ref)
+    own_faces(values, face_matrix(), faces_ref)
     mask_ref[...] = active[...].astype(F32)
     e_yz[...], e_x[...], windows[...] = yz_matrix(), x_matrix(), window_matrix()
     gain_ref[...] = 1.0 + as_column(scale[...])
@@ -543,6 +544,7 @@
         [(VMEM, shape((512, 512)))] + messages(2),
         [
             pltpu.VMEM((2, 24, 64, 128), BF),
+            pltpu.VMEM((512, 768), BF),
             pltpu.SMEM((4, 26), jnp.int32),
             pltpu.VMEM((4, 64, 512), BF),
             pltpu.VMEM((4, 64, 512), BF),

time: 77.5 us -> 77.5 us (level)
  no operation moved by 1% of the time
where the time goes in v6:
time: 77.5 us; the launch traced here: 76.9 us
  starting transfers between devices  37.8 us (49%)
  Pallas kernels  21.4 us (28%)
  waiting for transfers between devices  15 us (19%)
  local copies, waits for them, and re-layouts  1.71 us (2%)
  between operations  1.04 us (1%)
    pallas_call x10, Pallas kernels, call(): pl.pallas_call(kernel, out_shape=tuple((o for _, o in outs)), in_specs=[s...  21.4 us
    ppermute x8, starting transfers between devices, sent(): return lax.ppermute(array, 'brick', pairs)  21.2 us
    ppermute x8, waiting for transfers between devices, sent(): return lax.ppermute(array, 'brick', pairs)  10.9 us
    all_to_all x1, starting transfers between devices, shards(): parts = lax.all_to_all(sums.reshape(128, 16, 128), AXES, 0, 0, tiled=True)  10.8 us
    all_to_all x1, starting transfers between devices, shards(): sums = lax.all_to_all(shares, AXES, 0, 0, tiled=True)  5.73 us
    all_to_all x1, waiting for transfers between devices, shards(): parts = lax.all_to_all(sums.reshape(128, 16, 128), AXES, 0, 0, tiled=True)  3.03 us
    unnamed x22, local copies, waits for them, and re-layouts  1.71 us
  transfers between devices with their start and end apart: 10, of which 8 were waited for; matrix products, arithmetic and copies ran while one was open for 0% of the time, Pallas kernels for 11%

profile of v6, /device:TPU:1, one launch (start us, length us, event | category | flops | bytes accessed | tf_op | source)
XLA Modules:
  0.0 76.9 jit_solution(16958266772864739909)
XLA Ops:
  0.7 2.8 %first_kernel.1 = (bf16[512,512]{1,0:T(8,128)(2,1)}, bf16[8,64,128]{2,1,0:T(8,128)(2,1)}, bf16[8,64,128]{2,1,0:T(8,128)(2,1)}, bf16[2,64,128]{2,1,0:T(8,128)(2,1)}, bf16[2,64,128]{2,1,0:T(8,128)(2,1)}) custom-call(s32[4,26]{1,0:T(4,128)} %neighbours_any.3, bf16[4,64,512]{2,1,0:T(8,128)(2,1)} %features.1, bf16[4,64,512]{2,1,0:T(8,128)(2,1)} %cotangent_any.1, ...), custom_call_target="tpu_custom_call" | custom-call | flops 4000000000 | tf_op jit(solution)/shard_map/first_kernel/pallas_call | solution.py:522
  3.5 0.0 copy-start.5
  3.5 4.6 %collective-permute-start = (bf16[8,64,128]{2,1,0:T(8,128)(2,1)}, bf16[8,64,128]{2,1,0:T(8,128)(2,1)S(1)}, u32[]{:S(2)}, u32[]{:S(2)}) collective-permute-start(bf16[8,64,128]{2,1,0:T(8,128)(2,1)} %get-tuple-element.32), channel_id=1, source_target_pairs={{0,1},{1,2},{2,3},{3,4},{4,5},{5,6},{6,7},{8,9},{9,10},{10,11},{11... | collective-permute-start | bytes 393224 | tf_op jit(solution)/shard_map/ppermute | solution.py:483
  8.1 1.9 %collective-permute-start.1 = (bf16[8,64,128]{2,1,0:T(8,128)(2,1)}, bf16[8,64,128]{2,1,0:T(8,128)(2,1)S(1)}, u32[]{:S(2)}, u32[]{:S(2)}) collective-permute-start(bf16[8,64,128]{2,1,0:T(8,128)(2,1)} %get-tuple-element.37), channel_id=1, source_target_pairs={{1,0},{2,1},{3,2},{4,3},{5,4},{6,5},{7,6},{9,8},{10,9},{11,10},{12... | collective-permute-start | bytes 393224 | tf_op jit(solution)/shard_map/ppermute | solution.py:483
  10.0 0.0 copy-start.7
  10.1 0.6 copy-done.7
  10.7 0.0 copy-done.8
  10.7 1.0 %copy-done.9 = bf16[512,512]{1,0:T(8,128)(2,1)S(1)} copy-done((bf16[512,512]{1,0:T(8,128)(2,1)S(1)}, bf16[512,512]{1,0:T(8,128)(2,1)}, u32[]{:S(2)}) %copy-start.9) | copy-done | bytes 524312
  11.7 1.0 %prepare_kernel.1 = (bf16[2,24,64,128]{3,2,1,0:T(8,128)(2,1)S(1)}, f32[4,512]{1,0:T(4,128)S(1)}, bf16[192,576]{1,0:T(8,128)(2,1)S(1)}, bf16[192,576]{1,0:T(8,128...) custom-call(bf16[512,512]{1,0:T(8,128)(2,1)S(1)} %copy-done.9, ...), custom_call_target="tpu_custom_call" | custom-call | flops 3000000000 | tf_op jit(solution)/shard_map/prepare_kernel/pallas_call | solution.py:522
  12.8 1.8 %collective-permute-done.1.from_right = bf16[8,64,128]{2,1,0:T(8,128)(2,1)S(1)} collective-permute-done((bf16[8,64,128]{2,1,0:T(8,128)(2,1)}, bf16[8,64,128]{2,1,0:T(8,128)(2,1)S(1)}, u32[]{:S(2)}, u32[]{:S(2)}) %collective-permute-start.1) | collective-permute-done | bytes 131104 | tf_op jit(solution)/shard_map/ppermute | solution.py:483
  14.6 0.0 copy-start.6
  14.6 3.1 %collective-permute-start.2 = (bf16[6,64,128]{2,1,0:T(8,128)(2,1)S(1)}, bf16[6,64,128]{2,1,0:T(8,128)(2,1)S(1)}, u32[]{:S(2)}, u32[]{:S(2)}) collective-permute-start(bf16[6,64,128]{2,1,0:T(8,128)(2,1)S(1)} %get-tuple-element.40), channel_id=1, source_target_pairs={{0,8},{1,9},{2,10},{3,11},{4,12},{5,13},{6,14},{7,15},{8,16},{9,17... | collective-permute-start | bytes 294920 | tf_op jit(solution)/shard_map/ppermute | solution.py:483
  17.8 1.4 %collective-permute-start.3 = (bf16[6,64,128]{2,1,0:T(8,128)(2,1)S(1)}, bf16[6,64,128]{2,1,0:T(8,128)(2,1)S(1)}, u32[]{:S(2)}, u32[]{:S(2)}) collective-permute-start(bf16[6,64,128]{2,1,0:T(8,128)(2,1)S(1)} %get-tuple-element.41), channel_id=1, source_target_pairs={{8,0},{9,1},{10,2},{11,3},{12,4},{13,5},{14,6},{15,7},{16,8},{17,9... | collective-permute-start | bytes 294920 | tf_op jit(solution)/shard_map/ppermute | solution.py:483
  19.2 2.7 %tables_kernel.1 = (s32[104]{0:T(128)S(1)}, s32[288]{0:T(512)S(1)}) custom-call(s32[4,26]{1,0:T(4,128)S(1)} %copy-done.6, bf16[8,64,128]{2,1,0:T(8,128)(2,1)S(1)} %collective-permute-done.after_any.from_left), custom_call_target="tpu_custom_call" | custom-call | flops 3000000000 | tf_op jit(solution)/shard_map/tables_kernel/pallas_call | solution.py:522
  22.0 1.3 %collective-permute-done.3.from_down = bf16[6,64,128]{2,1,0:T(8,128)(2,1)S(1)} collective-permute-done((bf16[6,64,128]{2,1,0:T(8,128)(2,1)S(1)}, bf16[6,64,128]{2,1,0:T(8,128)(2,1)S(1)}, u32[]{:S(2)}, u32[]{:S(2)}) %collective-permute-start.3) | collective-permute-done | bytes 98336 | tf_op jit(solution)/shard_map/ppermute | solution.py:483
  23.3 7.7 %second_kernel.1 = (bf16[256,512]{1,0:T(8,128)(2,1)S(1)}, bf16[2048,128]{1,0:T(8,128)(2,1)}) custom-call(s32[104]{0:T(128)S(1)} %get-tuple-element.33.index_ref, bf16[512,512]{1,0:T(8,128)(2,1)S(1)} %copy-done.10, bf16[2,24,64,128]{3,2,1,0:T(8,128)(2,1)S(1)} %get-tuple-element.36.faces, bf16[8,64,128]{2,1,0:T(8,128)(2,1)S(1)} %collective-permute-done.after_any.from_left, ...), custom_call_target="tpu_custom_call" | custom-call | flops 10000000000 | tf_op jit(solution)/shard_map/second_kernel/pallas_call | solution.py:522
  31.0 10.8 %all-to-all-start = ((bf16[128,16,128]{2,1,0:T(8,128)(2,1)}), bf16[128,16,128]{2,1,0:T(8,128)(2,1)S(1)}, u32[]{:S(2)}, u32[]{:S(2)}) async-start(bf16[128,16,128]{2,1,0:T(8,128)(2,1)} %bitcast.2), calls=%async_computation | async-start | bytes 1048576 | tf_op jit(solution)/shard_map/all_to_all | solution.py:620
  41.8 1.0 %faces_kernel.1 = (bf16[24,64,128]{2,1,0:T(8,128)(2,1)S(1)}, bf16[4,64,128]{2,1,0:T(8,128)(2,1)S(1)}, bf16[4,64,128]{2,1,0:T(8,128)(2,1)S(1)}, bf16[1,64,128]{2,1,0:T(8,128)(2,1)S(1)}, bf16[1,64,128]{2,1,0:T(8,128)(2,1)S(1)}) custom-call(s32[288]{0:T(512)S(1)} %get-tuple-element.34.send_ref, bf16[256,512]{1,0:T(8,128)(2,1)S(1)} %get-tuple-element.50.hidden), custom_call_target="tpu_custom_call" | custom-call | flops 8000000000 | tf_op jit(solution)/shard_map/faces_kernel/pallas_call | solution.py:522
  42.8 3.5 %collective-permute-start.4 = (bf16[4,64,128]{2,1,0:T(8,128)(2,1)S(1)}, bf16[4,64,128]{2,1,0:T(8,128)(2,1)S(1)}, u32[]{:S(2)}, u32[]{:S(2)}) collective-permute-start(bf16[4,64,128]{2,1,0:T(8,128)(2,1)S(1)} %get-tuple-element.52), channel_id=1, source_target_pairs={{0,1},{1,2},{2,3},{3,4},{4,5},{5,6},{6,7},{8,9},{9,10},{10,11},{11... | collective-permute-start | bytes 196616 | tf_op jit(solution)/shard_map/ppermute | solution.py:483
  46.4 1.9 %collective-permute-start.5 = (bf16[4,64,128]{2,1,0:T(8,128)(2,1)S(1)}, bf16[4,64,128]{2,1,0:T(8,128)(2,1)S(1)}, u32[]{:S(2)}, u32[]{:S(2)}) collective-permute-start(bf16[4,64,128]{2,1,0:T(8,128)(2,1)S(1)} %get-tuple-element.53), channel_id=1, source_target_pairs={{1,0},{2,1},{3,2},{4,3},{5,4},{6,5},{7,6},{9,8},{10,9},{11,10},{12... | collective-permute-start | bytes 196616 | tf_op jit(solution)/shard_map/ppermute | solution.py:483
  48.3 0.7 collective-permute-done.4.left_any.from_left
  49.0 3.3 %collective-permute-done.5.right_any.from_right = bf16[4,64,128]{2,1,0:T(8,128)(2,1)S(1)} collective-permute-done((bf16[4,64,128]{2,1,0:T(8,128)(2,1)S(1)}, bf16[4,64,128]{2,1,0:T(8,128)(2,1)S(1)}, u32[]{:S(2)}, u32[]{:S(2)}) %collective-permute-start.5) | collective-permute-done | bytes 65568 | tf_op jit(solution)/shard_map/ppermute | solution.py:483
  52.3 3.0 %all-to-all-done.parts = bf16[128,16,128]{2,1,0:T(8,128)(2,1)S(1)} async-done(((bf16[128,16,128]{2,1,0:T(8,128)(2,1)}), bf16[128,16,128]{2,1,0:T(8,128)(2,1)S(1)}, u32[]{:S(2)}, u32[]{:S(2)}) %all-to-all-start) | async-done | bytes 524320 | tf_op jit(solution)/shard_map/all_to_all | solution.py:620
  55.3 0.9 %share_kernel.1.after_any = bf16[128,16,128]{2,1,0:T(8,128)(2,1)} custom-call(bf16[128,16,128]{2,1,0:T(8,128)(2,1)S(1)} %all-to-all-done.parts, bf16[4,64,128]{2,1,0:T(8,128)(2,1)S(1)} %collective-permute-done.4.left_any.from_left, bf16[4,64,128]{2,1,0:T(8,128)(2,1)S(1)} %collective-permute-done.5.right_any.from_right), custom_call_target="tpu_custom_call" | custom-call | flops 1000000000 | tf_op jit(solution)/shard_map/share_kernel/pallas_call | solution.py:522
  56.2 5.7 %all-to-all-start.1 = ((bf16[128,16,128]{2,1,0:T(8,128)(2,1)}), bf16[128,16,128]{2,1,0:T(8,128)(2,1)S(1)}, u32[]{:S(2)}, u32[]{:S(2)}) async-start(bf16[128,16,128]{2,1,0:T(8,128)(2,1)} %share_kernel.1.after_any), calls=%async_computation.1 | async-start | bytes 1048576 | tf_op jit(solution)/shard_map/all_to_all | solution.py:634
  62.0 3.4 %collective-permute-start.6 = (bf16[3,64,128]{2,1,0:T(8,128)(2,1)S(1)}, bf16[3,64,128]{2,1,0:T(8,128)(2,1)S(1)}, u32[]{:S(2)}, u32[]{:S(2)}) collective-permute-start(bf16[3,64,128]{2,1,0:T(8,128)(2,1)S(1)} %get-tuple-element.57), channel_id=1, source_target_pairs={{0,8},{1,9},{2,10},{3,11},{4,12},{5,13},{6,14},{7,15},{8,16},{9,17... | collective-permute-start | bytes 147464 | tf_op jit(solution)/shard_map/ppermute | solution.py:483
  65.4 1.3 %collective-permute-start.7 = (bf16[3,64,128]{2,1,0:T(8,128)(2,1)S(1)}, bf16[3,64,128]{2,1,0:T(8,128)(2,1)S(1)}, u32[]{:S(2)}, u32[]{:S(2)}) collective-permute-start(bf16[3,64,128]{2,1,0:T(8,128)(2,1)S(1)} %get-tuple-element.58), channel_id=1, source_target_pairs={{8,0},{9,1},{10,2},{11,3},{12,4},{13,5},{14,6},{15,7},{16,8},{17,9... | collective-permute-start | bytes 147464 | tf_op jit(solution)/shard_map/ppermute | solution.py:483
  66.7 0.6 collective-permute-done.6.from_up
  67.3 3.2 %collective-permute-done.7.from_down = bf16[3,64,128]{2,1,0:T(8,128)(2,1)S(1)} collective-permute-done((bf16[3,64,128]{2,1,0:T(8,128)(2,1)S(1)}, bf16[3,64,128]{2,1,0:T(8,128)(2,1)S(1)}, u32[]{:S(2)}, u32[]{:S(2)}) %collective-permute-start.7) | collective-permute-done | bytes 49184 | tf_op jit(solution)/shard_map/ppermute | solution.py:483
  70.5 3.9 %third_kernel.1 = bf16[4,64,512]{2,1,0:T(8,128)(2,1)} custom-call(s32[104]{0:T(128)S(1)} %get-tuple-element.33.index_ref, bf16[24,64,128]{2,1,0:T(8,128)(2,1)S(1)} %get-tuple-element.51.hidden_faces, bf16[4,64,128]{2,1,0:T(8,128)(2,1)S(1)} %collective-permute-done.4.left_any.from_left, bf16[4,64,128]{2,1,0:T(8,128)(2,1)S(1)} %collective-permute-done.5.right_any.from_right, ...), custom_call_target="tpu_custom_call" | custom-call | flops 2000000000 | tf_op jit(solution)/shard_map/third_kernel/pallas_call | solution.py:522
  74.4 1.0 %all-to-all-done.1 = bf16[128,16,128]{2,1,0:T(8,128)(2,1)S(1)} async-done(((bf16[128,16,128]{2,1,0:T(8,128)(2,1)}), bf16[128,16,128]{2,1,0:T(8,128)(2,1)S(1)}, u32[]{:S(2)}, u32[]{:S(2)}) %all-to-all-start.1) | async-done | bytes 524320 | tf_op jit(solution)/shard_map/all_to_all | solution.py:634
  75.5 1.3 %unpack_kernel.1 = (f32[27,64,64]{2,1,0:T(8,128)}, f32[27,64,64]{2,1,0:T(8,128)}) custom-call(bf16[2048,128]{1,0:T(8,128)(2,1)S(1)} %bitcast.4), custom_call_target="tpu_custom_call" | custom-call | tf_op jit(solution)/shard_map/unpack_kernel/pallas_call | solution.py:522
  (20 shorter events, 0.1 us)
Async XLA Ops:
  0.6 9.4 %copy-start.3 = (bf16[27,64,64]{2,1,0:T(8,128)(2,1)S(1)}, bf16[27,64,64]{2,1,0:T(8,128)(2,1)}, u32[]{:S(2)}) copy-start(bf16[27,64,64]{2,1,0:T(8,128)(2,1)} %weight.1) | copy-start | bytes 663556
  0.6 9.4 %copy-start.2 = (bf16[27,64,64]{2,1,0:T(8,128)(2,1)S(1)}, bf16[27,64,64]{2,1,0:T(8,128)(2,1)}, u32[]{:S(2)}) copy-start(bf16[27,64,64]{2,1,0:T(8,128)(2,1)} %first.1) | copy-start | bytes 663556
  3.5 6.6 %copy-start.5 = (s32[4,512]{1,0:T(4,128)S(1)}, s32[4,512]{1,0:T(4,128)}, u32[]{:S(2)}) copy-start(s32[4,512]{1,0:T(4,128)} %active.3) | copy-start | bytes 24580
  3.5 9.3 %collective-permute-start = (bf16[8,64,128]{2,1,0:T(8,128)(2,1)}, bf16[8,64,128]{2,1,0:T(8,128)(2,1)S(1)}, u32[]{:S(2)}, u32[]{:S(2)}) collective-permute-start(bf16[8,64,128]{2,1,0:T(8,128)(2,1)} %get-tuple-element.32), channel_id=1, source_target_pairs={{0,1},{1,2},{2,3},{3,4},{4,5},{5,6},{6,7},{8,9},{9,10},{10,11},{11... | collective-permute-start | bytes 393224 | tf_op jit(solution)/shard_map/ppermute | solution.py:483
  8.1 6.5 %collective-permute-start.1 = (bf16[8,64,128]{2,1,0:T(8,128)(2,1)}, bf16[8,64,128]{2,1,0:T(8,128)(2,1)S(1)}, u32[]{:S(2)}, u32[]{:S(2)}) collective-permute-start(bf16[8,64,128]{2,1,0:T(8,128)(2,1)} %get-tuple-element.37), channel_id=1, source_target_pairs={{1,0},{2,1},{3,2},{4,3},{5,4},{6,5},{7,6},{9,8},{10,9},{11,10},{12... | collective-permute-start | bytes 393224 | tf_op jit(solution)/shard_map/ppermute | solution.py:483
  10.0 0.7 copy-start.7
  10.0 0.7 copy-start.8
  10.7 1.0 %copy-start.9 = (bf16[512,512]{1,0:T(8,128)(2,1)S(1)}, bf16[512,512]{1,0:T(8,128)(2,1)}, u32[]{:S(2)}) copy-start(bf16[512,512]{1,0:T(8,128)(2,1)} %get-tuple-element.35.values) | copy-start | bytes 1572868
  11.7 2.9 %copy-start = (bf16[2,64,128]{2,1,0:T(8,128)(2,1)S(1)}, bf16[2,64,128]{2,1,0:T(8,128)(2,1)}, u32[]{:S(2)}) copy-start(bf16[2,64,128]{2,1,0:T(8,128)(2,1)} %get-tuple-element.38.up.after_any) | copy-start | bytes 98308
  11.7 2.9 %copy-start.1 = (bf16[2,64,128]{2,1,0:T(8,128)(2,1)S(1)}, bf16[2,64,128]{2,1,0:T(8,128)(2,1)}, u32[]{:S(2)}) copy-start(bf16[2,64,128]{2,1,0:T(8,128)(2,1)} %get-tuple-element.39.down) | copy-start | bytes 98308
  14.6 4.6 %copy-start.6 = (s32[4,26]{1,0:T(4,128)S(1)}, s32[4,26]{1,0:T(4,128)}, u32[]{:S(2)}) copy-start(s32[4,26]{1,0:T(4,128)} %neighbours_any.3) | copy-start | bytes 1252
  14.6 7.3 %collective-permute-start.2 = (bf16[6,64,128]{2,1,0:T(8,128)(2,1)S(1)}, bf16[6,64,128]{2,1,0:T(8,128)(2,1)S(1)}, u32[]{:S(2)}, u32[]{:S(2)}) collective-permute-start(bf16[6,64,128]{2,1,0:T(8,128)(2,1)S(1)} %get-tuple-element.40), channel_id=1, source_target_pairs={{0,8},{1,9},{2,10},{3,11},{4,12},{5,13},{6,14},{7,15},{8,16},{9,17... | collective-permute-start | bytes 294920 | tf_op jit(solution)/shard_map/ppermute | solution.py:483
  17.8 5.5 %copy-start.10 = (bf16[512,512]{1,0:T(8,128)(2,1)S(1)}, bf16[512,512]{1,0:T(8,128)(2,1)}, u32[]{:S(2)}) copy-start(bf16[512,512]{1,0:T(8,128)(2,1)} %get-tuple-element.35.values) | copy-start | bytes 1572868
  17.8 5.5 %collective-permute-start.3 = (bf16[6,64,128]{2,1,0:T(8,128)(2,1)S(1)}, bf16[6,64,128]{2,1,0:T(8,128)(2,1)S(1)}, u32[]{:S(2)}, u32[]{:S(2)}) collective-permute-start(bf16[6,64,128]{2,1,0:T(8,128)(2,1)S(1)} %get-tuple-element.41), channel_id=1, source_target_pairs={{8,0},{9,1},{10,2},{11,3},{12,4},{13,5},{14,6},{15,7},{16,8},{17,9... | collective-permute-start | bytes 294920 | tf_op jit(solution)/shard_map/ppermute | solution.py:483
  31.0 24.3 %all-to-all-start = ((bf16[128,16,128]{2,1,0:T(8,128)(2,1)}), bf16[128,16,128]{2,1,0:T(8,128)(2,1)S(1)}, u32[]{:S(2)}, u32[]{:S(2)}) async-start(bf16[128,16,128]{2,1,0:T(8,128)(2,1)} %bitcast.2), calls=%async_computation | async-start | bytes 1048576 | tf_op jit(solution)/shard_map/all_to_all | solution.py:620
  42.8 6.2 %collective-permute-start.4 = (bf16[4,64,128]{2,1,0:T(8,128)(2,1)S(1)}, bf16[4,64,128]{2,1,0:T(8,128)(2,1)S(1)}, u32[]{:S(2)}, u32[]{:S(2)}) collective-permute-start(bf16[4,64,128]{2,1,0:T(8,128)(2,1)S(1)} %get-tuple-element.52), channel_id=1, source_target_pairs={{0,1},{1,2},{2,3},{3,4},{4,5},{5,6},{6,7},{8,9},{9,10},{10,11},{11... | collective-permute-start | bytes 196616 | tf_op jit(solution)/shard_map/ppermute | solution.py:483
  46.4 5.9 %collective-permute-start.5 = (bf16[4,64,128]{2,1,0:T(8,128)(2,1)S(1)}, bf16[4,64,128]{2,1,0:T(8,128)(2,1)S(1)}, u32[]{:S(2)}, u32[]{:S(2)}) collective-permute-start(bf16[4,64,128]{2,1,0:T(8,128)(2,1)S(1)} %get-tuple-element.53), channel_id=1, source_target_pairs={{1,0},{2,1},{3,2},{4,3},{5,4},{6,5},{7,6},{9,8},{10,9},{11,10},{12... | collective-permute-start | bytes 196616 | tf_op jit(solution)/shard_map/ppermute | solution.py:483
  56.2 19.2 %all-to-all-start.1 = ((bf16[128,16,128]{2,1,0:T(8,128)(2,1)}), bf16[128,16,128]{2,1,0:T(8,128)(2,1)S(1)}, u32[]{:S(2)}, u32[]{:S(2)}) async-start(bf16[128,16,128]{2,1,0:T(8,128)(2,1)} %share_kernel.1.after_any), calls=%async_computation.1 | async-start | bytes 1048576 | tf_op jit(solution)/shard_map/all_to_all | solution.py:634
  61.9 8.6 %copy-start.4 = (bf16[4,64,512]{2,1,0:T(8,128)(2,1)S(1)}, bf16[4,64,512]{2,1,0:T(8,128)(2,1)}, u32[]{:S(2)}) copy-start(bf16[4,64,512]{2,1,0:T(8,128)(2,1)} %features.1) | copy-start | bytes 786436
  62.0 5.3 %collective-permute-start.6 = (bf16[3,64,128]{2,1,0:T(8,128)(2,1)S(1)}, bf16[3,64,128]{2,1,0:T(8,128)(2,1)S(1)}, u32[]{:S(2)}, u32[]{:S(2)}) collective-permute-start(bf16[3,64,128]{2,1,0:T(8,128)(2,1)S(1)} %get-tuple-element.57), channel_id=1, source_target_pairs={{0,8},{1,9},{2,10},{3,11},{4,12},{5,13},{6,14},{7,15},{8,16},{9,17... | collective-permute-start | bytes 147464 | tf_op jit(solution)/shard_map/ppermute | solution.py:483
  65.4 5.1 %collective-permute-start.7 = (bf16[3,64,128]{2,1,0:T(8,128)(2,1)S(1)}, bf16[3,64,128]{2,1,0:T(8,128)(2,1)S(1)}, u32[]{:S(2)}, u32[]{:S(2)}) collective-permute-start(bf16[3,64,128]{2,1,0:T(8,128)(2,1)S(1)} %get-tuple-element.58), channel_id=1, source_target_pairs={{8,0},{9,1},{10,2},{11,3},{12,4},{13,5},{14,6},{15,7},{16,8},{17,9... | collective-permute-start | bytes 147464 | tf_op jit(solution)/shard_map/ppermute | solution.py:483

commit v7 on v6

--- a/solution.py
+++ b/solution.py
@@ -465,11 +465,14 @@
                     grad[26 - k] = block
                 else:
                     grad[k] = block.T
-            nine = pl.ds(18 - 9 * i if t == 0 else 9 * i, 9)
-            copies.append(
-                pltpu.make_async_copy(grad.at[nine], grad_any.at[nine], sems.at[3 * t + i])
-            )
-            copies[-1].start()
+                if jl % 3 == 2:
+                    three = pl.ds(26 - k if t == 0 else k - 2, 3)
+                    copies.append(
+                        pltpu.make_async_copy(
+                            grad.at[three], grad_any.at[three], sems.at[len(copies)]
+                        )
+                    )
+                    copies[-1].start()
     for copy in copies:
         copy.wait()
 
@@ -656,7 +659,7 @@
         [
             pltpu.VMEM((27, 64, 64), F32),
             pltpu.VMEM((27, 64, 64), F32),
-            pltpu.SemaphoreType.DMA((6,)),
+            pltpu.SemaphoreType.DMA((18,)),
         ],
         16,
         0,

time: 77.5 us -> 77.6 us (level)
  no operation moved by 1% of the time
where the time goes in v7:
time: 77.6 us; the launch traced here: 77 us
  starting transfers between devices  37.8 us (49%)
  Pallas kernels  21.5 us (28%)
  waiting for transfers between devices  15 us (19%)
  local copies, waits for them, and re-layouts  1.71 us (2%)
  between operations  1.04 us (1%)
    pallas_call x10, Pallas kernels, call(): pl.pallas_call(kernel, out_shape=tuple((o for _, o in outs)), in_specs=[s...  21.5 us
    ppermute x8, starting transfers between devices, sent(): return lax.ppermute(array, 'brick', pairs)  21.2 us
    ppermute x8, waiting for transfers between devices, sent(): return lax.ppermute(array, 'brick', pairs)  10.9 us
    all_to_all x1, starting transfers between devices, shards(): parts = lax.all_to_all(sums.reshape(128, 16, 128), AXES, 0, 0, tiled=True)  10.8 us
    all_to_all x1, starting transfers between devices, shards(): sums = lax.all_to_all(shares, AXES, 0, 0, tiled=True)  5.73 us
    all_to_all x1, waiting for transfers between devices, shards(): parts = lax.all_to_all(sums.reshape(128, 16, 128), AXES, 0, 0, tiled=True)  3.03 us
    unnamed x22, local copies, waits for them, and re-layouts  1.71 us
  transfers between devices with their start and end apart: 10, of which 8 were waited for; matrix products, arithmetic and copies ran while one was open for 0% of the time, Pallas kernels for 11%

profile of v7, /device:TPU:1, one launch (start us, length us, event | category | flops | bytes accessed | tf_op | source)
XLA Modules:
  0.0 77.0 jit_solution(14464987551385371388)
XLA Ops:
  0.7 2.8 %first_kernel.1 = (bf16[512,512]{1,0:T(8,128)(2,1)}, bf16[8,64,128]{2,1,0:T(8,128)(2,1)}, bf16[8,64,128]{2,1,0:T(8,128)(2,1)}, bf16[2,64,128]{2,1,0:T(8,128)(2,1)}, bf16[2,64,128]{2,1,0:T(8,128)(2,1)}) custom-call(s32[4,26]{1,0:T(4,128)} %neighbours_any.3, bf16[4,64,512]{2,1,0:T(8,128)(2,1)} %features.1, bf16[4,64,512]{2,1,0:T(8,128)(2,1)} %cotangent_any.1, ...), custom_call_target="tpu_custom_call" | custom-call | flops 4000000000 | tf_op jit(solution)/shard_map/first_kernel/pallas_call | solution.py:525
  3.5 0.0 copy-start.5
  3.5 4.6 %collective-permute-start = (bf16[8,64,128]{2,1,0:T(8,128)(2,1)}, bf16[8,64,128]{2,1,0:T(8,128)(2,1)S(1)}, u32[]{:S(2)}, u32[]{:S(2)}) collective-permute-start(bf16[8,64,128]{2,1,0:T(8,128)(2,1)} %get-tuple-element.32), channel_id=1, source_target_pairs={{0,1},{1,2},{2,3},{3,4},{4,5},{5,6},{6,7},{8,9},{9,10},{10,11},{11... | collective-permute-start | bytes 393224 | tf_op jit(solution)/shard_map/ppermute | solution.py:486
  8.1 1.9 %collective-permute-start.1 = (bf16[8,64,128]{2,1,0:T(8,128)(2,1)}, bf16[8,64,128]{2,1,0:T(8,128)(2,1)S(1)}, u32[]{:S(2)}, u32[]{:S(2)}) collective-permute-start(bf16[8,64,128]{2,1,0:T(8,128)(2,1)} %get-tuple-element.37), channel_id=1, source_target_pairs={{1,0},{2,1},{3,2},{4,3},{5,4},{6,5},{7,6},{9,8},{10,9},{11,10},{12... | collective-permute-start | bytes 393224 | tf_op jit(solution)/shard_map/ppermute | solution.py:486
  10.0 0.0 copy-start.7
  10.0 0.0 copy-start.8
  10.1 0.6 copy-done.7
  10.7 0.0 copy-done.8
  10.7 1.0 %copy-done.9 = bf16[512,512]{1,0:T(8,128)(2,1)S(1)} copy-done((bf16[512,512]{1,0:T(8,128)(2,1)S(1)}, bf16[512,512]{1,0:T(8,128)(2,1)}, u32[]{:S(2)}) %copy-start.9) | copy-done | bytes 524312
  11.7 1.0 %prepare_kernel.1 = (bf16[2,24,64,128]{3,2,1,0:T(8,128)(2,1)S(1)}, f32[4,512]{1,0:T(4,128)S(1)}, bf16[192,576]{1,0:T(8,128)(2,1)S(1)}, bf16[192,576]{1,0:T(8,128...) custom-call(bf16[512,512]{1,0:T(8,128)(2,1)S(1)} %copy-done.9, ...), custom_call_target="tpu_custom_call" | custom-call | flops 3000000000 | tf_op jit(solution)/shard_map/prepare_kernel/pallas_call | solution.py:525
  12.8 1.8 %collective-permute-done.1.from_right = bf16[8,64,128]{2,1,0:T(8,128)(2,1)S(1)} collective-permute-done((bf16[8,64,128]{2,1,0:T(8,128)(2,1)}, bf16[8,64,128]{2,1,0:T(8,128)(2,1)S(1)}, u32[]{:S(2)}, u32[]{:S(2)}) %collective-permute-start.1) | collective-permute-done | bytes 131104 | tf_op jit(solution)/shard_map/ppermute | solution.py:486
  14.6 3.1 %collective-permute-start.2 = (bf16[6,64,128]{2,1,0:T(8,128)(2,1)S(1)}, bf16[6,64,128]{2,1,0:T(8,128)(2,1)S(1)}, u32[]{:S(2)}, u32[]{:S(2)}) collective-permute-start(bf16[6,64,128]{2,1,0:T(8,128)(2,1)S(1)} %get-tuple-element.40), channel_id=1, source_target_pairs={{0,8},{1,9},{2,10},{3,11},{4,12},{5,13},{6,14},{7,15},{8,16},{9,17... | collective-permute-start | bytes 294920 | tf_op jit(solution)/shard_map/ppermute | solution.py:486
  17.8 1.4 %collective-permute-start.3 = (bf16[6,64,128]{2,1,0:T(8,128)(2,1)S(1)}, bf16[6,64,128]{2,1,0:T(8,128)(2,1)S(1)}, u32[]{:S(2)}, u32[]{:S(2)}) collective-permute-start(bf16[6,64,128]{2,1,0:T(8,128)(2,1)S(1)} %get-tuple-element.41), channel_id=1, source_target_pairs={{8,0},{9,1},{10,2},{11,3},{12,4},{13,5},{14,6},{15,7},{16,8},{17,9... | collective-permute-start | bytes 294920 | tf_op jit(solution)/shard_map/ppermute | solution.py:486
  19.2 2.7 %tables_kernel.1 = (s32[104]{0:T(128)S(1)}, s32[288]{0:T(512)S(1)}) custom-call(s32[4,26]{1,0:T(4,128)S(1)} %copy-done.6, bf16[8,64,128]{2,1,0:T(8,128)(2,1)S(1)} %collective-permute-done.after_any.from_left), custom_call_target="tpu_custom_call" | custom-call | flops 3000000000 | tf_op jit(solution)/shard_map/tables_kernel/pallas_call | solution.py:525
  22.0 1.3 %collective-permute-done.3.from_down = bf16[6,64,128]{2,1,0:T(8,128)(2,1)S(1)} collective-permute-done((bf16[6,64,128]{2,1,0:T(8,128)(2,1)S(1)}, bf16[6,64,128]{2,1,0:T(8,128)(2,1)S(1)}, u32[]{:S(2)}, u32[]{:S(2)}) %collective-permute-start.3) | collective-permute-done | bytes 98336 | tf_op jit(solution)/shard_map/ppermute | solution.py:486
  23.3 7.7 %second_kernel.1 = (bf16[256,512]{1,0:T(8,128)(2,1)S(1)}, bf16[2048,128]{1,0:T(8,128)(2,1)}) custom-call(s32[104]{0:T(128)S(1)} %get-tuple-element.33.index_ref, bf16[512,512]{1,0:T(8,128)(2,1)S(1)} %copy-done.10, bf16[2,24,64,128]{3,2,1,0:T(8,128)(2,1)S(1)} %get-tuple-element.36.faces, bf16[8,64,128]{2,1,0:T(8,128)(2,1)S(1)} %collective-permute-done.after_any.from_left, ...), custom_call_target="tpu_custom_call" | custom-call | flops 10000000000 | tf_op jit(solution)/shard_map/second_kernel/pallas_call | solution.py:525
  31.0 10.8 %all-to-all-start = ((bf16[128,16,128]{2,1,0:T(8,128)(2,1)}), bf16[128,16,128]{2,1,0:T(8,128)(2,1)S(1)}, u32[]{:S(2)}, u32[]{:S(2)}) async-start(bf16[128,16,128]{2,1,0:T(8,128)(2,1)} %bitcast.2), calls=%async_computation | async-start | bytes 1048576 | tf_op jit(solution)/shard_map/all_to_all | solution.py:623
  41.8 1.0 %faces_kernel.1 = (bf16[24,64,128]{2,1,0:T(8,128)(2,1)S(1)}, bf16[4,64,128]{2,1,0:T(8,128)(2,1)S(1)}, bf16[4,64,128]{2,1,0:T(8,128)(2,1)S(1)}, bf16[1,64,128]{2,1,0:T(8,128)(2,1)S(1)}, bf16[1,64,128]{2,1,0:T(8,128)(2,1)S(1)}) custom-call(s32[288]{0:T(512)S(1)} %get-tuple-element.34.send_ref, bf16[256,512]{1,0:T(8,128)(2,1)S(1)} %get-tuple-element.50.hidden), custom_call_target="tpu_custom_call" | custom-call | flops 8000000000 | tf_op jit(solution)/shard_map/faces_kernel/pallas_call | solution.py:525
  42.8 3.5 %collective-permute-start.4 = (bf16[4,64,128]{2,1,0:T(8,128)(2,1)S(1)}, bf16[4,64,128]{2,1,0:T(8,128)(2,1)S(1)}, u32[]{:S(2)}, u32[]{:S(2)}) collective-permute-start(bf16[4,64,128]{2,1,0:T(8,128)(2,1)S(1)} %get-tuple-element.52), channel_id=1, source_target_pairs={{0,1},{1,2},{2,3},{3,4},{4,5},{5,6},{6,7},{8,9},{9,10},{10,11},{11... | collective-permute-start | bytes 196616 | tf_op jit(solution)/shard_map/ppermute | solution.py:486
  46.4 1.9 %collective-permute-start.5 = (bf16[4,64,128]{2,1,0:T(8,128)(2,1)S(1)}, bf16[4,64,128]{2,1,0:T(8,128)(2,1)S(1)}, u32[]{:S(2)}, u32[]{:S(2)}) collective-permute-start(bf16[4,64,128]{2,1,0:T(8,128)(2,1)S(1)} %get-tuple-element.53), channel_id=1, source_target_pairs={{1,0},{2,1},{3,2},{4,3},{5,4},{6,5},{7,6},{9,8},{10,9},{11,10},{12... | collective-permute-start | bytes 196616 | tf_op jit(solution)/shard_map/ppermute | solution.py:486
  48.3 0.7 collective-permute-done.4.left_any.from_left
  49.0 3.3 %collective-permute-done.5.right_any.from_right = bf16[4,64,128]{2,1,0:T(8,128)(2,1)S(1)} collective-permute-done((bf16[4,64,128]{2,1,0:T(8,128)(2,1)S(1)}, bf16[4,64,128]{2,1,0:T(8,128)(2,1)S(1)}, u32[]{:S(2)}, u32[]{:S(2)}) %collective-permute-start.5) | collective-permute-done | bytes 65568 | tf_op jit(solution)/shard_map/ppermute | solution.py:486
  52.3 3.0 %all-to-all-done.parts = bf16[128,16,128]{2,1,0:T(8,128)(2,1)S(1)} async-done(((bf16[128,16,128]{2,1,0:T(8,128)(2,1)}), bf16[128,16,128]{2,1,0:T(8,128)(2,1)S(1)}, u32[]{:S(2)}, u32[]{:S(2)}) %all-to-all-start) | async-done | bytes 524320 | tf_op jit(solution)/shard_map/all_to_all | solution.py:623
  55.3 0.9 %share_kernel.1.after_any = bf16[128,16,128]{2,1,0:T(8,128)(2,1)} custom-call(bf16[128,16,128]{2,1,0:T(8,128)(2,1)S(1)} %all-to-all-done.parts, bf16[4,64,128]{2,1,0:T(8,128)(2,1)S(1)} %collective-permute-done.4.left_any.from_left, bf16[4,64,128]{2,1,0:T(8,128)(2,1)S(1)} %collective-permute-done.5.right_any.from_right), custom_call_target="tpu_custom_call" | custom-call | flops 1000000000 | tf_op jit(solution)/shard_map/share_kernel/pallas_call | solution.py:525
  56.2 5.7 %all-to-all-start.1 = ((bf16[128,16,128]{2,1,0:T(8,128)(2,1)}), bf16[128,16,128]{2,1,0:T(8,128)(2,1)S(1)}, u32[]{:S(2)}, u32[]{:S(2)}) async-start(bf16[128,16,128]{2,1,0:T(8,128)(2,1)} %share_kernel.1.after_any), calls=%async_computation.1 | async-start | bytes 1048576 | tf_op jit(solution)/shard_map/all_to_all | solution.py:637
  62.0 3.4 %collective-permute-start.6 = (bf16[3,64,128]{2,1,0:T(8,128)(2,1)S(1)}, bf16[3,64,128]{2,1,0:T(8,128)(2,1)S(1)}, u32[]{:S(2)}, u32[]{:S(2)}) collective-permute-start(bf16[3,64,128]{2,1,0:T(8,128)(2,1)S(1)} %get-tuple-element.57), channel_id=1, source_target_pairs={{0,8},{1,9},{2,10},{3,11},{4,12},{5,13},{6,14},{7,15},{8,16},{9,17... | collective-permute-start | bytes 147464 | tf_op jit(solution)/shard_map/ppermute | solution.py:486
  65.4 1.3 %collective-permute-start.7 = (bf16[3,64,128]{2,1,0:T(8,128)(2,1)S(1)}, bf16[3,64,128]{2,1,0:T(8,128)(2,1)S(1)}, u32[]{:S(2)}, u32[]{:S(2)}) collective-permute-start(bf16[3,64,128]{2,1,0:T(8,128)(2,1)S(1)} %get-tuple-element.58), channel_id=1, source_target_pairs={{8,0},{9,1},{10,2},{11,3},{12,4},{13,5},{14,6},{15,7},{16,8},{17,9... | collective-permute-start | bytes 147464 | tf_op jit(solution)/shard_map/ppermute | solution.py:486
  66.7 0.6 collective-permute-done.6.from_up
  67.3 3.2 %collective-permute-done.7.from_down = bf16[3,64,128]{2,1,0:T(8,128)(2,1)S(1)} collective-permute-done((bf16[3,64,128]{2,1,0:T(8,128)(2,1)S(1)}, bf16[3,64,128]{2,1,0:T(8,128)(2,1)S(1)}, u32[]{:S(2)}, u32[]{:S(2)}) %collective-permute-start.7) | collective-permute-done | bytes 49184 | tf_op jit(solution)/shard_map/ppermute | solution.py:486
  70.5 3.9 %third_kernel.1 = bf16[4,64,512]{2,1,0:T(8,128)(2,1)} custom-call(s32[104]{0:T(128)S(1)} %get-tuple-element.33.index_ref, bf16[24,64,128]{2,1,0:T(8,128)(2,1)S(1)} %get-tuple-element.51.hidden_faces, bf16[4,64,128]{2,1,0:T(8,128)(2,1)S(1)} %collective-permute-done.4.left_any.from_left, bf16[4,64,128]{2,1,0:T(8,128)(2,1)S(1)} %collective-permute-done.5.right_any.from_right, ...), custom_call_target="tpu_custom_call" | custom-call | flops 2000000000 | tf_op jit(solution)/shard_map/third_kernel/pallas_call | solution.py:525
  74.4 1.0 %all-to-all-done.1 = bf16[128,16,128]{2,1,0:T(8,128)(2,1)S(1)} async-done(((bf16[128,16,128]{2,1,0:T(8,128)(2,1)}), bf16[128,16,128]{2,1,0:T(8,128)(2,1)S(1)}, u32[]{:S(2)}, u32[]{:S(2)}) %all-to-all-start.1) | async-done | bytes 524320 | tf_op jit(solution)/shard_map/all_to_all | solution.py:637
  75.5 1.4 %unpack_kernel.1 = (f32[27,64,64]{2,1,0:T(8,128)}, f32[27,64,64]{2,1,0:T(8,128)}) custom-call(bf16[2048,128]{1,0:T(8,128)(2,1)S(1)} %bitcast.4), custom_call_target="tpu_custom_call" | custom-call | tf_op jit(solution)/shard_map/unpack_kernel/pallas_call | solution.py:525
  (20 shorter events, 0.1 us)
Async XLA Ops:
  0.6 9.4 %copy-start.3 = (bf16[27,64,64]{2,1,0:T(8,128)(2,1)S(1)}, bf16[27,64,64]{2,1,0:T(8,128)(2,1)}, u32[]{:S(2)}) copy-start(bf16[27,64,64]{2,1,0:T(8,128)(2,1)} %weight.1) | copy-start | bytes 663556
  0.6 9.4 %copy-start.2 = (bf16[27,64,64]{2,1,0:T(8,128)(2,1)S(1)}, bf16[27,64,64]{2,1,0:T(8,128)(2,1)}, u32[]{:S(2)}) copy-start(bf16[27,64,64]{2,1,0:T(8,128)(2,1)} %first.1) | copy-start | bytes 663556
  3.5 6.6 %copy-start.5 = (s32[4,512]{1,0:T(4,128)S(1)}, s32[4,512]{1,0:T(4,128)}, u32[]{:S(2)}) copy-start(s32[4,512]{1,0:T(4,128)} %active.3) | copy-start | bytes 24580
  3.5 9.3 %collective-permute-start = (bf16[8,64,128]{2,1,0:T(8,128)(2,1)}, bf16[8,64,128]{2,1,0:T(8,128)(2,1)S(1)}, u32[]{:S(2)}, u32[]{:S(2)}) collective-permute-start(bf16[8,64,128]{2,1,0:T(8,128)(2,1)} %get-tuple-element.32), channel_id=1, source_target_pairs={{0,1},{1,2},{2,3},{3,4},{4,5},{5,6},{6,7},{8,9},{9,10},{10,11},{11... | collective-permute-start | bytes 393224 | tf_op jit(solution)/shard_map/ppermute | solution.py:486
  8.1 6.5 %collective-permute-start.1 = (bf16[8,64,128]{2,1,0:T(8,128)(2,1)}, bf16[8,64,128]{2,1,0:T(8,128)(2,1)S(1)}, u32[]{:S(2)}, u32[]{:S(2)}) collective-permute-start(bf16[8,64,128]{2,1,0:T(8,128)(2,1)} %get-tuple-element.37), channel_id=1, source_target_pairs={{1,0},{2,1},{3,2},{4,3},{5,4},{6,5},{7,6},{9,8},{10,9},{11,10},{12... | collective-permute-start | bytes 393224 | tf_op jit(solution)/shard_map/ppermute | solution.py:486
  10.0 0.7 copy-start.7
  10.0 0.7 copy-start.8
  10.7 1.0 %copy-start.9 = (bf16[512,512]{1,0:T(8,128)(2,1)S(1)}, bf16[512,512]{1,0:T(8,128)(2,1)}, u32[]{:S(2)}) copy-start(bf16[512,512]{1,0:T(8,128)(2,1)} %get-tuple-element.35.values) | copy-start | bytes 1572868
  11.7 2.9 %copy-start = (bf16[2,64,128]{2,1,0:T(8,128)(2,1)S(1)}, bf16[2,64,128]{2,1,0:T(8,128)(2,1)}, u32[]{:S(2)}) copy-start(bf16[2,64,128]{2,1,0:T(8,128)(2,1)} %get-tuple-element.38.up.after_any) | copy-start | bytes 98308
  11.7 2.9 %copy-start.1 = (bf16[2,64,128]{2,1,0:T(8,128)(2,1)S(1)}, bf16[2,64,128]{2,1,0:T(8,128)(2,1)}, u32[]{:S(2)}) copy-start(bf16[2,64,128]{2,1,0:T(8,128)(2,1)} %get-tuple-element.39.down) | copy-start | bytes 98308
  14.6 4.6 %copy-start.6 = (s32[4,26]{1,0:T(4,128)S(1)}, s32[4,26]{1,0:T(4,128)}, u32[]{:S(2)}) copy-start(s32[4,26]{1,0:T(4,128)} %neighbours_any.3) | copy-start | bytes 1252
  14.6 7.3 %collective-permute-start.2 = (bf16[6,64,128]{2,1,0:T(8,128)(2,1)S(1)}, bf16[6,64,128]{2,1,0:T(8,128)(2,1)S(1)}, u32[]{:S(2)}, u32[]{:S(2)}) collective-permute-start(bf16[6,64,128]{2,1,0:T(8,128)(2,1)S(1)} %get-tuple-element.40), channel_id=1, source_target_pairs={{0,8},{1,9},{2,10},{3,11},{4,12},{5,13},{6,14},{7,15},{8,16},{9,17... | collective-permute-start | bytes 294920 | tf_op jit(solution)/shard_map/ppermute | solution.py:486
  17.8 5.5 %copy-start.10 = (bf16[512,512]{1,0:T(8,128)(2,1)S(1)}, bf16[512,512]{1,0:T(8,128)(2,1)}, u32[]{:S(2)}) copy-start(bf16[512,512]{1,0:T(8,128)(2,1)} %get-tuple-element.35.values) | copy-start | bytes 1572868
  17.8 5.5 %collective-permute-start.3 = (bf16[6,64,128]{2,1,0:T(8,128)(2,1)S(1)}, bf16[6,64,128]{2,1,0:T(8,128)(2,1)S(1)}, u32[]{:S(2)}, u32[]{:S(2)}) collective-permute-start(bf16[6,64,128]{2,1,0:T(8,128)(2,1)S(1)} %get-tuple-element.41), channel_id=1, source_target_pairs={{8,0},{9,1},{10,2},{11,3},{12,4},{13,5},{14,6},{15,7},{16,8},{17,9... | collective-permute-start | bytes 294920 | tf_op jit(solution)/shard_map/ppermute | solution.py:486
  31.0 24.3 %all-to-all-start = ((bf16[128,16,128]{2,1,0:T(8,128)(2,1)}), bf16[128,16,128]{2,1,0:T(8,128)(2,1)S(1)}, u32[]{:S(2)}, u32[]{:S(2)}) async-start(bf16[128,16,128]{2,1,0:T(8,128)(2,1)} %bitcast.2), calls=%async_computation | async-start | bytes 1048576 | tf_op jit(solution)/shard_map/all_to_all | solution.py:623
  42.8 6.2 %collective-permute-start.4 = (bf16[4,64,128]{2,1,0:T(8,128)(2,1)S(1)}, bf16[4,64,128]{2,1,0:T(8,128)(2,1)S(1)}, u32[]{:S(2)}, u32[]{:S(2)}) collective-permute-start(bf16[4,64,128]{2,1,0:T(8,128)(2,1)S(1)} %get-tuple-element.52), channel_id=1, source_target_pairs={{0,1},{1,2},{2,3},{3,4},{4,5},{5,6},{6,7},{8,9},{9,10},{10,11},{11... | collective-permute-start | bytes 196616 | tf_op jit(solution)/shard_map/ppermute | solution.py:486
  46.4 5.9 %collective-permute-start.5 = (bf16[4,64,128]{2,1,0:T(8,128)(2,1)S(1)}, bf16[4,64,128]{2,1,0:T(8,128)(2,1)S(1)}, u32[]{:S(2)}, u32[]{:S(2)}) collective-permute-start(bf16[4,64,128]{2,1,0:T(8,128)(2,1)S(1)} %get-tuple-element.53), channel_id=1, source_target_pairs={{1,0},{2,1},{3,2},{4,3},{5,4},{6,5},{7,6},{9,8},{10,9},{11,10},{12... | collective-permute-start | bytes 196616 | tf_op jit(solution)/shard_map/ppermute | solution.py:486
  56.2 19.2 %all-to-all-start.1 = ((bf16[128,16,128]{2,1,0:T(8,128)(2,1)}), bf16[128,16,128]{2,1,0:T(8,128)(2,1)S(1)}, u32[]{:S(2)}, u32[]{:S(2)}) async-start(bf16[128,16,128]{2,1,0:T(8,128)(2,1)} %share_kernel.1.after_any), calls=%async_computation.1 | async-start | bytes 1048576 | tf_op jit(solution)/shard_map/all_to_all | solution.py:637
  61.9 8.6 %copy-start.4 = (bf16[4,64,512]{2,1,0:T(8,128)(2,1)S(1)}, bf16[4,64,512]{2,1,0:T(8,128)(2,1)}, u32[]{:S(2)}) copy-start(bf16[4,64,512]{2,1,0:T(8,128)(2,1)} %features.1) | copy-start | bytes 786436
  62.0 5.3 %collective-permute-start.6 = (bf16[3,64,128]{2,1,0:T(8,128)(2,1)S(1)}, bf16[3,64,128]{2,1,0:T(8,128)(2,1)S(1)}, u32[]{:S(2)}, u32[]{:S(2)}) collective-permute-start(bf16[3,64,128]{2,1,0:T(8,128)(2,1)S(1)} %get-tuple-element.57), channel_id=1, source_target_pairs={{0,8},{1,9},{2,10},{3,11},{4,12},{5,13},{6,14},{7,15},{8,16},{9,17... | collective-permute-start | bytes 147464 | tf_op jit(solution)/shard_map/ppermute | solution.py:486
  65.4 5.1 %collective-permute-start.7 = (bf16[3,64,128]{2,1,0:T(8,128)(2,1)S(1)}, bf16[3,64,128]{2,1,0:T(8,128)(2,1)S(1)}, u32[]{:S(2)}, u32[]{:S(2)}) collective-permute-start(bf16[3,64,128]{2,1,0:T(8,128)(2,1)S(1)} %get-tuple-element.58), channel_id=1, source_target_pairs={{8,0},{9,1},{10,2},{11,3},{12,4},{13,5},{14,6},{15,7},{16,8},{17,9... | collective-permute-start | bytes 147464 | tf_op jit(solution)/shard_map/ppermute | solution.py:486
